TPU v7x, 32 devices: a whole 2x2x4 slice. The times are simulated.
32 devices in a mesh: groups: 2 (over y), ctx: 2 (over x), exp: 4 (over z), tp: 2 (over core).
Axes of the slice: x: 2, y: 2, z: 4, core: 2. Of those that a mesh axis runs over, the one named last changes fastest.
Arguments:
- queries: bfloat16 [512, 8192], P(('groups', 'ctx'), ('exp', 'tp')), parts along dimension 0, may hold values from -6 to 6
- keys: bfloat16 [512, 8192], P(('groups', 'ctx'), ('exp', 'tp')), parts along dimension 0, may hold values from -6 to 6
- values: bfloat16 [512, 8192], P(('groups', 'ctx'), ('exp', 'tp')), parts along dimension 0, may hold values from -6 to 6
- log_decay: float32 [512, 64], P(('groups', 'ctx'), ('exp', 'tp')), parts along dimension 0, may hold values from -1 to 0
- moe_input: bfloat16 [64, 6144], P(('groups', 'ctx', 'exp'), 'tp'), parts along dimension 0, may hold values from -6 to 6
- route_ids: int32 [64, 2], P(('groups', 'ctx', 'exp')), parts along dimension 0, may hold values from 0 to 3, all different within a row; in each aligned block of 4 rows (0 to 3, 4 to 7, ...) at most 3 rows name the same one
- route_weight: float32 [64, 2], P(('groups', 'ctx', 'exp')), parts along dimension 0, may hold values from 0.2 to 1
- gate_up: bfloat16 [4, 6144, 2, 4608], P('exp', 'tp', None, 'ctx'), may hold values from -0.078125 to 0.078125
- down: bfloat16 [4, 4608, 6144], P('exp', None, ('tp', 'ctx')), may hold values from -0.09375 to 0.09375
Outputs:
- attended: bfloat16 [512, 8192], P(('groups', 'ctx'), ('exp', 'tp')), parts along dimension 0
- moe_out: bfloat16 [64, 6144], P(('groups', 'ctx', 'exp'), 'tp'), parts along dimension 0
There are 2 independent parts, one for each index of `groups`. A program takes and returns all parts, laid end to end along the dimension named above; an argument that names none is the same for every part. Nothing has to cross between parts.
Inputs may be any that keep to these rules, and one draw needn't show every extreme that they name: `route_ids`: each row names two different experts. In each aligned block of 4 rows (the rows of one device) no expert is named more than 3 times, and some block names one expert exactly 3 times.
All inputs are finite; a program needn't handle non-finite values.
Results may differ from a plain program's by a relative error of at most 0.023.
Values may be sent and summed in bfloat16 or wider, within the bound.
No kernel may reach another device: no remote copies, remote signals or barrier semaphores. Data moves between devices by JAX's collectives and lax.ppermute only.
A program may use at most 128 MiB of HBM per device.

v0:
```python
import jax
import jax.numpy as jnp
from jax import lax
from jax.sharding import PartitionSpec as P


def prefix(shard, axis, combine, identity):
    devices, here = (lax.axis_size(axis), lax.axis_index(axis))
    everything = jax.tree.map(
        lambda part, kind: lax.all_gather(part.astype(kind), axis),
        shard,
        (jnp.bfloat16, jnp.bfloat16),
    )
    start = jax.tree.map(
        lambda part, zero: jnp.broadcast_to(jnp.asarray(zero, part.dtype), part.shape),
        shard,
        identity,
    )

    def step(k, before):
        reached = k < here
        new = combine(
            before, jax.tree.map(lambda part, own: part[k].astype(own.dtype), everything, shard)
        )
        return jax.tree.map(lambda a, b: jnp.where(reached, a, b), new, before)

    return lax.fori_loop(0, devices, step, start)


def block_terms(queries, keys, values, log_decay):
    rows = queries.shape[0]
    heads = log_decay.shape[1]
    qb = queries.reshape(rows, heads, -1)
    kb = keys.reshape(rows, heads, -1)
    vb = values.reshape(rows, heads, -1)
    cum = jnp.cumsum(log_decay, axis=0)
    diff = jnp.transpose(cum)[:, :, None] - jnp.transpose(cum)[:, None, :]
    causal = jnp.arange(rows)[:, None] >= jnp.arange(rows)[None, :]
    decay = jnp.where(causal[None, :, :], jnp.exp(jnp.minimum(diff, 0.0)), 0.0)
    scores = jnp.einsum("thd,shd->hts", qb, kb, preferred_element_type=jnp.float32)
    weights = (scores * decay).astype(jnp.bfloat16)
    intra = jnp.einsum("hts,shd->thd", weights, vb, preferred_element_type=jnp.float32)
    last = cum[-1]
    kscaled = kb.astype(jnp.float32) * jnp.exp(last[None, :] - cum)[:, :, None]
    local = jnp.einsum(
        "shd,she->hde", kscaled, vb.astype(jnp.float32), precision=lax.Precision.HIGHEST
    )
    return (qb, cum, intra, local, jnp.exp(last))


def chain_states(preceding_positions, later):
    return (
        preceding_positions[0] * later[0],
        later[0][:, None, None] * preceding_positions[1] + later[1],
    )


def route_slots(route_ids, expert_list, slots_each):
    flat_ids = route_ids.reshape(-1)
    onehot = (flat_ids[:, None] == jnp.arange(expert_list)[None, :]).astype(jnp.int32)
    slot = jnp.sum((jnp.cumsum(onehot, axis=0) - 1) * onehot, axis=1)
    target = flat_ids * slots_each + slot
    pick = jnp.arange(expert_list * slots_each)[:, None] == target[None, :]
    return (target, pick)


def on_device(queries, keys, values, log_decay, moe_input, route_ids, route_weight, gate_up, down):
    qb, cum, intra, local, totals = block_terms(queries, keys, values, log_decay)
    heads = log_decay.shape[1]
    width = local.shape[1]
    identity = (jnp.ones((heads,), jnp.float32), jnp.zeros((heads, width, width), jnp.float32))
    entering = prefix((totals, local), "ctx", chain_states, identity)
    qscaled = qb.astype(jnp.float32) * jnp.exp(cum)[:, :, None]
    inter = jnp.einsum("thd,hde->the", qscaled, entering[1], precision=lax.Precision.HIGHEST)
    mixed = intra + inter
    normed = mixed * lax.rsqrt(jnp.mean(mixed * mixed, axis=-1, keepdims=True) + 1e-06)
    attended = normed.astype(jnp.bfloat16).reshape(queries.shape)
    expert_list = lax.axis_size("exp")
    ctx_count = lax.axis_size("ctx")
    tok_rows = moe_input.shape[0]
    half_width = moe_input.shape[1]
    slots_each = min(tok_rows, tok_rows * 2 // expert_list + tok_rows // 4)
    target, pick = route_slots(route_ids, expert_list, slots_each)
    doubled = jnp.repeat(moe_input, 2, axis=0)
    send = jnp.dot(pick.astype(jnp.bfloat16), doubled, preferred_element_type=jnp.float32)
    send = send.astype(jnp.bfloat16).reshape(expert_list, slots_each, half_width)
    arrived = lax.all_to_all(send, "exp", split_axis=0, concat_axis=0, tiled=True)
    slot_rows = arrived.reshape(expert_list * slots_each, half_width)
    w_both = gate_up.reshape(half_width, -1)
    ff_local = w_both.shape[1] // 2
    partial_value = jnp.dot(
        lax.all_gather(slot_rows, "ctx", axis=0, tiled=True),
        w_both,
        preferred_element_type=jnp.float32,
    )
    summed = lax.psum(partial_value.astype(jnp.bfloat16), "tp").astype(jnp.float32)
    hidden = (jax.nn.silu(summed[:, :ff_local]) * summed[:, ff_local:]).astype(jnp.bfloat16)
    w_down = down.reshape(down.shape[1], down.shape[2])
    expert_out = jnp.dot(
        lax.all_gather(hidden, "ctx", axis=1, tiled=True),
        w_down,
        preferred_element_type=jnp.float32,
    ).astype(jnp.bfloat16)
    col_width = expert_out.shape[1]
    stacked = expert_out.reshape(ctx_count, expert_list, slots_each, col_width)
    back = lax.all_to_all(
        lax.all_to_all(stacked, "ctx", split_axis=0, concat_axis=3, tiled=True),
        "exp",
        split_axis=1,
        concat_axis=1,
        tiled=True,
    )
    flat = back.reshape(expert_list * slots_each, half_width)
    selected_routes = flat[target].astype(jnp.float32).reshape(tok_rows, 2, half_width)
    merged_output = jnp.sum(selected_routes * route_weight[:, :, None], axis=1)
    return (attended, merged_output.astype(jnp.bfloat16))


def solution(mesh):
    in_specs = (
        P(("groups", "ctx"), ("exp", "tp")),
        P(("groups", "ctx"), ("exp", "tp")),
        P(("groups", "ctx"), ("exp", "tp")),
        P(("groups", "ctx"), ("exp", "tp")),
        P(("groups", "ctx", "exp"), "tp"),
        P(("groups", "ctx", "exp"), None),
        P(("groups", "ctx", "exp"), None),
        P("exp", "tp", None, "ctx"),
        P("exp", None, ("tp", "ctx")),
    )
    out_specs = (P(("groups", "ctx"), ("exp", "tp")), P(("groups", "ctx", "exp"), "tp"))
    return jax.shard_map(
        on_device, mesh=mesh, in_specs=in_specs, out_specs=out_specs, check_vma=False
    )
```

profile of v0, /device:TPU:0, one launch (start us, length us, event | category | flops | bytes accessed | tf_op | source)
XLA Modules:
  0.0 135.3 jit_solution(3343451838918969356)
XLA Ops:
  7.2 0.8 copy.72
  8.3 0.8 broadcast_in_dim.16
  9.2 0.7 reshape.141
  10.0 6.3 %all-to-all-start = ((bf16[4,3,3072]{2,1,0:T(4,128)(2,1)}), bf16[4,3,3072]{2,1,0:T(4,128)(2,1)S(1)}, u32[]{:S(2)}, u32[]{:S(2)}) async-start(bf16[4,3,3072]{2,1,0:T(4,128)(2,1)} %reshape.141), calls=%async_computation | async-start | bytes 196608 | tf_op jit(solution)/shard_map/all_to_all | solution.py:87
  16.3 0.8 copy.62
  17.4 1.1 copy.83
  18.9 8.4 %all-gather = bf16[16,128,128]{2,1,0:T(8,128)(2,1)S(1)} all-gather(bf16[8,128,128]{2,1,0:T(8,128)(2,1)S(1)} %convolution_convert_fusion.2), channel_id=2, replica_groups=mesh['groups'=2,'ctx'=2,'exp'=4,'tp'=2] {'ctx'}, dimensions={0}, use_global_device_ids=true | all-gather | bytes 786432 | tf_op jit(solution)/shard_map/all_gather | solution.py:10
  27.4 4.2 %all-gather.1 = bf16[2,1,8]{2,1,0:T(2,128)(2,1)S(1)} all-gather(bf16[1,1,8]{2,1,0:T(2,128)(2,1)S(1)} %get-tuple-element.136), channel_id=1, replica_groups=mesh['groups'=2,'ctx'=2,'exp'=4,'tp'=2] {'ctx'}, dimensions={0}, use_global_device_ids=true | all-gather | bytes 48 | tf_op jit(solution)/shard_map/all_gather | solution.py:10
  32.0 2.2 %convolution_bitcast_fusion.1 = f32[128,8,128]{0,2,1:T(8,128)S(1)} fusion(f32[8,128,128]{2,1,0:T(8,128)S(1)} %get-tuple-element.96, f32[128,8]{0,1:T(8,128)S(1)} %copy.70, bf16[128,1024]{1,0:T(8,128)(2,1)} %param.11), kind=kOutput, calls=%fused_computation.11 | convolution fusion | flops 201588736 | bytes 1314816 | tf_op jit(solution)/shard_map/thd,hde->the/dot_general | solution.py:74
  34.2 1.5 %multiply_reduce_fusion = (f32[128,8]{0,1:T(8,128)S(1)}, f32[128,8,128]{0,2,1:T(8,128)S(1)}) fusion(f32[128,8,128]{0,2,1:T(8,128)S(1)} %convolution_bitcast_fusion.1, bf16[128,8,128]{0,2,1:T(8,128)(2,1)S(1)} %bitcast.88, f32[8,128]{1,0:T(8,128)S(1)} %copy.63, pred[128,128]{1,0:T(8,128)(4,1)S(1)} %iota_compare_fusion, bf16[128,1024]{1,0:T(8,128)(2,1)S(1)} %copy-done, ...), kind=kOutput, calls=%fused_computation.16 | convolution fusion | flops 68156416 | bytes 1859584 | tf_op jit(solution)/shard_map/hts,shd->thd/dot_general | solution.py:42
  35.7 0.7 broadcast_multiply_fusion
  36.4 20.0 %copy.86 = bf16[384,8,2,2304]{3,1,2,0:T(8,128)(2,1)} copy(bf16[384,8,2,2304]{3,2,1,0:T(2,128)(2,1)} %bitcast.85) | data formatting | bytes 56623104
  56.7 5.3 %all-gather.2 = bf16[2,12,3072]{2,1,0:T(8,128)(2,1)S(1)} all-gather(bf16[1,12,3072]{2,1,0:T(8,128)(2,1)S(1)} %reshape.161), channel_id=1, replica_groups=mesh['groups'=2,'ctx'=2,'exp'=4,'tp'=2] {'ctx'}, dimensions={0}, use_global_device_ids=true | all-gather | bytes 221184 | tf_op jit(solution)/shard_map/all_gather | solution.py:92
  62.1 11.7 %convolution_convert_fusion = bf16[24,4608]{1,0:T(8,128)(2,1)} fusion(bf16[24,3072]{1,0:T(8,128)(2,1)S(1)} %reshape.162, bf16[3072,4608]{1,0:T(8,128)(2,1)} %bitcast.84), kind=kOutput, calls=%fused_computation.6 | convolution fusion | flops 679587840 | bytes 28680192 | tf_op jit(solution)/shard_map/dot_general | solution.py:91
  73.9 19.4 %all-reduce.2.cloned.1.call-done = bf16[24,4608]{1,0:T(8,128)(2,1)} async-done(((bf16[24,4608]{1,0:T(8,128)(2,1)}), bf16[24,4608]{1,0:T(8,128)(2,1)}) %all-reduce.2.cloned.1.call-update) | async-done | bytes 221200 | tf_op jit(solution)/shard_map/psum | solution.py:96
  93.3 1.0 convert_element_type.82
  94.3 5.9 %all_gather.20 = bf16[24,4608]{1,0:T(8,128)(2,1)S(1)} all-gather(bf16[24,2304]{1,0:T(8,128)(2,1)S(1)} %fusion.32), channel_id=1, replica_groups=mesh['groups'=2,'ctx'=2,'exp'=4,'tp'=2] {'ctx'}, dimensions={1}, use_global_device_ids=true | all-gather | bytes 331776 | tf_op jit(solution)/shard_map/all_gather | solution.py:100
  100.3 7.0 %fusion.3 = bf16[24,1536]{1,0:T(8,128)(2,1)S(1)} fusion(bf16[24,4608]{1,0:T(8,128)(2,1)S(1)} %all_gather.20, bf16[1,4608,1536]{2,1,0:T(8,128)(2,1)} %param.19), kind=kOutput, calls=%fused_computation.8 | convolution fusion | flops 339775488 | bytes 14450688 | tf_op jit(solution)/shard_map/dot_general | solution.py:99
  108.0 3.3 %all-to-all-start.1 = ((bf16[2,4,3,1536]{3,1,2,0:T(4,128)(2,1)}), bf16[2,4,3,1536]{3,1,2,0:T(4,128)(2,1)S(1)}, u32[]{:S(2)}, u32[]{:S(2)}) async-start(bf16[2,4,3,1536]{3,1,2,0:T(4,128)(2,1)} %copy.73), calls=%async_computation.1 | async-start | bytes 147456 | tf_op jit(solution)/shard_map/all_to_all | solution.py:107
  111.3 0.9 copy.78
  112.2 3.2 %all-to-all-done.1 = bf16[2,4,3,1536]{3,1,2,0:T(4,128)(2,1)S(1)} async-done(((bf16[2,4,3,1536]{3,1,2,0:T(4,128)(2,1)}), bf16[2,4,3,1536]{3,1,2,0:T(4,128)(2,1)S(1)}, u32[]{:S(2)}, u32[]{:S(2)}) %all-to-all-start.1) | async-done | bytes 73760 | tf_op jit(solution)/shard_map/all_to_all | solution.py:107
  116.2 4.9 %all-to-all-start.2 = ((bf16[1,4,3,3072]{3,2,0,1:T(4,128)(2,1)}), bf16[1,4,3,3072]{3,2,0,1:T(4,128)(2,1)S(1)}, u32[]{:S(2)}, u32[]{:S(2)}) async-start(bf16[1,4,3,3072]{3,2,0,1:T(4,128)(2,1)} %reshape.166), calls=%async_computation.2 | async-start | bytes 196608 | tf_op jit(solution)/shard_map/all_to_all | solution.py:106
  121.1 5.8 %all-to-all-done.2 = bf16[1,4,3,3072]{3,2,0,1:T(4,128)(2,1)S(1)} async-done(((bf16[1,4,3,3072]{3,2,0,1:T(4,128)(2,1)}), bf16[1,4,3,3072]{3,2,0,1:T(4,128)(2,1)S(1)}, u32[]{:S(2)}, u32[]{:S(2)}) %all-to-all-start.2) | async-done | bytes 73760 | tf_op jit(solution)/shard_map/all_to_all | solution.py:106
  127.6 0.8 multiply_reduce_fusion.1
  (48 shorter events, 4.6 us)
Async XLA Ops:
  7.2 11.3 %copy-start = (bf16[128,1024]{1,0:T(8,128)(2,1)S(1)}, bf16[128,1024]{1,0:T(8,128)(2,1)}, u32[]{:S(2)}) copy-start(bf16[128,1024]{1,0:T(8,128)(2,1)} %param.13) | copy-start | bytes 786436
  10.0 46.7 %all-to-all-start = ((bf16[4,3,3072]{2,1,0:T(4,128)(2,1)}), bf16[4,3,3072]{2,1,0:T(4,128)(2,1)S(1)}, u32[]{:S(2)}, u32[]{:S(2)}) async-start(bf16[4,3,3072]{2,1,0:T(4,128)(2,1)} %reshape.141), calls=%async_computation | async-start | bytes 196608 | tf_op jit(solution)/shard_map/all_to_all | solution.py:87
  16.3 77.0 %all-reduce.2.cloned.1.call-start = ((), (), s32[]{:S(2)}) async-start(), calls=%async_computation.3 | async-start | bytes 442368 | tf_op jit(solution)/shard_map/psum | solution.py:96
  62.0 66.4 %copy-start.1 = (bf16[128,1024]{1,0:T(8,128)(2,1)S(1)}, bf16[128,1024]{1,0:T(8,128)(2,1)}, u32[]{:S(2)}) copy-start(bf16[128,1024]{1,0:T(8,128)(2,1)} %param.13) | copy-start | bytes 786436
  62.0 50.1 %copy-start.2 = (f32[4,2]{0,1:T(2,128)S(1)}, f32[4,2]{0,1:T(2,128)}, u32[]{:S(2)}) copy-start(f32[4,2]{0,1:T(2,128)} %param.17) | copy-start | bytes 100
  108.0 7.5 %all-to-all-start.1 = ((bf16[2,4,3,1536]{3,1,2,0:T(4,128)(2,1)}), bf16[2,4,3,1536]{3,1,2,0:T(4,128)(2,1)S(1)}, u32[]{:S(2)}, u32[]{:S(2)}) async-start(bf16[2,4,3,1536]{3,1,2,0:T(4,128)(2,1)} %copy.73), calls=%async_computation.1 | async-start | bytes 147456 | tf_op jit(solution)/shard_map/all_to_all | solution.py:107
  116.2 10.7 %all-to-all-start.2 = ((bf16[1,4,3,3072]{3,2,0,1:T(4,128)(2,1)}), bf16[1,4,3,3072]{3,2,0,1:T(4,128)(2,1)S(1)}, u32[]{:S(2)}, u32[]{:S(2)}) async-start(bf16[1,4,3,3072]{3,2,0,1:T(4,128)(2,1)} %reshape.166), calls=%async_computation.2 | async-start | bytes 196608 | tf_op jit(solution)/shard_map/all_to_all | solution.py:106
Sparse Core Ops, SparseCore 0:
  73.9 19.2 all-reduce.1
where the time goes:
time: 136 us; the launch traced here: 135 us
  waiting for transfers between devices  28.4 us (21%)
  local copies, waits for them, and re-layouts  27.9 us (21%)
  blocking collectives  23.9 us (18%)
  matrix products  22.9 us (17%)
  starting transfers between devices  14.5 us (11%)
  between operations  14.2 us (10%)
  other arithmetic  3.33 us (2%)
    unnamed x14, local copies, waits for them, and re-layouts  22.7 us
    psum x1, waiting for transfers between devices, on_device(): lax.psum(partial_value.astype(jnp.bfloat16), 'tp').astype(jnp.float32)  19.4 us
    all_gather x2, blocking collectives, prefix(): lax.all_gather(part.astype(kind), axis)  12.6 us
    dot_general x1, matrix products, on_device(): jnp.dot(lax.all_gather(slot_rows, 'ctx', axis=0, tiled=True), w_both, pre...  11.7 us
    dot_general x1, matrix products, on_device(): jnp.dot(lax.all_gather(hidden, 'ctx', axis=1, tiled=True), w_down, prefer...  6.96 us
    all_to_all x1, starting transfers between devices, on_device(): lax.all_to_all(send, 'exp', split_axis=0, concat_axis=0, tiled=True)  6.32 us
    all_gather x1, blocking collectives, on_device(): lax.all_gather(hidden, 'ctx', axis=1, tiled=True)  5.94 us
    all_to_all x1, waiting for transfers between devices, on_device(): lax.all_to_all(lax.all_to_all(stacked, 'ctx', split_axis=0, concat_axis=3...  5.82 us
  transfers between devices with their start and end apart: 4, of which 3 were waited for; matrix products, arithmetic and copies ran while one was open for 21% of the time, Pallas kernels for 0%

commit v1 on v0

--- a/solution.py
+++ b/solution.py
@@ -1,7 +1,17 @@
+import functools
+
 import jax
 import jax.numpy as jnp
 from jax import lax
+from jax.experimental import pallas as pl
+from jax.experimental.pallas import tpu as pltpu
 from jax.sharding import PartitionSpec as P
+
+F32, BF16 = (jnp.float32, jnp.bfloat16)
+WHOLE = pl.BlockSpec(memory_space=pltpu.VMEM)
+SCALARS = pl.BlockSpec(memory_space=pltpu.SMEM)
+THERE = pl.BlockSpec(memory_space=pl.ANY)
+MIB = 1 << 20
 
 
 def prefix(shard, axis, combine, identity):
@@ -64,7 +74,7 @@
     return (target, pick)
 
 
-def on_device(queries, keys, values, log_decay, moe_input, route_ids, route_weight, gate_up, down):
+def on_device_any(queries, keys, values, log_decay, moe_input, route_ids, route_weight, gate_up, down):
     qb, cum, intra, local, totals = block_terms(queries, keys, values, log_decay)
     heads = log_decay.shape[1]
     width = local.shape[1]
@@ -115,6 +125,247 @@
     merged_output = jnp.sum(selected_routes * route_weight[:, :, None], axis=1)
     return (attended, merged_output.astype(jnp.bfloat16))
 
+def cost(flops, read, transcendentals=0):
+    return pl.CostEstimate(flops=flops, bytes_accessed=read, transcendentals=transcendentals)
+
+
+def head_columns(h, width):
+    return slice(h * width, (h + 1) * width)
+
+
+def attend_kernel(heads, q_ref, k_ref, v_ref, decay_ref, weights_ref, intra_ref, local_ref, cum_ref, held_ref, sem):
+    fetch = pltpu.make_async_copy(weights_ref, held_ref, sem)
+    fetch.start()
+    rows = q_ref.shape[0]
+    width = q_ref.shape[1] // heads
+    s_at = lax.broadcasted_iota(jnp.int32, (rows, rows), 0)
+    t_at = lax.broadcasted_iota(jnp.int32, (rows, rows), 1)
+    before = (s_at <= t_at).astype(F32)
+    cum_t = jnp.dot(
+        decay_ref[...], before, precision=lax.Precision.HIGHEST, preferred_element_type=F32
+    )
+    cum = jnp.transpose(cum_t)
+    cum_ref[...] = cum
+    for h in range(heads):
+        at = head_columns(h, width)
+        q, k, v = (q_ref[:, at], k_ref[:, at], v_ref[:, at])
+        column, row = (cum[:, h : h + 1], cum_t[h : h + 1, :])
+        decay = jnp.where(s_at >= t_at, jnp.exp(jnp.minimum(column - row, 0.0)), 0.0)
+        scores = lax.dot_general(q, k, (((1,), (1,)), ((), ())), preferred_element_type=F32)
+        intra_ref[:, at] = jnp.dot(
+            (scores * decay).astype(BF16), v, preferred_element_type=F32
+        )
+        rest = jnp.exp(cum[rows - 1 :, h : h + 1] - column)
+        scaled = (k.astype(F32) * rest).astype(BF16)
+        local = lax.dot_general(scaled, v, (((0,), (0,)), ((), ())), preferred_element_type=F32)
+        local_ref[h * width : (h + 1) * width, :] = local.astype(BF16)
+    fetch.wait()
+
+
+def attend(queries, keys, values, log_decay, gate_up):
+    rows, heads = log_decay.shape
+    width = queries.shape[1] // heads
+    return pl.pallas_call(
+        functools.partial(attend_kernel, heads),
+        in_specs=[WHOLE, WHOLE, WHOLE, WHOLE, THERE],
+        out_specs=[WHOLE] * 4,
+        out_shape=[
+            jax.ShapeDtypeStruct(queries.shape, F32),
+            jax.ShapeDtypeStruct((heads * width, width), BF16),
+            jax.ShapeDtypeStruct((rows, heads), F32),
+            pltpu.VMEM(gate_up.shape, BF16),
+        ],
+        scratch_shapes=[pltpu.SemaphoreType.DMA],
+        compiler_params=pltpu.CompilerParams(vmem_limit_bytes=8 * MIB),
+        cost_estimate=cost(6 * rows * rows * heads * width, 2 * gate_up.size, heads * rows * rows),
+        name="attend",
+    )(queries, keys, values, jnp.transpose(log_decay), gate_up)
+
+
+def finish_kernel(heads, q_ref, intra_ref, cum_ref, state_ref, out_ref):
+    width = q_ref.shape[1] // heads
+    for h in range(heads):
+        at = head_columns(h, width)
+        grown = jnp.exp(cum_ref[:, h : h + 1])
+        state = state_ref[h * width : (h + 1) * width, :]
+        mixed = intra_ref[:, at] + grown * jnp.dot(
+            q_ref[:, at], state, preferred_element_type=F32
+        )
+        mean = jnp.mean(mixed * mixed, axis=1, keepdims=True)
+        out_ref[:, at] = (mixed * lax.rsqrt(mean + 1e-06)).astype(BF16)
+
+
+def finish(queries, intra, cum, state):
+    rows, heads = cum.shape
+    return pl.pallas_call(
+        functools.partial(finish_kernel, heads),
+        in_specs=[WHOLE] * 4,
+        out_specs=WHOLE,
+        out_shape=jax.ShapeDtypeStruct(queries.shape, BF16),
+        compiler_params=pltpu.CompilerParams(vmem_limit_bytes=8 * MIB),
+        cost_estimate=cost(2 * queries.size * 128, 10 * queries.size, queries.size),
+        name="finish",
+    )(queries, intra, cum, state)
+
+
+def gate_up_kernel(x_ref, weights_ref, down_ref, sums_ref, held_ref, spread, sem):
+    fetch = pltpu.make_async_copy(down_ref, held_ref, sem)
+    fetch.start()
+    depth, _, units = weights_ref.shape
+    rows = x_ref.shape[0] * x_ref.shape[1]
+    lanes = 128
+    source = lax.broadcasted_iota(jnp.int32, (lanes, 2 * lanes), 0)
+    goal = lax.broadcasted_iota(jnp.int32, (lanes, 2 * lanes), 1)
+    even = (goal == 2 * source).astype(BF16)
+    odd = (goal == 2 * source + 1).astype(BF16)
+    x = x_ref[...].reshape(rows, depth)
+    for b in range(depth // lanes):
+        part = x[:, b * lanes : (b + 1) * lanes]
+        to = slice(2 * b * lanes, 2 * (b + 1) * lanes)
+        spread[:rows, to] = jnp.dot(part, even, preferred_element_type=F32).astype(BF16)
+        spread[rows:, to] = jnp.dot(part, odd, preferred_element_type=F32).astype(BF16)
+    step = 768
+    total = jnp.zeros((2 * rows, units), F32)
+    for start in range(0, depth, step):
+        weights = weights_ref[start : start + step].reshape(2 * step, units)
+        total += jnp.dot(
+            spread[:, 2 * start : 2 * (start + step)], weights, preferred_element_type=F32
+        )
+    sums_ref[...] = total.astype(BF16)
+    fetch.wait()
+
+
+def gate_up_sums(x, weights, down):
+    rows = x.shape[0] * x.shape[1]
+    depth, _, units = weights.shape
+    return pl.pallas_call(
+        gate_up_kernel,
+        in_specs=[WHOLE, WHOLE, THERE],
+        out_specs=[WHOLE, WHOLE],
+        out_shape=[
+            jax.ShapeDtypeStruct((2 * rows, units), BF16),
+            pltpu.VMEM(down.shape, BF16),
+        ],
+        scratch_shapes=[pltpu.VMEM((2 * rows, 2 * depth), BF16), pltpu.SemaphoreType.DMA],
+        compiler_params=pltpu.CompilerParams(vmem_limit_bytes=8 * MIB),
+        cost_estimate=cost(4 * rows * weights.size, 2 * weights.size),
+        name="gate_up_sums",
+    )(x, pltpu.with_memory_space_constraint(weights, pltpu.VMEM), down)
+
+
+def hidden_kernel(own_ref, other_ref, out_ref):
+    rows = out_ref.shape[0]
+    summed = own_ref[...].astype(F32) + other_ref[...].astype(F32)
+    gate, up = (summed[:rows], summed[rows:])
+    out_ref[...] = (gate / (1.0 + jnp.exp(-gate)) * up).astype(BF16)
+
+
+def hidden_units(own, other):
+    rows, units = own.shape
+    return pl.pallas_call(
+        hidden_kernel,
+        in_specs=[WHOLE] * 2,
+        out_specs=WHOLE,
+        out_shape=jax.ShapeDtypeStruct((rows // 2, units), BF16),
+        compiler_params=pltpu.CompilerParams(vmem_limit_bytes=8 * MIB),
+        cost_estimate=cost(4 * own.size, 5 * own.size, own.size // 2),
+        name="hidden_units",
+    )(own, other)
+
+
+def down_own_kernel(here_ref, hidden_ref, down_ref, out_ref):
+    units = hidden_ref.shape[1]
+    first = pl.multiple_of(here_ref[0] * units, units)
+    out_ref[...] = jnp.dot(
+        hidden_ref[...], down_ref[pl.ds(first, units), :], preferred_element_type=F32
+    )
+
+
+def down_other_kernel(here_ref, hidden_ref, down_ref, own_ref, out_ref):
+    units = hidden_ref.shape[1]
+    first = pl.multiple_of(here_ref[0] * units, units)
+    total = own_ref[...] + jnp.dot(
+        hidden_ref[...], down_ref[pl.ds(first, units), :], preferred_element_type=F32
+    )
+    out_ref[...] = total.astype(BF16).reshape(out_ref.shape)
+
+
+def down_sums(place, hidden, down, own=None, peers=None):
+    rows, units = hidden.shape
+    columns = down.shape[1]
+    place = place.astype(jnp.int32).reshape(1)
+    down = pltpu.with_memory_space_constraint(down, pltpu.VMEM)
+    if own is None:
+        kernel, operands = (down_own_kernel, (place, hidden, down))
+        out_shape = jax.ShapeDtypeStruct((rows, columns), F32)
+    else:
+        kernel, operands = (down_other_kernel, (place, hidden, down, own))
+        out_shape = jax.ShapeDtypeStruct((peers, rows // peers, columns), BF16)
+    return pl.pallas_call(
+        kernel,
+        in_specs=[SCALARS] + [WHOLE] * (len(operands) - 1),
+        out_specs=WHOLE,
+        out_shape=out_shape,
+        compiler_params=pltpu.CompilerParams(vmem_limit_bytes=8 * MIB),
+        cost_estimate=cost(2 * rows * units * columns, 2 * units * columns),
+        name="down_own" if own is None else "down_other",
+    )(*operands)
+
+
+def merge_kernel(ids_ref, weight_ref, back_ref, out_ref):
+    ctx_count, _, rows, columns = back_ref.shape
+    for i in range(rows):
+        for c in range(ctx_count):
+            picked = [
+                back_ref[c, ids_ref[k, i], i : i + 1, :].astype(F32) * weight_ref[k, i]
+                for k in range(2)
+            ]
+            out_ref[i : i + 1, c * columns : (c + 1) * columns] = (picked[0] + picked[1]).astype(BF16)
+
+
+def merge(route_ids, route_weight, back):
+    ctx_count, _, rows, columns = back.shape
+    return pl.pallas_call(
+        merge_kernel,
+        in_specs=[SCALARS, SCALARS, WHOLE],
+        out_specs=WHOLE,
+        out_shape=jax.ShapeDtypeStruct((rows, ctx_count * columns), BF16),
+        compiler_params=pltpu.CompilerParams(vmem_limit_bytes=8 * MIB),
+        cost_estimate=cost(4 * back.size, 2 * back.size),
+        name="merge",
+    )(jnp.transpose(route_ids), jnp.transpose(route_weight), back)
+
+
+def on_device(queries, keys, values, log_decay, moe_input, route_ids, route_weight, gate_up, down):
+    ctx_count, expert_list = (lax.axis_size("ctx"), lax.axis_size("exp"))
+    if ctx_count != 2 or lax.axis_size("tp") != 2 or gate_up.shape[3] % 128:
+        return on_device_any(
+            queries, keys, values, log_decay, moe_input, route_ids, route_weight, gate_up, down
+        )
+    here = lax.axis_index("ctx")
+    peers = ctx_count * expert_list
+    swap = [(0, 1), (1, 0)]
+    tokens = lax.all_to_all(
+        jnp.broadcast_to(moe_input[None], (peers,) + moe_input.shape),
+        ("ctx", "exp"),
+        split_axis=0,
+        concat_axis=0,
+        tiled=True,
+    )
+    intra, local, cum, weights = attend(
+        queries, keys, values, log_decay, gate_up.reshape(gate_up.shape[1:])
+    )
+    state = lax.ppermute(local, "ctx", [(0, 1)])
+    sums, w_down = gate_up_sums(tokens, weights, down.reshape(down.shape[1:]))
+    hidden = hidden_units(sums, lax.ppermute(sums, "tp", swap))
+    hidden_other = lax.ppermute(hidden, "ctx", swap)
+    own = down_sums(here, hidden, w_down)
+    expert_out = down_sums(1 - here, hidden_other, w_down, own, peers)
+    back = lax.all_to_all(expert_out, ("ctx", "exp"), split_axis=0, concat_axis=0, tiled=True)
+    attended = finish(queries, intra, cum, state)
+    back = back.reshape((ctx_count, expert_list) + back.shape[1:])
+    return (attended, merge(route_ids, route_weight, back))
+
 
 def solution(mesh):
     in_specs = (

time: 136 us -> 80 us (0.59)
  blocking collectives: 23.9 us -> 0 us
  matrix products: 22.9 us -> 0 us
  Pallas kernels: 0 us -> 21.4 us
  waiting for transfers between devices: 28.4 us -> 7.37 us
  between operations: 14.2 us -> 0.71 us
  local copies, waits for them, and re-layouts: 27.9 us -> 33.5 us
  other arithmetic: 3.33 us -> 0 us
  starting transfers between devices: 14.5 us -> 16.4 us
    all_gather x4 -> x0, blocking collectives: 23.9 us -> none  [the longest x2 12.6 us: prefix(): lax.all_gather(part.astype(kind), axis)]
    dot_general x6 -> x0, matrix products: 22.9 us -> none  [the longest x1 11.7 us: on_device(): jnp.dot(lax.all_gather(slot_rows, 'ctx', axis=0, tiled=True), w_both, pre...]
    pallas_call x0 -> x7, Pallas kernels: none -> 21.4 us  [the longest x1 9.07 us: attend(): pl.pallas_call(functools.partial(attend_kernel, heads), in_specs=[WHOLE,...]
    psum x1 -> x0, waiting for transfers between devices: 19.4 us -> none  [on_device(): lax.psum(partial_value.astype(jnp.bfloat16), 'tp').astype(jnp.float32)]
    unnamed x14 -> x22, local copies, waits for them, and re-layouts: 22.7 us -> 32 us
    ppermute x0 -> x3, starting transfers between devices: none -> 4.02 us  [the longest x1 2.08 us: on_device(): hidden_other = lax.ppermute(hidden, 'ctx', swap)]
    all_to_all x3 -> x2, waiting for transfers between devices: 9.02 us -> 5.78 us  [the longest x1 5.78 us: on_device(): lax.all_to_all(expert_out, ('ctx', 'exp'), split_axis=0, concat_axis=0, t...]
    reshape x7 -> x0, local copies, waits for them, and re-layouts: 2.75 us -> none  [the longest x1 1.14 us: block_terms(): kb = keys.reshape(rows, heads, -1)]
  transfers between devices with their start and end apart: 4 -> 5, of which waited for: 3 -> 2; matrix products, arithmetic and copies ran while one was open for 21% -> 0% of each run, Pallas kernels for 0% -> 17%
where the time goes in v1:
time: 80 us; the launch traced here: 79.4 us
  local copies, waits for them, and re-layouts  33.5 us (42%)
  Pallas kernels  21.4 us (27%)
  starting transfers between devices  16.4 us (20%)
  waiting for transfers between devices  7.37 us (9%)
    unnamed x22, local copies, waits for them, and re-layouts  32 us
    pallas_call x1, Pallas kernels, attend(): pl.pallas_call(functools.partial(attend_kernel, heads), in_specs=[WHOLE,...  9.07 us
    all_to_all x1, starting transfers between devices, on_device(): lax.all_to_all(jnp.broadcast_to(moe_input[None], (peers,) + moe_input.sha...  7.25 us
    pallas_call x1, Pallas kernels, gate_up_sums(): pl.pallas_call(gate_up_kernel, in_specs=[WHOLE, WHOLE, THERE], out_specs=...  6.27 us
    all_to_all x1, waiting for transfers between devices, on_device(): lax.all_to_all(expert_out, ('ctx', 'exp'), split_axis=0, concat_axis=0, t...  5.78 us
    all_to_all x1, starting transfers between devices, on_device(): lax.all_to_all(expert_out, ('ctx', 'exp'), split_axis=0, concat_axis=0, t...  5.08 us
    pallas_call x2, Pallas kernels, down_sums(): pl.pallas_call(kernel, in_specs=[SCALARS] + [WHOLE] * (len(operands) - 1)...  3.27 us
    ppermute x1, starting transfers between devices, on_device(): hidden_other = lax.ppermute(hidden, 'ctx', swap)  2.08 us
  transfers between devices with their start and end apart: 5, of which 2 were waited for; matrix products, arithmetic and copies ran while one was open for 0% of the time, Pallas kernels for 17%

profile of v1, /device:TPU:0, one launch (start us, length us, event | category | flops | bytes accessed | tf_op | source)
XLA Modules:
  0.0 79.4 jit_solution(1733743229388955429)
XLA Ops:
  0.6 1.5 %broadcast_in_dim.2 = bf16[8,4,3072]{2,1,0:T(4,128)(2,1)} broadcast(bf16[4,3072]{1,0:T(4,128)(2,1)} %param.13), dimensions={1,2} | broadcast | bytes 221184 | tf_op jit(solution)/shard_map/broadcast_in_dim | solution.py:349
  2.1 7.3 %all-to-all-start = ((bf16[8,4,3072]{2,1,0:T(4,128)(2,1)}), bf16[8,4,3072]{2,1,0:T(4,128)(2,1)S(1)}, u32[]{:S(2)}, u32[]{:S(2)}) async-start(bf16[8,4,3072]{2,1,0:T(4,128)(2,1)} %broadcast_in_dim.2), calls=%async_computation | async-start | bytes 393216 | tf_op jit(solution)/shard_map/all_to_all | solution.py:348
  9.4 0.9 %copy-done.4 = bf16[128,1024]{1,0:T(8,128)(2,1)S(1)} copy-done((bf16[128,1024]{1,0:T(8,128)(2,1)S(1)}, bf16[128,1024]{1,0:T(8,128)(2,1)}, u32[]{:S(2)}) %copy-start.4) | copy-done | bytes 262168
  10.3 0.9 %copy-done.6 = bf16[128,1024]{1,0:T(8,128)(2,1)S(1)} copy-done((bf16[128,1024]{1,0:T(8,128)(2,1)S(1)}, bf16[128,1024]{1,0:T(8,128)(2,1)}, u32[]{:S(2)}) %copy-start.6) | copy-done | bytes 262168
  11.3 0.9 %copy-done.7 = bf16[128,1024]{1,0:T(8,128)(2,1)S(1)} copy-done((bf16[128,1024]{1,0:T(8,128)(2,1)S(1)}, bf16[128,1024]{1,0:T(8,128)(2,1)}, u32[]{:S(2)}) %copy-start.7) | copy-done | bytes 262168
  12.2 0.7 copy-done.8
  12.9 9.1 %attend.1 = (f32[128,1024]{1,0:T(8,128)S(1)}, bf16[1024,128]{1,0:T(8,128)(2,1)S(1)}, f32[128,8]{1,0:T(8,128)S(1)}, bf16[3072,2,2304]{2,1,0:T(2,128)(2,1)S(1)}) custom-call(bf16[128,1024]{1,0:T(8,128)(2,1)S(1)} %copy-done.4, bf16[128,1024]{1,0:T(8,128)(2,1)S(1)} %copy-done.6, bf16[128,1024]{1,0:T(8,128)(2,1)S(1)} %copy-done.7, f32[8,128]{1,0:T(8,128)S(1)} %bitcast.9, ...), custom_call_target="tpu_custom_call" | custom-call | flops 100663296 | bytes 28311552 | tf_op jit(solution)/shard_map/attend/pallas_call | solution.py:168
  22.0 9.3 %copy-done.2 = bf16[3072,2,2304]{2,1,0:T(2,128)(2,1)} copy-done((bf16[3072,2,2304]{2,1,0:T(2,128)(2,1)}, bf16[3072,2,2304]{2,1,0:T(2,128)(2,1)S(1)}, u32[]{:S(2)}) %copy-start.2) | copy-done | bytes 28311576
  31.3 0.0 all-to-all-done.x_ref
  31.3 9.1 %copy-done.3 = bf16[3072,2,2304]{2,1,0:T(2,128)(2,1)S(1)} copy-done((bf16[3072,2,2304]{2,1,0:T(2,128)(2,1)S(1)}, bf16[3072,2,2304]{2,1,0:T(2,128)(2,1)}, u32[]{:S(2)}) %copy-start.3) | copy-done | bytes 28311576
  40.4 6.3 %gate_up_sums.1 = (bf16[64,2304]{1,0:T(8,128)(2,1)S(1)}, bf16[4608,1536]{1,0:T(8,128)(2,1)S(1)}) custom-call(bf16[8,4,3072]{2,1,0:T(4,128)(2,1)S(1)} %all-to-all-done.x_ref, bf16[3072,2,2304]{2,1,0:T(2,128)(2,1)S(1)} %copy-done.3, bf16[4608,1536]{1,0:T(8,128)(2,1)} %bitcast.13), custom_call_target="tpu_custom_call" | custom-call | flops 1811939328 | bytes 28311552 | tf_op jit(solution)/shard_map/gate_up_sums/pallas_call | solution.py:241
  46.7 5.1 %copy-done = bf16[4608,1536]{1,0:T(8,128)(2,1)} copy-done((bf16[4608,1536]{1,0:T(8,128)(2,1)}, bf16[4608,1536]{1,0:T(8,128)(2,1)S(1)}, u32[]{:S(2)}) %copy-start) | copy-done | bytes 14155800
  51.7 0.0 collective-permute-start.1
  51.7 1.6 %collective-permute-done.1.other_ref = bf16[64,2304]{1,0:T(8,128)(2,1)S(1)} collective-permute-done((bf16[64,2304]{1,0:T(8,128)(2,1)S(1)}, bf16[64,2304]{1,0:T(8,128)(2,1)S(1)}, u32[]{:S(2)}, u32[]{:S(2)}) %collective-permute-start.1) | collective-permute-done | bytes 294944 | tf_op jit(solution)/shard_map/ppermute | solution.py:360
  53.3 0.1 hidden_units.1.hidden_ref
  53.4 2.1 %collective-permute-start.2 = (bf16[32,2304]{1,0:T(8,128)(2,1)S(1)}, bf16[32,2304]{1,0:T(8,128)(2,1)S(1)}, u32[]{:S(2)}, u32[]{:S(2)}) collective-permute-start(bf16[32,2304]{1,0:T(8,128)(2,1)S(1)} %hidden_units.1.hidden_ref), channel_id=1, source_target_pairs={{0,8},{8,0},{1,9},{9,1},{2,10},{10,2},{3,11},{11,3},{4,12},{12,4},... | collective-permute-start | bytes 442376 | tf_op jit(solution)/shard_map/ppermute | solution.py:361
  55.5 1.9 %collective-permute-start = (bf16[1024,128]{1,0:T(8,128)(2,1)S(1)}, bf16[1024,128]{1,0:T(8,128)(2,1)S(1)}, u32[]{:S(2)}, u32[]{:S(2)}) collective-permute-start(bf16[1024,128]{1,0:T(8,128)(2,1)S(1)} %get-tuple-element.10), channel_id=1, source_target_pairs={{0,8},{1,9},{2,10},{3,11},{4,12},{5,13},{6,14},{7,15},{16,24},{17,... | collective-permute-start | bytes 786440 | tf_op jit(solution)/shard_map/ppermute | solution.py:358
  57.5 5.0 %copy-done.1 = bf16[4608,1536]{1,0:T(8,128)(2,1)S(1)} copy-done((bf16[4608,1536]{1,0:T(8,128)(2,1)S(1)}, bf16[4608,1536]{1,0:T(8,128)(2,1)}, u32[]{:S(2)}) %copy-start.1) | copy-done | bytes 14155800
  62.5 1.3 %down_own.1.own_ref = f32[32,1536]{1,0:T(8,128)S(1)} custom-call(s32[1]{0:T(128)} %bitcast.6.here_ref, bf16[32,2304]{1,0:T(8,128)(2,1)S(1)} %hidden_units.1.hidden_ref, bf16[4608,1536]{1,0:T(8,128)(2,1)S(1)} %copy-done.1), custom_call_target="tpu_custom_call" | custom-call | flops 226492416 | bytes 7077888 | tf_op jit(solution)/shard_map/down_own/pallas_call | solution.py:304
  63.8 2.0 %down_other.1 = bf16[8,4,1536]{2,1,0:T(4,128)(2,1)} custom-call(s32[1]{0:T(128)} %bitcast.4.here_ref, bf16[32,2304]{1,0:T(8,128)(2,1)S(1)} %collective-permute-done.2.hidden_ref, bf16[4608,1536]{1,0:T(8,128)(2,1)S(1)} %copy-done.1, f32[32,1536]{1,0:T(8,128)S(1)} %down_own.1.own_ref), custom_call_target="tpu_custom_call" | custom-call | flops 226492416 | bytes 7077888 | tf_op jit(solution)/shard_map/down_other/pallas_call | solution.py:304
  65.8 5.1 %all-to-all-start.1 = ((bf16[8,4,1536]{2,1,0:T(4,128)(2,1)}), bf16[8,4,1536]{2,1,0:T(4,128)(2,1)S(1)}, u32[]{:S(2)}, u32[]{:S(2)}) async-start(bf16[8,4,1536]{2,1,0:T(4,128)(2,1)} %down_other.1), calls=%async_computation.1 | async-start | bytes 196608 | tf_op jit(solution)/shard_map/all_to_all | solution.py:364
  70.9 1.5 %finish.1 = bf16[128,1024]{1,0:T(8,128)(2,1)} custom-call(bf16[128,1024]{1,0:T(8,128)(2,1)S(1)} %copy-done.5, f32[128,1024]{1,0:T(8,128)S(1)} %get-tuple-element.8.intra_ref, f32[128,8]{1,0:T(8,128)S(1)} %get-tuple-element.9.cum_ref, bf16[1024,128]{1,0:T(8,128)(2,1)S(1)} %collective-permute-done.state_ref), custom_call_target="tpu_custom_call" | custom-call | flops 33554432 | bytes 1310720 | tf_op jit(solution)/shard_map/finish/pallas_call | solution.py:200
  72.3 5.8 %all-to-all-done.1 = bf16[8,4,1536]{2,1,0:T(4,128)(2,1)S(1)} async-done(((bf16[8,4,1536]{2,1,0:T(4,128)(2,1)}), bf16[8,4,1536]{2,1,0:T(4,128)(2,1)S(1)}, u32[]{:S(2)}, u32[]{:S(2)}) %all-to-all-start.1) | async-done | bytes 98336 | tf_op jit(solution)/shard_map/all_to_all | solution.py:364
  78.1 1.2 %merge.1 = bf16[4,3072]{1,0:T(4,128)(2,1)} custom-call(s32[2,4]{1,0:T(2,128)S(1)} %bitcast.10, f32[2,4]{1,0:T(2,128)S(1)} %bitcast.11, bf16[2,4,4,1536]{3,2,1,0:T(4,128)(2,1)S(1)} %bitcast.8), custom_call_target="tpu_custom_call" | custom-call | flops 196608 | bytes 98304 | tf_op jit(solution)/shard_map/merge/pallas_call | solution.py:328
  (16 shorter events, 0.0 us)
Async XLA Ops:
  2.1 29.2 %all-to-all-start = ((bf16[8,4,3072]{2,1,0:T(4,128)(2,1)}), bf16[8,4,3072]{2,1,0:T(4,128)(2,1)S(1)}, u32[]{:S(2)}, u32[]{:S(2)}) async-start(bf16[8,4,3072]{2,1,0:T(4,128)(2,1)} %broadcast_in_dim.2), calls=%async_computation | async-start | bytes 393216 | tf_op jit(solution)/shard_map/all_to_all | solution.py:348
  9.3 0.9 %copy-start.4 = (bf16[128,1024]{1,0:T(8,128)(2,1)S(1)}, bf16[128,1024]{1,0:T(8,128)(2,1)}, u32[]{:S(2)}) copy-start(bf16[128,1024]{1,0:T(8,128)(2,1)} %q_ref.3) | copy-start | bytes 786436
  10.3 0.9 %copy-start.6 = (bf16[128,1024]{1,0:T(8,128)(2,1)S(1)}, bf16[128,1024]{1,0:T(8,128)(2,1)}, u32[]{:S(2)}) copy-start(bf16[128,1024]{1,0:T(8,128)(2,1)} %k_ref.1) | copy-start | bytes 786436
  11.3 0.9 %copy-start.7 = (bf16[128,1024]{1,0:T(8,128)(2,1)S(1)}, bf16[128,1024]{1,0:T(8,128)(2,1)}, u32[]{:S(2)}) copy-start(bf16[128,1024]{1,0:T(8,128)(2,1)} %v_ref.1) | copy-start | bytes 786436
  12.2 0.7 copy-start.8
  22.0 9.3 %copy-start.2 = (bf16[3072,2,2304]{2,1,0:T(2,128)(2,1)}, bf16[3072,2,2304]{2,1,0:T(2,128)(2,1)S(1)}, u32[]{:S(2)}) copy-start(bf16[3072,2,2304]{2,1,0:T(2,128)(2,1)S(1)} %get-tuple-element.11.weights_ref) | copy-start | bytes 84934656
  31.3 9.1 %copy-start.3 = (bf16[3072,2,2304]{2,1,0:T(2,128)(2,1)S(1)}, bf16[3072,2,2304]{2,1,0:T(2,128)(2,1)}, u32[]{:S(2)}) copy-start(bf16[3072,2,2304]{2,1,0:T(2,128)(2,1)} %copy-done.2) | copy-start | bytes 84934656
  40.4 30.5 %copy-start.5 = (bf16[128,1024]{1,0:T(8,128)(2,1)S(1)}, bf16[128,1024]{1,0:T(8,128)(2,1)}, u32[]{:S(2)}) copy-start(bf16[128,1024]{1,0:T(8,128)(2,1)} %q_ref.3) | copy-start | bytes 786436
  40.4 37.7 %copy-start.9 = (s32[4,2]{0,1:T(2,128)S(1)}, s32[4,2]{0,1:T(2,128)}, u32[]{:S(2)}) copy-start(s32[4,2]{0,1:T(2,128)} %param.14) | copy-start | bytes 100
  40.4 37.7 %copy-start.10 = (f32[4,2]{0,1:T(2,128)S(1)}, f32[4,2]{0,1:T(2,128)}, u32[]{:S(2)}) copy-start(f32[4,2]{0,1:T(2,128)} %param.15) | copy-start | bytes 100
  46.6 5.1 %copy-start = (bf16[4608,1536]{1,0:T(8,128)(2,1)}, bf16[4608,1536]{1,0:T(8,128)(2,1)S(1)}, u32[]{:S(2)}) copy-start(bf16[4608,1536]{1,0:T(8,128)(2,1)S(1)} %get-tuple-element.13.down_ref) | copy-start | bytes 42467332
  51.7 1.6 %collective-permute-start.1 = (bf16[64,2304]{1,0:T(8,128)(2,1)S(1)}, bf16[64,2304]{1,0:T(8,128)(2,1)S(1)}, u32[]{:S(2)}, u32[]{:S(2)}) collective-permute-start(bf16[64,2304]{1,0:T(8,128)(2,1)S(1)} %get-tuple-element.12.own_ref), channel_id=1, source_target_pairs={{0,1},{1,0},{2,3},{3,2},{4,5},{5,4},{6,7},{7,6},{8,9},{9,8},{10,11... | collective-permute-start | bytes 884744 | tf_op jit(solution)/shard_map/ppermute | solution.py:360
  53.4 10.4 %collective-permute-start.2 = (bf16[32,2304]{1,0:T(8,128)(2,1)S(1)}, bf16[32,2304]{1,0:T(8,128)(2,1)S(1)}, u32[]{:S(2)}, u32[]{:S(2)}) collective-permute-start(bf16[32,2304]{1,0:T(8,128)(2,1)S(1)} %hidden_units.1.hidden_ref), channel_id=1, source_target_pairs={{0,8},{8,0},{1,9},{9,1},{2,10},{10,2},{3,11},{11,3},{4,12},{12,4},... | collective-permute-start | bytes 442376 | tf_op jit(solution)/shard_map/ppermute | solution.py:361
  55.5 15.3 %collective-permute-start = (bf16[1024,128]{1,0:T(8,128)(2,1)S(1)}, bf16[1024,128]{1,0:T(8,128)(2,1)S(1)}, u32[]{:S(2)}, u32[]{:S(2)}) collective-permute-start(bf16[1024,128]{1,0:T(8,128)(2,1)S(1)} %get-tuple-element.10), channel_id=1, source_target_pairs={{0,8},{1,9},{2,10},{3,11},{4,12},{5,13},{6,14},{7,15},{16,24},{17,... | collective-permute-start | bytes 786440 | tf_op jit(solution)/shard_map/ppermute | solution.py:358
  57.5 5.0 %copy-start.1 = (bf16[4608,1536]{1,0:T(8,128)(2,1)S(1)}, bf16[4608,1536]{1,0:T(8,128)(2,1)}, u32[]{:S(2)}) copy-start(bf16[4608,1536]{1,0:T(8,128)(2,1)} %copy-done) | copy-start | bytes 42467332
  65.8 12.3 %all-to-all-start.1 = ((bf16[8,4,1536]{2,1,0:T(4,128)(2,1)}), bf16[8,4,1536]{2,1,0:T(4,128)(2,1)S(1)}, u32[]{:S(2)}, u32[]{:S(2)}) async-start(bf16[8,4,1536]{2,1,0:T(4,128)(2,1)} %down_other.1), calls=%async_computation.1 | async-start | bytes 196608 | tf_op jit(solution)/shard_map/all_to_all | solution.py:364

commit v2 on v1

--- a/solution.py
+++ b/solution.py
@@ -133,19 +133,24 @@
     return slice(h * width, (h + 1) * width)
 
 
-def attend_kernel(heads, q_ref, k_ref, v_ref, decay_ref, weights_ref, intra_ref, local_ref, cum_ref, held_ref, sem):
-    fetch = pltpu.make_async_copy(weights_ref, held_ref, sem)
-    fetch.start()
+def attend_kernel(heads, q_hbm, k_hbm, v_hbm, decay_hbm, intra_ref, local_ref, cum_ref, q_ref, k_ref, v_ref, decay_ref, sems):
+    pairs = ((decay_hbm, decay_ref), (q_hbm, q_ref), (k_hbm, k_ref), (v_hbm, v_ref))
+    fetches = [pltpu.make_async_copy(a, b, sems.at[i]) for i, (a, b) in enumerate(pairs)]
+    for fetch in fetches:
+        fetch.start()
     rows = q_ref.shape[0]
     width = q_ref.shape[1] // heads
     s_at = lax.broadcasted_iota(jnp.int32, (rows, rows), 0)
     t_at = lax.broadcasted_iota(jnp.int32, (rows, rows), 1)
     before = (s_at <= t_at).astype(F32)
+    fetches[0].wait()
     cum_t = jnp.dot(
         decay_ref[...], before, precision=lax.Precision.HIGHEST, preferred_element_type=F32
     )
     cum = jnp.transpose(cum_t)
     cum_ref[...] = cum
+    for fetch in fetches[1:]:
+        fetch.wait()
     for h in range(heads):
         at = head_columns(h, width)
         q, k, v = (q_ref[:, at], k_ref[:, at], v_ref[:, at])
@@ -159,27 +164,26 @@
         scaled = (k.astype(F32) * rest).astype(BF16)
         local = lax.dot_general(scaled, v, (((0,), (0,)), ((), ())), preferred_element_type=F32)
         local_ref[h * width : (h + 1) * width, :] = local.astype(BF16)
-    fetch.wait()
-
-
-def attend(queries, keys, values, log_decay, gate_up):
+
+
+def attend(queries, keys, values, log_decay):
     rows, heads = log_decay.shape
     width = queries.shape[1] // heads
     return pl.pallas_call(
         functools.partial(attend_kernel, heads),
-        in_specs=[WHOLE, WHOLE, WHOLE, WHOLE, THERE],
-        out_specs=[WHOLE] * 4,
+        in_specs=[THERE] * 4,
+        out_specs=[WHOLE] * 3,
         out_shape=[
             jax.ShapeDtypeStruct(queries.shape, F32),
             jax.ShapeDtypeStruct((heads * width, width), BF16),
             jax.ShapeDtypeStruct((rows, heads), F32),
-            pltpu.VMEM(gate_up.shape, BF16),
         ],
-        scratch_shapes=[pltpu.SemaphoreType.DMA],
-        compiler_params=pltpu.CompilerParams(vmem_limit_bytes=8 * MIB),
-        cost_estimate=cost(6 * rows * rows * heads * width, 2 * gate_up.size, heads * rows * rows),
+        scratch_shapes=[pltpu.VMEM(queries.shape, BF16)] * 3
+        + [pltpu.VMEM((heads, rows), F32), pltpu.SemaphoreType.DMA((4,))],
+        compiler_params=pltpu.CompilerParams(vmem_limit_bytes=8 * MIB),
+        cost_estimate=cost(6 * rows * rows * heads * width, 6 * queries.size, heads * rows * rows),
         name="attend",
-    )(queries, keys, values, jnp.transpose(log_decay), gate_up)
+    )(queries, keys, values, jnp.transpose(log_decay))
 
 
 def finish_kernel(heads, q_ref, intra_ref, cum_ref, state_ref, out_ref):
@@ -208,10 +212,17 @@
     )(queries, intra, cum, state)
 
 
-def gate_up_kernel(x_ref, weights_ref, down_ref, sums_ref, held_ref, spread, sem):
-    fetch = pltpu.make_async_copy(down_ref, held_ref, sem)
-    fetch.start()
+def gate_up_kernel(step, x_ref, weights_hbm, sums_ref, weights_ref, spread, sems):
     depth, _, units = weights_ref.shape
+    starts = range(0, depth, step)
+    fetches = [
+        pltpu.make_async_copy(
+            weights_hbm.at[pl.ds(start, step)], weights_ref.at[pl.ds(start, step)], sems.at[i]
+        )
+        for i, start in enumerate(starts)
+    ]
+    for fetch in fetches:
+        fetch.start()
     rows = x_ref.shape[0] * x_ref.shape[1]
     lanes = 128
     source = lax.broadcasted_iota(jnp.int32, (lanes, 2 * lanes), 0)
@@ -224,33 +235,34 @@
         to = slice(2 * b * lanes, 2 * (b + 1) * lanes)
         spread[:rows, to] = jnp.dot(part, even, preferred_element_type=F32).astype(BF16)
         spread[rows:, to] = jnp.dot(part, odd, preferred_element_type=F32).astype(BF16)
-    step = 768
     total = jnp.zeros((2 * rows, units), F32)
-    for start in range(0, depth, step):
+    for start, fetch in zip(starts, fetches):
+        fetch.wait()
         weights = weights_ref[start : start + step].reshape(2 * step, units)
         total += jnp.dot(
             spread[:, 2 * start : 2 * (start + step)], weights, preferred_element_type=F32
         )
     sums_ref[...] = total.astype(BF16)
-    fetch.wait()
-
-
-def gate_up_sums(x, weights, down):
+
+
+def gate_up_sums(x, weights):
     rows = x.shape[0] * x.shape[1]
     depth, _, units = weights.shape
-    return pl.pallas_call(
-        gate_up_kernel,
-        in_specs=[WHOLE, WHOLE, THERE],
-        out_specs=[WHOLE, WHOLE],
-        out_shape=[
-            jax.ShapeDtypeStruct((2 * rows, units), BF16),
-            pltpu.VMEM(down.shape, BF16),
+    step = 384
+    return pl.pallas_call(
+        functools.partial(gate_up_kernel, step),
+        in_specs=[WHOLE, THERE],
+        out_specs=WHOLE,
+        out_shape=jax.ShapeDtypeStruct((2 * rows, units), BF16),
+        scratch_shapes=[
+            pltpu.VMEM(weights.shape, BF16),
+            pltpu.VMEM((2 * rows, 2 * depth), BF16),
+            pltpu.SemaphoreType.DMA((depth // step,)),
         ],
-        scratch_shapes=[pltpu.VMEM((2 * rows, 2 * depth), BF16), pltpu.SemaphoreType.DMA],
-        compiler_params=pltpu.CompilerParams(vmem_limit_bytes=8 * MIB),
+        compiler_params=pltpu.CompilerParams(vmem_limit_bytes=36 * MIB),
         cost_estimate=cost(4 * rows * weights.size, 2 * weights.size),
         name="gate_up_sums",
-    )(x, pltpu.with_memory_space_constraint(weights, pltpu.VMEM), down)
+    )(x, weights)
 
 
 def hidden_kernel(own_ref, other_ref, out_ref):
@@ -273,37 +285,36 @@
     )(own, other)
 
 
-def down_own_kernel(here_ref, hidden_ref, down_ref, out_ref):
+def down_own_kernel(hidden_ref, down_ref, out_ref):
     units = hidden_ref.shape[1]
-    first = pl.multiple_of(here_ref[0] * units, units)
+    first = pl.multiple_of(lax.axis_index("ctx") * units, units)
     out_ref[...] = jnp.dot(
         hidden_ref[...], down_ref[pl.ds(first, units), :], preferred_element_type=F32
     )
 
 
-def down_other_kernel(here_ref, hidden_ref, down_ref, own_ref, out_ref):
+def down_other_kernel(hidden_ref, down_ref, own_ref, out_ref):
     units = hidden_ref.shape[1]
-    first = pl.multiple_of(here_ref[0] * units, units)
+    first = pl.multiple_of((1 - lax.axis_index("ctx")) * units, units)
     total = own_ref[...] + jnp.dot(
         hidden_ref[...], down_ref[pl.ds(first, units), :], preferred_element_type=F32
     )
     out_ref[...] = total.astype(BF16).reshape(out_ref.shape)
 
 
-def down_sums(place, hidden, down, own=None, peers=None):
+def down_sums(hidden, down, own=None, peers=None):
     rows, units = hidden.shape
     columns = down.shape[1]
-    place = place.astype(jnp.int32).reshape(1)
     down = pltpu.with_memory_space_constraint(down, pltpu.VMEM)
     if own is None:
-        kernel, operands = (down_own_kernel, (place, hidden, down))
+        kernel, operands = (down_own_kernel, (hidden, down))
         out_shape = jax.ShapeDtypeStruct((rows, columns), F32)
     else:
-        kernel, operands = (down_other_kernel, (place, hidden, down, own))
+        kernel, operands = (down_other_kernel, (hidden, down, own))
         out_shape = jax.ShapeDtypeStruct((peers, rows // peers, columns), BF16)
     return pl.pallas_call(
         kernel,
-        in_specs=[SCALARS] + [WHOLE] * (len(operands) - 1),
+        in_specs=[WHOLE] * len(operands),
         out_specs=WHOLE,
         out_shape=out_shape,
         compiler_params=pltpu.CompilerParams(vmem_limit_bytes=8 * MIB),
@@ -312,24 +323,29 @@
     )(*operands)
 
 
-def merge_kernel(ids_ref, weight_ref, back_ref, out_ref):
-    ctx_count, _, rows, columns = back_ref.shape
-    for i in range(rows):
-        for c in range(ctx_count):
-            picked = [
-                back_ref[c, ids_ref[k, i], i : i + 1, :].astype(F32) * weight_ref[k, i]
-                for k in range(2)
-            ]
-            out_ref[i : i + 1, c * columns : (c + 1) * columns] = (picked[0] + picked[1]).astype(BF16)
+def merge_kernel(ids_ref, weight_ref, back_ref, out_ref, table):
+    ctx_count, experts, rows, columns = back_ref.shape
+    ids, weight = (ids_ref[...], weight_ref[...])
+    for e in range(experts):
+        table[e : e + 1, :rows] = jnp.sum(
+            jnp.where(ids == e, weight, 0.0), axis=0, keepdims=True
+        )
+    share = jnp.transpose(table[...])
+    for c in range(ctx_count):
+        total = jnp.zeros((rows, columns), F32)
+        for e in range(experts):
+            total += share[:rows, e : e + 1] * back_ref[c, e].astype(F32)
+        out_ref[:, c * columns : (c + 1) * columns] = total.astype(BF16)
 
 
 def merge(route_ids, route_weight, back):
-    ctx_count, _, rows, columns = back.shape
+    ctx_count, experts, rows, columns = back.shape
     return pl.pallas_call(
         merge_kernel,
-        in_specs=[SCALARS, SCALARS, WHOLE],
+        in_specs=[WHOLE] * 3,
         out_specs=WHOLE,
         out_shape=jax.ShapeDtypeStruct((rows, ctx_count * columns), BF16),
+        scratch_shapes=[pltpu.VMEM((8, 128), F32)],
         compiler_params=pltpu.CompilerParams(vmem_limit_bytes=8 * MIB),
         cost_estimate=cost(4 * back.size, 2 * back.size),
         name="merge",
@@ -342,7 +358,6 @@
         return on_device_any(
             queries, keys, values, log_decay, moe_input, route_ids, route_weight, gate_up, down
         )
-    here = lax.axis_index("ctx")
     peers = ctx_count * expert_list
     swap = [(0, 1), (1, 0)]
     tokens = lax.all_to_all(
@@ -352,15 +367,14 @@
         concat_axis=0,
         tiled=True,
     )
-    intra, local, cum, weights = attend(
-        queries, keys, values, log_decay, gate_up.reshape(gate_up.shape[1:])
-    )
+    intra, local, cum = attend(queries, keys, values, log_decay)
     state = lax.ppermute(local, "ctx", [(0, 1)])
-    sums, w_down = gate_up_sums(tokens, weights, down.reshape(down.shape[1:]))
+    sums = gate_up_sums(tokens, gate_up.reshape(gate_up.shape[1:]))
+    sums, w_down = lax.optimization_barrier((sums, down.reshape(down.shape[1:])))
     hidden = hidden_units(sums, lax.ppermute(sums, "tp", swap))
     hidden_other = lax.ppermute(hidden, "ctx", swap)
-    own = down_sums(here, hidden, w_down)
-    expert_out = down_sums(1 - here, hidden_other, w_down, own, peers)
+    own = down_sums(hidden, w_down)
+    expert_out = down_sums(hidden_other, w_down, own, peers)
     back = lax.all_to_all(expert_out, ("ctx", "exp"), split_axis=0, concat_axis=0, tiled=True)
     attended = finish(queries, intra, cum, state)
     back = back.reshape((ctx_count, expert_list) + back.shape[1:])

time: 80 us -> 50.2 us (0.63)
  local copies, waits for them, and re-layouts: 33.5 us -> 0.99 us
  blocking collectives: 0 us -> 15.9 us
  starting transfers between devices: 16.4 us -> 7.44 us
  Pallas kernels: 21.4 us -> 17.5 us
    unnamed x22 -> x20, local copies, waits for them, and re-layouts: 32 us -> 0.05 us
    all_to_all x0 -> x1, blocking collectives: none -> 15.9 us  [on_device(): lax.all_to_all(jnp.broadcast_to(moe_input[None], (peers,) + moe_input.sha...]
    all_to_all x1 -> x0, starting transfers between devices: 7.25 us -> none  [on_device(): lax.all_to_all(jnp.broadcast_to(moe_input[None], (peers,) + moe_input.sha...]
    pallas_call x5, Pallas kernels: 19.9 us -> 15.9 us  [the longest x1 10.6 us: gate_up_sums(): pl.pallas_call(functools.partial(gate_up_kernel, step), in_specs=[WHOLE,...]
    all_to_all x1, starting transfers between devices: 5.08 us -> 3.36 us  [on_device(): lax.all_to_all(expert_out, ('ctx', 'exp'), split_axis=0, concat_axis=0, t...]
    ppermute x1, starting transfers between devices: 2.08 us -> 0.63 us  [on_device(): hidden_other = lax.ppermute(hidden, 'ctx', swap)]
    ppermute x1, starting transfers between devices: 1.93 us -> 3.38 us  [on_device(): state = lax.ppermute(local, 'ctx', [(0, 1)])]
  transfers between devices with their start and end apart: 5 -> 4, of which waited for: 2 -> 2; matrix products, arithmetic and copies ran while one was open for 0% -> 0% of each run, Pallas kernels for 17% -> 12%
where the time goes in v2:
time: 50.2 us; the launch traced here: 49.9 us
  Pallas kernels  17.5 us (35%)
  blocking collectives  15.9 us (32%)
  starting transfers between devices  7.44 us (15%)
  waiting for transfers between devices  7.3 us (15%)
  local copies, waits for them, and re-layouts  0.99 us (2%)
  between operations  0.79 us (2%)
    all_to_all x1, blocking collectives, on_device(): lax.all_to_all(jnp.broadcast_to(moe_input[None], (peers,) + moe_input.sha...  15.9 us
    pallas_call x1, Pallas kernels, gate_up_sums(): pl.pallas_call(functools.partial(gate_up_kernel, step), in_specs=[WHOLE,...  10.6 us
    all_to_all x1, waiting for transfers between devices, on_device(): lax.all_to_all(expert_out, ('ctx', 'exp'), split_axis=0, concat_axis=0, t...  5.72 us
    ppermute x1, starting transfers between devices, on_device(): state = lax.ppermute(local, 'ctx', [(0, 1)])  3.38 us
    all_to_all x1, starting transfers between devices, on_device(): lax.all_to_all(expert_out, ('ctx', 'exp'), split_axis=0, concat_axis=0, t...  3.36 us
    pallas_call x2, Pallas kernels, down_sums(): pl.pallas_call(kernel, in_specs=[WHOLE] * len(operands), out_specs=WHOLE,...  3.28 us
    ppermute x1, waiting for transfers between devices, on_device(): hidden = hidden_units(sums, lax.ppermute(sums, 'tp', swap))  1.57 us
    pallas_call x1, Pallas kernels, finish(): pl.pallas_call(functools.partial(finish_kernel, heads), in_specs=[WHOLE]...  1.46 us
  transfers between devices with their start and end apart: 4, of which 2 were waited for; matrix products, arithmetic and copies ran while one was open for 0% of the time, Pallas kernels for 12%

profile of v2, /device:TPU:0, one launch (start us, length us, event | category | flops | bytes accessed | tf_op | source)
XLA Modules:
  0.0 49.9 jit_solution(16111509587459423302)
XLA Ops:
  0.6 0.0 slice-start
  0.6 0.0 copy-start
  0.7 0.0 copy-start.1
  0.7 0.0 copy-start.2
  0.7 0.0 copy-start.3
  0.7 0.9 %broadcast_in_dim.2 = bf16[8,4,3072]{2,1,0:T(4,128)(2,1)S(1)} broadcast(bf16[4,3072]{1,0:T(4,128)(2,1)} %param.13), dimensions={1,2} | broadcast | bytes 221184 | tf_op jit(solution)/shard_map/broadcast_in_dim | solution.py:364
  1.6 15.9 %all_to_all.10.x_ref = bf16[8,4,3072]{2,1,0:T(4,128)(2,1)S(1)} all-to-all(bf16[8,4,3072]{2,1,0:T(4,128)(2,1)S(1)} %broadcast_in_dim.2), channel_id=1, replica_groups=mesh['groups'=2,'ctx'=2,'exp'=4,'tp'=2] {'ctx','exp'}, dimensions={0} | all-to-all | bytes 393216 | tf_op jit(solution)/shard_map/all_to_all | solution.py:363
  17.5 0.0 copy-start.5
  17.6 10.6 %gate_up_sums.1.own_ref = bf16[64,2304]{1,0:T(8,128)(2,1)S(1)} custom-call(bf16[8,4,3072]{2,1,0:T(4,128)(2,1)S(1)} %all_to_all.10.x_ref, bf16[3072,2,2304]{2,1,0:T(2,128)(2,1)} %bitcast.14), custom_call_target="tpu_custom_call" | custom-call | flops 1811939328 | bytes 28311552 | tf_op jit(solution)/shard_map/gate_up_sums/pallas_call | solution.py:252
  28.1 0.1 collective-permute-start.1
  28.2 1.6 %collective-permute-done.1.other_ref = bf16[64,2304]{1,0:T(8,128)(2,1)S(1)} collective-permute-done((bf16[64,2304]{1,0:T(8,128)(2,1)S(1)}, bf16[64,2304]{1,0:T(8,128)(2,1)S(1)}, u32[]{:S(2)}, u32[]{:S(2)}) %collective-permute-start.1) | collective-permute-done | bytes 294944 | tf_op jit(solution)/shard_map/ppermute | solution.py:374
  29.8 0.1 hidden_units.1.hidden_ref
  29.9 0.6 %collective-permute-start.2 = (bf16[32,2304]{1,0:T(8,128)(2,1)S(1)}, bf16[32,2304]{1,0:T(8,128)(2,1)S(1)}, u32[]{:S(2)}, u32[]{:S(2)}) collective-permute-start(bf16[32,2304]{1,0:T(8,128)(2,1)S(1)} %hidden_units.1.hidden_ref), channel_id=1, source_target_pairs={{0,8},{8,0},{1,9},{9,1},{2,10},{10,2},{3,11},{11,3},{4,12},{12,4},... | collective-permute-start | bytes 442376 | tf_op jit(solution)/shard_map/ppermute | solution.py:375
  30.6 0.0 copy-done.3
  30.6 1.3 %attend.1 = (f32[128,1024]{1,0:T(8,128)S(1)}, bf16[1024,128]{1,0:T(8,128)(2,1)S(1)}, f32[128,8]{1,0:T(8,128)S(1)}) custom-call(bf16[128,1024]{1,0:T(8,128)(2,1)S(1)} %copy-done, bf16[128,1024]{1,0:T(8,128)(2,1)S(1)} %copy-done.1, bf16[128,1024]{1,0:T(8,128)(2,1)S(1)} %copy-done.2, f32[8,128]{1,0:T(8,128)S(1)} %bitcast.11), custom_call_target="tpu_custom_call" | custom-call | flops 100663296 | bytes 786432 | tf_op jit(solution)/shard_map/attend/pallas_call | solution.py:172
  31.8 3.4 %collective-permute-start = (bf16[1024,128]{1,0:T(8,128)(2,1)S(1)}, bf16[1024,128]{1,0:T(8,128)(2,1)S(1)}, u32[]{:S(2)}, u32[]{:S(2)}) collective-permute-start(bf16[1024,128]{1,0:T(8,128)(2,1)S(1)} %get-tuple-element.9), channel_id=1, source_target_pairs={{0,8},{1,9},{2,10},{3,11},{4,12},{5,13},{6,14},{7,15},{16,24},{17,... | collective-permute-start | bytes 786440 | tf_op jit(solution)/shard_map/ppermute | solution.py:371
  35.3 1.3 %down_own.1.own_ref = f32[32,1536]{1,0:T(8,128)S(1)} custom-call(bf16[32,2304]{1,0:T(8,128)(2,1)S(1)} %hidden_units.1.hidden_ref, bf16[4608,1536]{1,0:T(8,128)(2,1)S(1)} %bitcast.8), custom_call_target="tpu_custom_call" | custom-call | flops 226492416 | bytes 7077888 | tf_op jit(solution)/shard_map/down_own/pallas_call | solution.py:315
  36.6 0.0 collective-permute-done.2.hidden_ref
  36.6 2.0 %down_other.1 = bf16[8,4,1536]{2,1,0:T(4,128)(2,1)} custom-call(bf16[32,2304]{1,0:T(8,128)(2,1)S(1)} %collective-permute-done.2.hidden_ref, bf16[4608,1536]{1,0:T(8,128)(2,1)S(1)} %bitcast.9, f32[32,1536]{1,0:T(8,128)S(1)} %down_own.1.own_ref), custom_call_target="tpu_custom_call" | custom-call | flops 226492416 | bytes 7077888 | tf_op jit(solution)/shard_map/down_other/pallas_call | solution.py:315
  38.6 3.4 %all-to-all-start.1 = ((bf16[8,4,1536]{2,1,0:T(4,128)(2,1)}), bf16[8,4,1536]{2,1,0:T(4,128)(2,1)S(1)}, u32[]{:S(2)}, u32[]{:S(2)}) async-start(bf16[8,4,1536]{2,1,0:T(4,128)(2,1)} %down_other.1), calls=%async_computation.1 | async-start | bytes 196608 | tf_op jit(solution)/shard_map/all_to_all | solution.py:378
  41.9 0.0 collective-permute-done.state_ref
  42.0 1.5 %finish.1 = bf16[128,1024]{1,0:T(8,128)(2,1)} custom-call(bf16[128,1024]{1,0:T(8,128)(2,1)S(1)} %copy-done, f32[128,1024]{1,0:T(8,128)S(1)} %get-tuple-element.7.intra_ref, f32[128,8]{1,0:T(8,128)S(1)} %get-tuple-element.8.cum_ref, bf16[1024,128]{1,0:T(8,128)(2,1)S(1)} %collective-permute-done.state_ref), custom_call_target="tpu_custom_call" | custom-call | flops 33554432 | bytes 1310720 | tf_op jit(solution)/shard_map/finish/pallas_call | solution.py:204
  43.4 5.7 %all-to-all-done.1 = bf16[8,4,1536]{2,1,0:T(4,128)(2,1)S(1)} async-done(((bf16[8,4,1536]{2,1,0:T(4,128)(2,1)}), bf16[8,4,1536]{2,1,0:T(4,128)(2,1)S(1)}, u32[]{:S(2)}, u32[]{:S(2)}) %all-to-all-start.1) | async-done | bytes 98336 | tf_op jit(solution)/shard_map/all_to_all | solution.py:378
  49.1 0.8 %merge.1 = bf16[4,3072]{1,0:T(4,128)(2,1)} custom-call(s32[2,4]{1,0:T(2,128)S(1)} %bitcast.12, f32[2,4]{1,0:T(2,128)S(1)} %bitcast.13, bf16[2,4,4,1536]{3,2,1,0:T(4,128)(2,1)S(1)} %bitcast.10), custom_call_target="tpu_custom_call" | custom-call | flops 196608 | bytes 98304 | tf_op jit(solution)/shard_map/merge/pallas_call | solution.py:343
  (14 shorter events, 0.0 us)
Async XLA Ops:
  0.6 34.6 %slice-start = ((s8[14155776]{0:T(1024)(128)(4,1)}), s8[4194304]{0:T(1024)(128)(4,1)S(1)}, s32[]{:S(2)}) async-start(s8[14155776]{0:T(1024)(128)(4,1)} %bitcast.6), calls=%async_computation.2 | async-start | bytes 8388608
  0.6 29.9 %copy-start = (bf16[128,1024]{1,0:T(8,128)(2,1)S(1)}, bf16[128,1024]{1,0:T(8,128)(2,1)}, u32[]{:S(2)}) copy-start(bf16[128,1024]{1,0:T(8,128)(2,1)} %q_ref.1) | copy-start | bytes 786436
  0.7 29.9 %copy-start.1 = (bf16[128,1024]{1,0:T(8,128)(2,1)S(1)}, bf16[128,1024]{1,0:T(8,128)(2,1)}, u32[]{:S(2)}) copy-start(bf16[128,1024]{1,0:T(8,128)(2,1)} %k_hbm.1) | copy-start | bytes 786436
  0.7 29.9 %copy-start.2 = (bf16[128,1024]{1,0:T(8,128)(2,1)S(1)}, bf16[128,1024]{1,0:T(8,128)(2,1)}, u32[]{:S(2)}) copy-start(bf16[128,1024]{1,0:T(8,128)(2,1)} %v_hbm.1) | copy-start | bytes 786436
  0.7 29.9 %copy-start.3 = (f32[128,8]{0,1:T(8,128)S(1)}, f32[128,8]{0,1:T(8,128)}, u32[]{:S(2)}) copy-start(f32[128,8]{0,1:T(8,128)} %param.12) | copy-start | bytes 12292
  17.5 17.7 %slice-start.1 = ((s8[14155776]{0:T(1024)(128)(4,1)}), s8[4194304]{0:T(1024)(128)(4,1)S(1)}, s32[]{:S(2)}) async-start(s8[14155776]{0:T(1024)(128)(4,1)} %bitcast.6), calls=%async_computation.3 | async-start | bytes 8388608
  17.5 17.7 %slice-start.2 = ((s8[14155776]{0:T(1024)(128)(4,1)}), s8[4194304]{0:T(1024)(128)(4,1)S(1)}, s32[]{:S(2)}) async-start(s8[14155776]{0:T(1024)(128)(4,1)} %bitcast.6), calls=%async_computation.4 | async-start | bytes 8388608
  17.5 17.7 %slice-start.3 = ((s8[14155776]{0:T(1024)(128)(4,1)}), s8[1572864]{0:T(1024)(128)(4,1)S(1)}, s32[]{:S(2)}) async-start(s8[14155776]{0:T(1024)(128)(4,1)} %bitcast.6), calls=%async_computation.5 | async-start | bytes 3145728
  17.5 31.6 %copy-start.4 = (s32[4,2]{0,1:T(2,128)S(1)}, s32[4,2]{0,1:T(2,128)}, u32[]{:S(2)}) copy-start(s32[4,2]{0,1:T(2,128)} %param.14) | copy-start | bytes 100
  17.5 31.6 %copy-start.5 = (f32[4,2]{0,1:T(2,128)S(1)}, f32[4,2]{0,1:T(2,128)}, u32[]{:S(2)}) copy-start(f32[4,2]{0,1:T(2,128)} %param.15) | copy-start | bytes 100
  28.1 1.6 %collective-permute-start.1 = (bf16[64,2304]{1,0:T(8,128)(2,1)S(1)}, bf16[64,2304]{1,0:T(8,128)(2,1)S(1)}, u32[]{:S(2)}, u32[]{:S(2)}) collective-permute-start(bf16[64,2304]{1,0:T(8,128)(2,1)S(1)} %gate_up_sums.1.own_ref), channel_id=1, source_target_pairs={{0,1},{1,0},{2,3},{3,2},{4,5},{5,4},{6,7},{7,6},{8,9},{9,8},{10,11... | collective-permute-start | bytes 884744 | tf_op jit(solution)/shard_map/ppermute | solution.py:374
  29.9 6.7 %collective-permute-start.2 = (bf16[32,2304]{1,0:T(8,128)(2,1)S(1)}, bf16[32,2304]{1,0:T(8,128)(2,1)S(1)}, u32[]{:S(2)}, u32[]{:S(2)}) collective-permute-start(bf16[32,2304]{1,0:T(8,128)(2,1)S(1)} %hidden_units.1.hidden_ref), channel_id=1, source_target_pairs={{0,8},{8,0},{1,9},{9,1},{2,10},{10,2},{3,11},{11,3},{4,12},{12,4},... | collective-permute-start | bytes 442376 | tf_op jit(solution)/shard_map/ppermute | solution.py:375
  31.8 10.1 %collective-permute-start = (bf16[1024,128]{1,0:T(8,128)(2,1)S(1)}, bf16[1024,128]{1,0:T(8,128)(2,1)S(1)}, u32[]{:S(2)}, u32[]{:S(2)}) collective-permute-start(bf16[1024,128]{1,0:T(8,128)(2,1)S(1)} %get-tuple-element.9), channel_id=1, source_target_pairs={{0,8},{1,9},{2,10},{3,11},{4,12},{5,13},{6,14},{7,15},{16,24},{17,... | collective-permute-start | bytes 786440 | tf_op jit(solution)/shard_map/ppermute | solution.py:371
  38.6 10.6 %all-to-all-start.1 = ((bf16[8,4,1536]{2,1,0:T(4,128)(2,1)}), bf16[8,4,1536]{2,1,0:T(4,128)(2,1)S(1)}, u32[]{:S(2)}, u32[]{:S(2)}) async-start(bf16[8,4,1536]{2,1,0:T(4,128)(2,1)} %down_other.1), calls=%async_computation.1 | async-start | bytes 196608 | tf_op jit(solution)/shard_map/all_to_all | solution.py:378

commit v3 on v2

--- a/solution.py
+++ b/solution.py
@@ -133,8 +133,17 @@
     return slice(h * width, (h + 1) * width)
 
 
-def attend_kernel(heads, q_hbm, k_hbm, v_hbm, decay_hbm, intra_ref, local_ref, cum_ref, q_ref, k_ref, v_ref, decay_ref, sems):
-    pairs = ((decay_hbm, decay_ref), (q_hbm, q_ref), (k_hbm, k_ref), (v_hbm, v_ref))
+def attend_kernel(
+    heads, q_hbm, k_hbm, v_hbm, decay_hbm, weights_hbm, intra_ref, local_ref, cum_ref, held_ref,
+    q_ref, k_ref, v_ref, decay_ref, sems,
+):
+    pairs = (
+        (decay_hbm, decay_ref),
+        (q_hbm, q_ref),
+        (k_hbm, k_ref),
+        (v_hbm, v_ref),
+        (weights_hbm.at[pl.ds(0, held_ref.shape[0])], held_ref),
+    )
     fetches = [pltpu.make_async_copy(a, b, sems.at[i]) for i, (a, b) in enumerate(pairs)]
     for fetch in fetches:
         fetch.start()
@@ -149,7 +158,7 @@
     )
     cum = jnp.transpose(cum_t)
     cum_ref[...] = cum
-    for fetch in fetches[1:]:
+    for fetch in fetches[1:4]:
         fetch.wait()
     for h in range(heads):
         at = head_columns(h, width)
@@ -164,26 +173,29 @@
         scaled = (k.astype(F32) * rest).astype(BF16)
         local = lax.dot_general(scaled, v, (((0,), (0,)), ((), ())), preferred_element_type=F32)
         local_ref[h * width : (h + 1) * width, :] = local.astype(BF16)
-
-
-def attend(queries, keys, values, log_decay):
+    fetches[4].wait()
+
+
+def attend(queries, keys, values, log_decay, weights, depth):
     rows, heads = log_decay.shape
     width = queries.shape[1] // heads
+    operands = (queries, keys, values, jnp.transpose(log_decay), weights)
     return pl.pallas_call(
         functools.partial(attend_kernel, heads),
-        in_specs=[THERE] * 4,
-        out_specs=[WHOLE] * 3,
+        in_specs=[THERE] * 5,
+        out_specs=[WHOLE] * 4,
         out_shape=[
             jax.ShapeDtypeStruct(queries.shape, F32),
             jax.ShapeDtypeStruct((heads * width, width), BF16),
             jax.ShapeDtypeStruct((rows, heads), F32),
+            pltpu.VMEM((depth,) + weights.shape[1:], BF16),
         ],
         scratch_shapes=[pltpu.VMEM(queries.shape, BF16)] * 3
-        + [pltpu.VMEM((heads, rows), F32), pltpu.SemaphoreType.DMA((4,))],
+        + [pltpu.VMEM((heads, rows), F32), pltpu.SemaphoreType.DMA((5,))],
         compiler_params=pltpu.CompilerParams(vmem_limit_bytes=8 * MIB),
-        cost_estimate=cost(6 * rows * rows * heads * width, 6 * queries.size, heads * rows * rows),
+        cost_estimate=cost(10**10, 6 * queries.size, heads * rows * rows),
         name="attend",
-    )(queries, keys, values, jnp.transpose(log_decay))
+    )(*(pltpu.with_memory_space_constraint(x, pltpu.HBM) for x in operands))
 
 
 def finish_kernel(heads, q_ref, intra_ref, cum_ref, state_ref, out_ref):
@@ -212,57 +224,102 @@
     )(queries, intra, cum, state)
 
 
-def gate_up_kernel(step, x_ref, weights_hbm, sums_ref, weights_ref, spread, sems):
-    depth, _, units = weights_ref.shape
-    starts = range(0, depth, step)
-    fetches = [
-        pltpu.make_async_copy(
-            weights_hbm.at[pl.ds(start, step)], weights_ref.at[pl.ds(start, step)], sems.at[i]
-        )
-        for i, start in enumerate(starts)
-    ]
-    for fetch in fetches:
-        fetch.start()
-    rows = x_ref.shape[0] * x_ref.shape[1]
+def join_kernel(first_ref, second_ref, out_ref):
+    count = first_ref.shape[0]
+    out_ref[:count] = first_ref[...]
+    out_ref[count:] = second_ref[...]
+
+
+def join(first, second):
+    return pl.pallas_call(
+        join_kernel,
+        in_specs=[WHOLE] * 2,
+        out_specs=WHOLE,
+        out_shape=jax.ShapeDtypeStruct((2 * first.shape[0],) + first.shape[1:], first.dtype),
+        compiler_params=pltpu.CompilerParams(vmem_limit_bytes=4 * MIB),
+        cost_estimate=cost(3 * 10**9, 8 * first.size),
+        name="join",
+    )(first, second)
+
+
+def hold_kernel(first, after_ref, weights_hbm, held_ref, sem):
+    fetch = pltpu.make_async_copy(
+        weights_hbm.at[pl.ds(first, held_ref.shape[0])], held_ref, sem
+    )
+    fetch.start()
+    fetch.wait()
+
+
+def hold(after, weights, first, depth):
+    return pl.pallas_call(
+        functools.partial(hold_kernel, first),
+        in_specs=[THERE, THERE],
+        out_specs=WHOLE,
+        out_shape=pltpu.VMEM((depth,) + weights.shape[1:], BF16),
+        scratch_shapes=[pltpu.SemaphoreType.DMA],
+        compiler_params=pltpu.CompilerParams(vmem_limit_bytes=4 * MIB),
+        cost_estimate=cost(0, 2 * depth * weights.shape[1] * weights.shape[2]),
+        name="hold",
+    )(after, pltpu.with_memory_space_constraint(weights, pltpu.HBM))
+
+
+def gate_up_kernel(
+    near_ref, far_ref, a_ref, b_ref, c_ref, weights_hbm, sums_ref, spread, last_ref, sem
+):
+    held = (a_ref, b_ref, c_ref, last_ref)
+    first = sum(part.shape[0] for part in held[:-1])
+    fetch = pltpu.make_async_copy(
+        weights_hbm.at[pl.ds(first, last_ref.shape[0])], last_ref, sem
+    )
+    fetch.start()
+    depth, _, units = weights_hbm.shape
+    rows = near_ref.shape[0] * near_ref.shape[1]
     lanes = 128
     source = lax.broadcasted_iota(jnp.int32, (lanes, 2 * lanes), 0)
     goal = lax.broadcasted_iota(jnp.int32, (lanes, 2 * lanes), 1)
     even = (goal == 2 * source).astype(BF16)
     odd = (goal == 2 * source + 1).astype(BF16)
-    x = x_ref[...].reshape(rows, depth)
+    x = jnp.concatenate([near_ref[...].reshape(rows, depth), far_ref[...].reshape(rows, depth)])
+    rows = 2 * rows
     for b in range(depth // lanes):
         part = x[:, b * lanes : (b + 1) * lanes]
         to = slice(2 * b * lanes, 2 * (b + 1) * lanes)
         spread[:rows, to] = jnp.dot(part, even, preferred_element_type=F32).astype(BF16)
         spread[rows:, to] = jnp.dot(part, odd, preferred_element_type=F32).astype(BF16)
     total = jnp.zeros((2 * rows, units), F32)
-    for start, fetch in zip(starts, fetches):
-        fetch.wait()
-        weights = weights_ref[start : start + step].reshape(2 * step, units)
+    start = 0
+    for part in held:
+        if part is last_ref:
+            fetch.wait()
+        end = start + 2 * part.shape[0]
         total += jnp.dot(
-            spread[:, 2 * start : 2 * (start + step)], weights, preferred_element_type=F32
-        )
+            spread[:, start:end],
+            part[...].reshape(end - start, units),
+            preferred_element_type=F32,
+        )
+        start = end
     sums_ref[...] = total.astype(BF16)
 
 
-def gate_up_sums(x, weights):
-    rows = x.shape[0] * x.shape[1]
+def gate_up_sums(near, far, held, weights):
+    rows = 2 * near.shape[0] * near.shape[1]
     depth, _, units = weights.shape
-    step = 384
-    return pl.pallas_call(
-        functools.partial(gate_up_kernel, step),
-        in_specs=[WHOLE, THERE],
+    rest = depth - sum(part.shape[0] for part in held)
+    held = [pltpu.with_memory_space_constraint(part, pltpu.VMEM) for part in held]
+    return pl.pallas_call(
+        gate_up_kernel,
+        in_specs=[WHOLE] * 5 + [THERE],
         out_specs=WHOLE,
         out_shape=jax.ShapeDtypeStruct((2 * rows, units), BF16),
         scratch_shapes=[
-            pltpu.VMEM(weights.shape, BF16),
             pltpu.VMEM((2 * rows, 2 * depth), BF16),
-            pltpu.SemaphoreType.DMA((depth // step,)),
+            pltpu.VMEM((rest,) + weights.shape[1:], BF16),
+            pltpu.SemaphoreType.DMA,
         ],
-        compiler_params=pltpu.CompilerParams(vmem_limit_bytes=36 * MIB),
+        compiler_params=pltpu.CompilerParams(vmem_limit_bytes=16 * MIB),
         cost_estimate=cost(4 * rows * weights.size, 2 * weights.size),
         name="gate_up_sums",
-    )(x, weights)
+    )(near, far, *held, pltpu.with_memory_space_constraint(weights, pltpu.HBM))
 
 
 def hidden_kernel(own_ref, other_ref, out_ref):
@@ -296,10 +353,15 @@
 def down_other_kernel(hidden_ref, down_ref, own_ref, out_ref):
     units = hidden_ref.shape[1]
     first = pl.multiple_of((1 - lax.axis_index("ctx")) * units, units)
-    total = own_ref[...] + jnp.dot(
-        hidden_ref[...], down_ref[pl.ds(first, units), :], preferred_element_type=F32
-    )
-    out_ref[...] = total.astype(BF16).reshape(out_ref.shape)
+    experts = lax.axis_size("exp")
+    rows = out_ref.shape[1]
+    other = jnp.dot(hidden_ref[...], down_ref[pl.ds(first, units), :], preferred_element_type=F32)
+    pairs = [other[2 * rows * i : 2 * rows * (i + 1)] for i in (1, 0, 3, 2)]
+    total = (own_ref[...] + jnp.concatenate(pairs)).astype(BF16)
+    for block in range(out_ref.shape[0]):
+        ctx = lax.axis_index("ctx") ^ ((block >> 1) & 1)
+        exp = lax.axis_index("exp") ^ (2 * (block & 1) + (block >> 2))
+        out_ref[ctx * experts + exp] = total[block * rows : (block + 1) * rows]
 
 
 def down_sums(hidden, down, own=None, peers=None):
@@ -354,23 +416,25 @@
 
 def on_device(queries, keys, values, log_decay, moe_input, route_ids, route_weight, gate_up, down):
     ctx_count, expert_list = (lax.axis_size("ctx"), lax.axis_size("exp"))
-    if ctx_count != 2 or lax.axis_size("tp") != 2 or gate_up.shape[3] % 128:
+    if (ctx_count, expert_list, lax.axis_size("tp")) != (2, 4, 2) or gate_up.shape[3] % 128:
         return on_device_any(
             queries, keys, values, log_decay, moe_input, route_ids, route_weight, gate_up, down
         )
     peers = ctx_count * expert_list
     swap = [(0, 1), (1, 0)]
-    tokens = lax.all_to_all(
-        jnp.broadcast_to(moe_input[None], (peers,) + moe_input.shape),
-        ("ctx", "exp"),
-        split_axis=0,
-        concat_axis=0,
-        tiled=True,
-    )
-    intra, local, cum = attend(queries, keys, values, log_decay)
+    own_tokens = moe_input[None]
+    tokens = join(own_tokens, lax.ppermute(own_tokens, "exp", [(e, e ^ 2) for e in range(4)]))
+    weights, w_down = (gate_up.reshape(gate_up.shape[1:]), down.reshape(down.shape[1:]))
+    quarter = weights.shape[0] // 4
+    intra, local, cum, held = attend(queries, keys, values, log_decay, weights, quarter)
+    tokens, local = lax.optimization_barrier((tokens, local))
+    held_next = hold(tokens, weights, quarter, quarter)
+    arrived, held_next = lax.optimization_barrier((lax.ppermute(tokens, "ctx", swap), held_next))
+    tokens = join(tokens, arrived)
+    held_last = hold(tokens, weights, 2 * quarter, quarter)
+    far_tokens = lax.ppermute(tokens, "exp", [(e, e ^ 1) for e in range(4)])
     state = lax.ppermute(local, "ctx", [(0, 1)])
-    sums = gate_up_sums(tokens, gate_up.reshape(gate_up.shape[1:]))
-    sums, w_down = lax.optimization_barrier((sums, down.reshape(down.shape[1:])))
+    sums = gate_up_sums(tokens, far_tokens, (held, held_next, held_last), weights)
     hidden = hidden_units(sums, lax.ppermute(sums, "tp", swap))
     hidden_other = lax.ppermute(hidden, "ctx", swap)
     own = down_sums(hidden, w_down)

time: 50.2 us -> 46.8 us (0.932)
  blocking collectives: 15.9 us -> 0 us
  starting transfers between devices: 7.44 us -> 16.4 us
  Pallas kernels: 17.5 us -> 21.3 us
  local copies, waits for them, and re-layouts: 0.99 us -> 0.04 us
  waiting for transfers between devices: 7.3 us -> 7.94 us
    all_to_all x1 -> x0, blocking collectives: 15.9 us -> none  [on_device(): lax.all_to_all(jnp.broadcast_to(moe_input[None], (peers,) + moe_input.sha...]
    ppermute x0 -> x3, starting transfers between devices: none -> 7.3 us  [the longest x1 4.1 us: on_device(): lax.ppermute(own_tokens, 'exp', [(e, e ^ 2) for e in range(4)])]
    pallas_call x1, Pallas kernels: 1.26 us -> 3.34 us  [attend(): pl.pallas_call(functools.partial(attend_kernel, heads), in_specs=[THERE]...]
    pallas_call x1 -> x5, Pallas kernels: 10.6 us -> 12.3 us  [the longest x1 6.26 us: gate_up_sums(): pl.pallas_call(gate_up_kernel, in_specs=[WHOLE] * 5 + [THERE], out_specs=...]
    all_to_all x1, starting transfers between devices: 3.36 us -> 4.98 us  [on_device(): lax.all_to_all(expert_out, ('ctx', 'exp'), split_axis=0, concat_axis=0, t...]
    broadcast_in_dim x1 -> x0, local copies, waits for them, and re-layouts: 0.94 us -> none  [on_device(): jnp.broadcast_to(moe_input[None], (peers,) + moe_input.shape)]
    ppermute x1, waiting for transfers between devices: 0.01 us -> 0.56 us  [on_device(): hidden_other = lax.ppermute(hidden, 'ctx', swap)]
  transfers between devices with their start and end apart: 4 -> 7, of which waited for: 2 -> 3; matrix products, arithmetic and copies ran while one was open for 0% -> 0% of each run, Pallas kernels for 12% -> 30%
where the time goes in v3:
time: 46.8 us; the launch traced here: 46.5 us
  Pallas kernels  21.3 us (46%)
  starting transfers between devices  16.4 us (35%)
  waiting for transfers between devices  7.94 us (17%)
  between operations  0.83 us (2%)
    pallas_call x1, Pallas kernels, gate_up_sums(): pl.pallas_call(gate_up_kernel, in_specs=[WHOLE] * 5 + [THERE], out_specs=...  6.26 us
    pallas_call x2, Pallas kernels, hold(): pl.pallas_call(functools.partial(hold_kernel, first), in_specs=[THERE, TH...  6.03 us
    all_to_all x1, waiting for transfers between devices, on_device(): lax.all_to_all(expert_out, ('ctx', 'exp'), split_axis=0, concat_axis=0, t...  5.78 us
    all_to_all x1, starting transfers between devices, on_device(): lax.all_to_all(expert_out, ('ctx', 'exp'), split_axis=0, concat_axis=0, t...  4.98 us
    ppermute x1, starting transfers between devices, on_device(): lax.ppermute(own_tokens, 'exp', [(e, e ^ 2) for e in range(4)])  4.1 us
    pallas_call x1, Pallas kernels, attend(): pl.pallas_call(functools.partial(attend_kernel, heads), in_specs=[THERE]...  3.34 us
    pallas_call x2, Pallas kernels, down_sums(): pl.pallas_call(kernel, in_specs=[WHOLE] * len(operands), out_specs=WHOLE,...  3.27 us
    ppermute x1, starting transfers between devices, on_device(): state = lax.ppermute(local, 'ctx', [(0, 1)])  2.88 us
  transfers between devices with their start and end apart: 7, of which 3 were waited for; matrix products, arithmetic and copies ran while one was open for 0% of the time, Pallas kernels for 30%

profile of v3, /device:TPU:0, one launch (start us, length us, event | category | flops | bytes accessed | tf_op | source)
XLA Modules:
  0.0 46.5 jit_solution(644937009950252108)
XLA Ops:
  0.6 4.1 %collective-permute-start = (bf16[1,4,3072]{2,1,0:T(4,128)(2,1)}, bf16[1,4,3072]{2,1,0:T(4,128)(2,1)S(1)}, u32[]{:S(2)}, u32[]{:S(2)}) collective-permute-start(bf16[1,4,3072]{2,1,0:T(4,128)(2,1)} %bitcast.14), channel_id=1, source_target_pairs={{0,4},{2,6},{4,0},{6,2},{1,5},{3,7},{5,1},{7,3},{8,12},{10,14},{12... | collective-permute-start | bytes 73736 | tf_op jit(solution)/shard_map/ppermute | solution.py:426
  4.7 3.3 %attend.1 = (f32[128,1024]{1,0:T(8,128)S(1)}, bf16[1024,128]{1,0:T(8,128)(2,1)S(1)}, f32[128,8]{1,0:T(8,128)S(1)}, bf16[768,2,2304]{2,1,0:T(2,128)(2,1)S(1)}) custom-call(bf16[128,1024]{1,0:T(8,128)(2,1)} %q_ref.1, bf16[128,1024]{1,0:T(8,128)(2,1)} %k_hbm.1, bf16[128,1024]{1,0:T(8,128)(2,1)} %v_hbm.1, f32[8,128]{1,0:T(8,128)} %bitcast.20, ...), custom_call_target="tpu_custom_call" | custom-call | flops 10000000000 | bytes 786432 | tf_op jit(solution)/shard_map/attend/pallas_call | solution.py:183
  8.1 0.0 collective-permute-done.second_ref
  8.1 1.6 %collective-permute-start.2 = (bf16[2,4,3072]{2,1,0:T(4,128)(2,1)S(1)}, bf16[2,4,3072]{2,1,0:T(4,128)(2,1)S(1)}, u32[]{:S(2)}, u32[]{:S(2)}) collective-permute-start(bf16[2,4,3072]{2,1,0:T(4,128)(2,1)S(1)} %join.2.after_ref.first_ref), channel_id=1, source_target_pairs={{0,8},{8,0},{1,9},{9,1},{2,10},{10,2},{3,11},{11,3},{4,12},{12,4},... | collective-permute-start | bytes 147464 | tf_op jit(solution)/shard_map/ppermute | solution.py:432
  9.7 3.0 %hold.2.b_ref = bf16[768,2,2304]{2,1,0:T(2,128)(2,1)S(1)} custom-call(bf16[2,4,3072]{2,1,0:T(4,128)(2,1)S(1)} %join.2.after_ref.first_ref, bf16[3072,2,2304]{2,1,0:T(2,128)(2,1)} %bitcast.17), custom_call_target="tpu_custom_call" | custom-call | bytes 7077888 | tf_op jit(solution)/shard_map/hold/pallas_call | solution.py:254
  12.7 0.0 collective-permute-done.2.second_ref
  12.7 1.6 %collective-permute-start.3 = (bf16[4,4,3072]{2,1,0:T(4,128)(2,1)S(1)}, bf16[4,4,3072]{2,1,0:T(4,128)(2,1)S(1)}, u32[]{:S(2)}, u32[]{:S(2)}) collective-permute-start(bf16[4,4,3072]{2,1,0:T(4,128)(2,1)S(1)} %join.3.after_ref.near_ref), channel_id=1, source_target_pairs={{0,2},{2,0},{4,6},{6,4},{1,3},{3,1},{5,7},{7,5},{8,10},{10,8},{12,... | collective-permute-start | bytes 294920 | tf_op jit(solution)/shard_map/ppermute | solution.py:435
  14.4 3.0 %hold.3.c_ref = bf16[768,2,2304]{2,1,0:T(2,128)(2,1)S(1)} custom-call(bf16[4,4,3072]{2,1,0:T(4,128)(2,1)S(1)} %join.3.after_ref.near_ref, bf16[3072,2,2304]{2,1,0:T(2,128)(2,1)} %bitcast.18), custom_call_target="tpu_custom_call" | custom-call | bytes 7077888 | tf_op jit(solution)/shard_map/hold/pallas_call | solution.py:254
  17.4 0.0 collective-permute-done.3.far_ref
  17.4 0.0 slice-start.1
  17.4 6.3 %gate_up_sums.1.own_ref = bf16[64,2304]{1,0:T(8,128)(2,1)S(1)} custom-call(bf16[4,4,3072]{2,1,0:T(4,128)(2,1)S(1)} %join.3.after_ref.near_ref, bf16[4,4,3072]{2,1,0:T(4,128)(2,1)S(1)} %collective-permute-done.3.far_ref, bf16[768,2,2304]{2,1,0:T(2,128)(2,1)S(1)} %get-tuple-element.16.a_ref, bf16[768,2,2304]{2,1,0:T(2,128)(2,1)S(1)} %hold.2.b_ref, ...), custom_call_target="tpu_custom_call" | custom-call | flops 1811939328 | bytes 28311552 | tf_op jit(solution)/shard_map/gate_up_sums/pallas_call | solution.py:309
  23.7 0.1 collective-permute-start.4
  23.8 1.6 %collective-permute-done.4.other_ref = bf16[64,2304]{1,0:T(8,128)(2,1)S(1)} collective-permute-done((bf16[64,2304]{1,0:T(8,128)(2,1)S(1)}, bf16[64,2304]{1,0:T(8,128)(2,1)S(1)}, u32[]{:S(2)}, u32[]{:S(2)}) %collective-permute-start.4) | collective-permute-done | bytes 294944 | tf_op jit(solution)/shard_map/ppermute | solution.py:438
  25.4 0.1 hidden_units.1.hidden_ref
  25.5 1.1 %collective-permute-start.5 = (bf16[32,2304]{1,0:T(8,128)(2,1)S(1)}, bf16[32,2304]{1,0:T(8,128)(2,1)S(1)}, u32[]{:S(2)}, u32[]{:S(2)}) collective-permute-start(bf16[32,2304]{1,0:T(8,128)(2,1)S(1)} %hidden_units.1.hidden_ref), channel_id=1, source_target_pairs={{0,8},{8,0},{1,9},{9,1},{2,10},{10,2},{3,11},{11,3},{4,12},{12,4},... | collective-permute-start | bytes 442376 | tf_op jit(solution)/shard_map/ppermute | solution.py:439
  26.6 2.9 %collective-permute-start.1 = (bf16[1024,128]{1,0:T(8,128)(2,1)S(1)}, bf16[1024,128]{1,0:T(8,128)(2,1)S(1)}, u32[]{:S(2)}, u32[]{:S(2)}) collective-permute-start(bf16[1024,128]{1,0:T(8,128)(2,1)S(1)} %get-tuple-element.13), channel_id=1, source_target_pairs={{0,8},{1,9},{2,10},{3,11},{4,12},{5,13},{6,14},{7,15},{16,24},{17,... | collective-permute-start | bytes 786440 | tf_op jit(solution)/shard_map/ppermute | solution.py:436
  29.6 1.3 %down_own.1.own_ref = f32[32,1536]{1,0:T(8,128)S(1)} custom-call(bf16[32,2304]{1,0:T(8,128)(2,1)S(1)} %hidden_units.1.hidden_ref, bf16[4608,1536]{1,0:T(8,128)(2,1)S(1)} %bitcast.9), custom_call_target="tpu_custom_call" | custom-call | flops 226492416 | bytes 7077888 | tf_op jit(solution)/shard_map/down_own/pallas_call | solution.py:377
  30.9 0.0 copy-start.2
  30.9 0.6 %collective-permute-done.5.hidden_ref = bf16[32,2304]{1,0:T(8,128)(2,1)S(1)} collective-permute-done((bf16[32,2304]{1,0:T(8,128)(2,1)S(1)}, bf16[32,2304]{1,0:T(8,128)(2,1)S(1)}, u32[]{:S(2)}, u32[]{:S(2)}) %collective-permute-start.5) | collective-permute-done | bytes 147488 | tf_op jit(solution)/shard_map/ppermute | solution.py:439
  31.5 2.0 %down_other.1 = bf16[8,4,1536]{2,1,0:T(4,128)(2,1)} custom-call(bf16[32,2304]{1,0:T(8,128)(2,1)S(1)} %collective-permute-done.5.hidden_ref, bf16[4608,1536]{1,0:T(8,128)(2,1)S(1)} %bitcast.10, f32[32,1536]{1,0:T(8,128)S(1)} %down_own.1.own_ref), custom_call_target="tpu_custom_call" | custom-call | flops 226492416 | bytes 7077888 | tf_op jit(solution)/shard_map/down_other/pallas_call | solution.py:377
  33.4 5.0 %all-to-all-start = ((bf16[8,4,1536]{2,1,0:T(4,128)(2,1)}), bf16[8,4,1536]{2,1,0:T(4,128)(2,1)S(1)}, u32[]{:S(2)}, u32[]{:S(2)}) async-start(bf16[8,4,1536]{2,1,0:T(4,128)(2,1)} %down_other.1), calls=%async_computation | async-start | bytes 196608 | tf_op jit(solution)/shard_map/all_to_all | solution.py:442
  38.4 1.5 %finish.1 = bf16[128,1024]{1,0:T(8,128)(2,1)} custom-call(bf16[128,1024]{1,0:T(8,128)(2,1)S(1)} %copy-done, f32[128,1024]{1,0:T(8,128)S(1)} %get-tuple-element.10.intra_ref, f32[128,8]{1,0:T(8,128)S(1)} %get-tuple-element.11.cum_ref, bf16[1024,128]{1,0:T(8,128)(2,1)S(1)} %collective-permute-done.1.state_ref), custom_call_target="tpu_custom_call" | custom-call | flops 33554432 | bytes 1310720 | tf_op jit(solution)/shard_map/finish/pallas_call | solution.py:216
  39.9 5.8 %all-to-all-done = bf16[8,4,1536]{2,1,0:T(4,128)(2,1)S(1)} async-done(((bf16[8,4,1536]{2,1,0:T(4,128)(2,1)}), bf16[8,4,1536]{2,1,0:T(4,128)(2,1)S(1)}, u32[]{:S(2)}, u32[]{:S(2)}) %all-to-all-start) | async-done | bytes 98336 | tf_op jit(solution)/shard_map/all_to_all | solution.py:442
  45.7 0.8 %merge.1 = bf16[4,3072]{1,0:T(4,128)(2,1)} custom-call(s32[2,4]{1,0:T(2,128)S(1)} %bitcast.12, f32[2,4]{1,0:T(2,128)S(1)} %bitcast.13, bf16[2,4,4,1536]{3,2,1,0:T(4,128)(2,1)S(1)} %bitcast.11), custom_call_target="tpu_custom_call" | custom-call | flops 196608 | bytes 98304 | tf_op jit(solution)/shard_map/merge/pallas_call | solution.py:405
  (18 shorter events, 0.0 us)
Async XLA Ops:
  0.6 7.5 %collective-permute-start = (bf16[1,4,3072]{2,1,0:T(4,128)(2,1)}, bf16[1,4,3072]{2,1,0:T(4,128)(2,1)S(1)}, u32[]{:S(2)}, u32[]{:S(2)}) collective-permute-start(bf16[1,4,3072]{2,1,0:T(4,128)(2,1)} %bitcast.14), channel_id=1, source_target_pairs={{0,4},{2,6},{4,0},{6,2},{1,5},{3,7},{5,1},{7,3},{8,12},{10,14},{12... | collective-permute-start | bytes 73736 | tf_op jit(solution)/shard_map/ppermute | solution.py:426
  4.7 3.4 %copy-start.3 = (bf16[4,3072]{1,0:T(4,128)(2,1)S(1)}, bf16[4,3072]{1,0:T(4,128)(2,1)}, u32[]{:S(2)}) copy-start(bf16[4,3072]{1,0:T(4,128)(2,1)} %param.13) | copy-start | bytes 73732
  8.1 4.6 %collective-permute-start.2 = (bf16[2,4,3072]{2,1,0:T(4,128)(2,1)S(1)}, bf16[2,4,3072]{2,1,0:T(4,128)(2,1)S(1)}, u32[]{:S(2)}, u32[]{:S(2)}) collective-permute-start(bf16[2,4,3072]{2,1,0:T(4,128)(2,1)S(1)} %join.2.after_ref.first_ref), channel_id=1, source_target_pairs={{0,8},{8,0},{1,9},{9,1},{2,10},{10,2},{3,11},{11,3},{4,12},{12,4},... | collective-permute-start | bytes 147464 | tf_op jit(solution)/shard_map/ppermute | solution.py:432
  12.7 4.7 %collective-permute-start.3 = (bf16[4,4,3072]{2,1,0:T(4,128)(2,1)S(1)}, bf16[4,4,3072]{2,1,0:T(4,128)(2,1)S(1)}, u32[]{:S(2)}, u32[]{:S(2)}) collective-permute-start(bf16[4,4,3072]{2,1,0:T(4,128)(2,1)S(1)} %join.3.after_ref.near_ref), channel_id=1, source_target_pairs={{0,2},{2,0},{4,6},{6,4},{1,3},{3,1},{5,7},{7,5},{8,10},{10,8},{12,... | collective-permute-start | bytes 294920 | tf_op jit(solution)/shard_map/ppermute | solution.py:435
  17.4 12.1 %slice-start = ((s8[14155776]{0:T(1024)(128)(4,1)}), s8[4194304]{0:T(1024)(128)(4,1)S(1)}, s32[]{:S(2)}) async-start(s8[14155776]{0:T(1024)(128)(4,1)} %bitcast.7), calls=%async_computation.1 | async-start | bytes 8388608
  17.4 12.1 %slice-start.1 = ((s8[14155776]{0:T(1024)(128)(4,1)}), s8[4194304]{0:T(1024)(128)(4,1)S(1)}, s32[]{:S(2)}) async-start(s8[14155776]{0:T(1024)(128)(4,1)} %bitcast.7), calls=%async_computation.2 | async-start | bytes 8388608
  17.4 12.1 %slice-start.2 = ((s8[14155776]{0:T(1024)(128)(4,1)}), s8[4194304]{0:T(1024)(128)(4,1)S(1)}, s32[]{:S(2)}) async-start(s8[14155776]{0:T(1024)(128)(4,1)} %bitcast.7), calls=%async_computation.3 | async-start | bytes 8388608
  17.4 12.1 %slice-start.3 = ((s8[14155776]{0:T(1024)(128)(4,1)}), s8[1572864]{0:T(1024)(128)(4,1)S(1)}, s32[]{:S(2)}) async-start(s8[14155776]{0:T(1024)(128)(4,1)} %bitcast.7), calls=%async_computation.4 | async-start | bytes 3145728
  23.7 1.6 %collective-permute-start.4 = (bf16[64,2304]{1,0:T(8,128)(2,1)S(1)}, bf16[64,2304]{1,0:T(8,128)(2,1)S(1)}, u32[]{:S(2)}, u32[]{:S(2)}) collective-permute-start(bf16[64,2304]{1,0:T(8,128)(2,1)S(1)} %gate_up_sums.1.own_ref), channel_id=1, source_target_pairs={{0,1},{1,0},{2,3},{3,2},{4,5},{5,4},{6,7},{7,6},{8,9},{9,8},{10,11... | collective-permute-start | bytes 884744 | tf_op jit(solution)/shard_map/ppermute | solution.py:438
  25.5 6.0 %collective-permute-start.5 = (bf16[32,2304]{1,0:T(8,128)(2,1)S(1)}, bf16[32,2304]{1,0:T(8,128)(2,1)S(1)}, u32[]{:S(2)}, u32[]{:S(2)}) collective-permute-start(bf16[32,2304]{1,0:T(8,128)(2,1)S(1)} %hidden_units.1.hidden_ref), channel_id=1, source_target_pairs={{0,8},{8,0},{1,9},{9,1},{2,10},{10,2},{3,11},{11,3},{4,12},{12,4},... | collective-permute-start | bytes 442376 | tf_op jit(solution)/shard_map/ppermute | solution.py:439
  26.6 11.8 %collective-permute-start.1 = (bf16[1024,128]{1,0:T(8,128)(2,1)S(1)}, bf16[1024,128]{1,0:T(8,128)(2,1)S(1)}, u32[]{:S(2)}, u32[]{:S(2)}) collective-permute-start(bf16[1024,128]{1,0:T(8,128)(2,1)S(1)} %get-tuple-element.13), channel_id=1, source_target_pairs={{0,8},{1,9},{2,10},{3,11},{4,12},{5,13},{6,14},{7,15},{16,24},{17,... | collective-permute-start | bytes 786440 | tf_op jit(solution)/shard_map/ppermute | solution.py:436
  30.9 7.5 %copy-start = (bf16[128,1024]{1,0:T(8,128)(2,1)S(1)}, bf16[128,1024]{1,0:T(8,128)(2,1)}, u32[]{:S(2)}) copy-start(bf16[128,1024]{1,0:T(8,128)(2,1)} %q_ref.1) | copy-start | bytes 786436
  30.9 14.8 %copy-start.1 = (s32[4,2]{0,1:T(2,128)S(1)}, s32[4,2]{0,1:T(2,128)}, u32[]{:S(2)}) copy-start(s32[4,2]{0,1:T(2,128)} %param.14) | copy-start | bytes 100
  30.9 14.8 %copy-start.2 = (f32[4,2]{0,1:T(2,128)S(1)}, f32[4,2]{0,1:T(2,128)}, u32[]{:S(2)}) copy-start(f32[4,2]{0,1:T(2,128)} %param.15) | copy-start | bytes 100
  33.4 12.2 %all-to-all-start = ((bf16[8,4,1536]{2,1,0:T(4,128)(2,1)}), bf16[8,4,1536]{2,1,0:T(4,128)(2,1)S(1)}, u32[]{:S(2)}, u32[]{:S(2)}) async-start(bf16[8,4,1536]{2,1,0:T(4,128)(2,1)} %down_other.1), calls=%async_computation | async-start | bytes 196608 | tf_op jit(solution)/shard_map/all_to_all | solution.py:442

commit v4 on v3

--- a/solution.py
+++ b/solution.py
@@ -200,9 +200,10 @@
 
 def finish_kernel(heads, q_ref, intra_ref, cum_ref, state_ref, out_ref):
     width = q_ref.shape[1] // heads
+    entered = lax.axis_index("ctx") > 0
     for h in range(heads):
         at = head_columns(h, width)
-        grown = jnp.exp(cum_ref[:, h : h + 1])
+        grown = jnp.where(entered, jnp.exp(cum_ref[:, h : h + 1]), 0.0)
         state = state_ref[h * width : (h + 1) * width, :]
         mixed = intra_ref[:, at] + grown * jnp.dot(
             q_ref[:, at], state, preferred_element_type=F32
@@ -275,17 +276,19 @@
     depth, _, units = weights_hbm.shape
     rows = near_ref.shape[0] * near_ref.shape[1]
     lanes = 128
-    source = lax.broadcasted_iota(jnp.int32, (lanes, 2 * lanes), 0)
-    goal = lax.broadcasted_iota(jnp.int32, (lanes, 2 * lanes), 1)
-    even = (goal == 2 * source).astype(BF16)
-    odd = (goal == 2 * source + 1).astype(BF16)
+    source = lax.broadcasted_iota(jnp.int32, (lanes, 4 * lanes), 0)
+    goal = lax.broadcasted_iota(jnp.int32, (lanes, 4 * lanes), 1)
+    places = jnp.where(goal < 2 * lanes, 2 * source, 2 * source + 2 * lanes + 1)
     x = jnp.concatenate([near_ref[...].reshape(rows, depth), far_ref[...].reshape(rows, depth)])
     rows = 2 * rows
-    for b in range(depth // lanes):
-        part = x[:, b * lanes : (b + 1) * lanes]
+    blocks = depth // lanes
+    stacked = jnp.concatenate([x[:, b * lanes : (b + 1) * lanes] for b in range(blocks)])
+    wide = jnp.dot(stacked, (goal == places).astype(BF16), preferred_element_type=F32)
+    wide = wide.astype(BF16)
+    for b in range(blocks):
         to = slice(2 * b * lanes, 2 * (b + 1) * lanes)
-        spread[:rows, to] = jnp.dot(part, even, preferred_element_type=F32).astype(BF16)
-        spread[rows:, to] = jnp.dot(part, odd, preferred_element_type=F32).astype(BF16)
+        spread[:rows, to] = wide[b * rows : (b + 1) * rows, : 2 * lanes]
+        spread[rows:, to] = wide[b * rows : (b + 1) * rows, 2 * lanes :]
     total = jnp.zeros((2 * rows, units), F32)
     start = 0
     for part in held:
@@ -322,11 +325,14 @@
     )(near, far, *held, pltpu.with_memory_space_constraint(weights, pltpu.HBM))
 
 
-def hidden_kernel(own_ref, other_ref, out_ref):
+def hidden_kernel(own_ref, other_ref, out_ref, part_ref):
     rows = out_ref.shape[0]
     summed = own_ref[...].astype(F32) + other_ref[...].astype(F32)
     gate, up = (summed[:rows], summed[rows:])
-    out_ref[...] = (gate / (1.0 + jnp.exp(-gate)) * up).astype(BF16)
+    hidden = (gate / (1.0 + jnp.exp(-gate)) * up).astype(BF16)
+    out_ref[...] = hidden
+    half = part_ref.shape[1]
+    part_ref[...] = jnp.where(lax.axis_index("tp") == 0, hidden[:, :half], hidden[:, half:])
 
 
 def hidden_units(own, other):
@@ -334,8 +340,11 @@
     return pl.pallas_call(
         hidden_kernel,
         in_specs=[WHOLE] * 2,
-        out_specs=WHOLE,
-        out_shape=jax.ShapeDtypeStruct((rows // 2, units), BF16),
+        out_specs=[WHOLE] * 2,
+        out_shape=[
+            jax.ShapeDtypeStruct((rows // 2, units), BF16),
+            jax.ShapeDtypeStruct((rows // 2, units // 2), BF16),
+        ],
         compiler_params=pltpu.CompilerParams(vmem_limit_bytes=8 * MIB),
         cost_estimate=cost(4 * own.size, 5 * own.size, own.size // 2),
         name="hidden_units",
@@ -350,12 +359,23 @@
     )
 
 
-def down_other_kernel(hidden_ref, down_ref, own_ref, out_ref):
-    units = hidden_ref.shape[1]
-    first = pl.multiple_of((1 - lax.axis_index("ctx")) * units, units)
+def other_product(part, down_ref, core):
+    units = part.shape[1]
+    first = pl.multiple_of((2 * (1 - lax.axis_index("ctx")) + core) * units, units)
+    return jnp.dot(part, down_ref[pl.ds(first, units), :], preferred_element_type=F32)
+
+
+def down_near_kernel(part_ref, down_ref, own_ref, out_ref):
+    other = other_product(part_ref[...], down_ref, lax.axis_index("tp"))
+    count = other.shape[0] // 4
+    pairs = [other[count * i : count * (i + 1)] for i in (1, 0, 3, 2)]
+    out_ref[...] = own_ref[...] + jnp.concatenate(pairs)
+
+
+def down_far_kernel(part_ref, down_ref, own_ref, out_ref):
     experts = lax.axis_size("exp")
     rows = out_ref.shape[1]
-    other = jnp.dot(hidden_ref[...], down_ref[pl.ds(first, units), :], preferred_element_type=F32)
+    other = other_product(part_ref[...], down_ref, 1 - lax.axis_index("tp"))
     pairs = [other[2 * rows * i : 2 * rows * (i + 1)] for i in (1, 0, 3, 2)]
     total = (own_ref[...] + jnp.concatenate(pairs)).astype(BF16)
     for block in range(out_ref.shape[0]):
@@ -364,25 +384,19 @@
         out_ref[ctx * experts + exp] = total[block * rows : (block + 1) * rows]
 
 
-def down_sums(hidden, down, own=None, peers=None):
+def down_sums(kernel, shape, dtype, hidden, down, *sums):
     rows, units = hidden.shape
     columns = down.shape[1]
     down = pltpu.with_memory_space_constraint(down, pltpu.VMEM)
-    if own is None:
-        kernel, operands = (down_own_kernel, (hidden, down))
-        out_shape = jax.ShapeDtypeStruct((rows, columns), F32)
-    else:
-        kernel, operands = (down_other_kernel, (hidden, down, own))
-        out_shape = jax.ShapeDtypeStruct((peers, rows // peers, columns), BF16)
     return pl.pallas_call(
         kernel,
-        in_specs=[WHOLE] * len(operands),
-        out_specs=WHOLE,
-        out_shape=out_shape,
+        in_specs=[WHOLE] * (2 + len(sums)),
+        out_specs=WHOLE,
+        out_shape=jax.ShapeDtypeStruct(shape, dtype),
         compiler_params=pltpu.CompilerParams(vmem_limit_bytes=8 * MIB),
         cost_estimate=cost(2 * rows * units * columns, 2 * units * columns),
-        name="down_own" if own is None else "down_other",
-    )(*operands)
+        name=kernel.__name__[:-7],
+    )(hidden, down, *sums)
 
 
 def merge_kernel(ids_ref, weight_ref, back_ref, out_ref, table):
@@ -433,12 +447,19 @@
     tokens = join(tokens, arrived)
     held_last = hold(tokens, weights, 2 * quarter, quarter)
     far_tokens = lax.ppermute(tokens, "exp", [(e, e ^ 1) for e in range(4)])
-    state = lax.ppermute(local, "ctx", [(0, 1)])
     sums = gate_up_sums(tokens, far_tokens, (held, held_next, held_last), weights)
-    hidden = hidden_units(sums, lax.ppermute(sums, "tp", swap))
-    hidden_other = lax.ppermute(hidden, "ctx", swap)
-    own = down_sums(hidden, w_down)
-    expert_out = down_sums(hidden_other, w_down, own, peers)
+    hidden, part = hidden_units(sums, lax.ppermute(sums, "tp", swap))
+    part = lax.ppermute(part, "ctx", swap)
+    sums_shape = (hidden.shape[0], w_down.shape[1])
+    total = down_sums(down_own_kernel, sums_shape, F32, hidden, w_down)
+    total, local = lax.optimization_barrier((total, local))
+    state = lax.ppermute(local, "ctx", swap)
+    part_far = lax.ppermute(part, "tp", swap)
+    total = down_sums(down_near_kernel, sums_shape, F32, part, w_down, total)
+    rows = moe_input.shape[0]
+    expert_out = down_sums(
+        down_far_kernel, (peers, rows, sums_shape[1]), BF16, part_far, w_down, total
+    )
     back = lax.all_to_all(expert_out, ("ctx", "exp"), split_axis=0, concat_axis=0, tiled=True)
     attended = finish(queries, intra, cum, state)
     back = back.reshape((ctx_count, expert_list) + back.shape[1:])

time: 46.8 us -> 44.8 us (0.957)
  starting transfers between devices: 16.4 us -> 13.9 us
  waiting for transfers between devices: 7.94 us -> 8.87 us
  Pallas kernels: 21.3 us -> 20.8 us
    ppermute x3 -> x4, starting transfers between devices: 4.07 us -> 2.18 us  [the longest x1 1.12 us: on_device(): part = lax.ppermute(part, 'ctx', swap)]
    ppermute x3 -> x4, waiting for transfers between devices: 2.13 us -> 3.07 us  [the longest x1 1.57 us: on_device(): hidden, part = hidden_units(sums, lax.ppermute(sums, 'tp', swap))]
    pallas_call x1, Pallas kernels: 6.26 us -> 5.68 us  [gate_up_sums(): pl.pallas_call(gate_up_kernel, in_specs=[WHOLE] * 5 + [THERE], out_specs=...]
    all_to_all x1, starting transfers between devices: 4.98 us -> 4.45 us  [on_device(): lax.all_to_all(expert_out, ('ctx', 'exp'), split_axis=0, concat_axis=0, t...]
    pallas_call x3 -> x4, Pallas kernels: 3.41 us -> 3.53 us  [the longest x3 3.38 us: down_sums(): pl.pallas_call(kernel, in_specs=[WHOLE] * (2 + len(sums)), out_specs=WHOL...]
  transfers between devices with their start and end apart: 7 -> 8, of which waited for: 3 -> 4; matrix products, arithmetic and copies ran while one was open for 0% -> 0% of each run, Pallas kernels for 30% -> 32%
where the time goes in v4:
time: 44.8 us; the launch traced here: 44.5 us
  Pallas kernels  20.8 us (46%)
  starting transfers between devices  13.9 us (31%)
  waiting for transfers between devices  8.87 us (20%)
  between operations  0.81 us (2%)
    pallas_call x2, Pallas kernels, hold(): pl.pallas_call(functools.partial(hold_kernel, first), in_specs=[THERE, TH...  6.03 us
    all_to_all x1, waiting for transfers between devices, on_device(): lax.all_to_all(expert_out, ('ctx', 'exp'), split_axis=0, concat_axis=0, t...  5.78 us
    pallas_call x1, Pallas kernels, gate_up_sums(): pl.pallas_call(gate_up_kernel, in_specs=[WHOLE] * 5 + [THERE], out_specs=...  5.68 us
    all_to_all x1, starting transfers between devices, on_device(): lax.all_to_all(expert_out, ('ctx', 'exp'), split_axis=0, concat_axis=0, t...  4.45 us
    ppermute x1, starting transfers between devices, on_device(): lax.ppermute(own_tokens, 'exp', [(e, e ^ 2) for e in range(4)])  4.1 us
    pallas_call x3, Pallas kernels, down_sums(): pl.pallas_call(kernel, in_specs=[WHOLE] * (2 + len(sums)), out_specs=WHOL...  3.38 us
    pallas_call x1, Pallas kernels, attend(): pl.pallas_call(functools.partial(attend_kernel, heads), in_specs=[THERE]...  3.34 us
    ppermute x1, starting transfers between devices, on_device(): far_tokens = lax.ppermute(tokens, 'exp', [(e, e ^ 1) for e in range(4)])  1.64 us
  transfers between devices with their start and end apart: 8, of which 4 were waited for; matrix products, arithmetic and copies ran while one was open for 0% of the time, Pallas kernels for 32%

profile of v4, /device:TPU:0, one launch (start us, length us, event | category | flops | bytes accessed | tf_op | source)
XLA Modules:
  0.0 44.5 jit_solution(5521288110703146883)
XLA Ops:
  0.6 4.1 %collective-permute-start = (bf16[1,4,3072]{2,1,0:T(4,128)(2,1)}, bf16[1,4,3072]{2,1,0:T(4,128)(2,1)S(1)}, u32[]{:S(2)}, u32[]{:S(2)}) collective-permute-start(bf16[1,4,3072]{2,1,0:T(4,128)(2,1)} %bitcast.15), channel_id=1, source_target_pairs={{0,4},{2,6},{4,0},{6,2},{1,5},{3,7},{5,1},{7,3},{8,12},{10,14},{12... | collective-permute-start | bytes 73736 | tf_op jit(solution)/shard_map/ppermute | solution.py:440
  4.7 3.3 %attend.1 = (f32[128,1024]{1,0:T(8,128)S(1)}, bf16[1024,128]{1,0:T(8,128)(2,1)S(1)}, f32[128,8]{1,0:T(8,128)S(1)}, bf16[768,2,2304]{2,1,0:T(2,128)(2,1)S(1)}) custom-call(bf16[128,1024]{1,0:T(8,128)(2,1)} %q_ref.1, bf16[128,1024]{1,0:T(8,128)(2,1)} %k_hbm.1, bf16[128,1024]{1,0:T(8,128)(2,1)} %v_hbm.1, f32[8,128]{1,0:T(8,128)} %bitcast.21, ...), custom_call_target="tpu_custom_call" | custom-call | flops 10000000000 | bytes 786432 | tf_op jit(solution)/shard_map/attend/pallas_call | solution.py:183
  8.1 1.6 %collective-permute-start.1 = (bf16[2,4,3072]{2,1,0:T(4,128)(2,1)S(1)}, bf16[2,4,3072]{2,1,0:T(4,128)(2,1)S(1)}, u32[]{:S(2)}, u32[]{:S(2)}) collective-permute-start(bf16[2,4,3072]{2,1,0:T(4,128)(2,1)S(1)} %join.2.after_ref.first_ref), channel_id=1, source_target_pairs={{0,8},{8,0},{1,9},{9,1},{2,10},{10,2},{3,11},{11,3},{4,12},{12,4},... | collective-permute-start | bytes 147464 | tf_op jit(solution)/shard_map/ppermute | solution.py:446
  9.7 3.0 %hold.2.b_ref = bf16[768,2,2304]{2,1,0:T(2,128)(2,1)S(1)} custom-call(bf16[2,4,3072]{2,1,0:T(4,128)(2,1)S(1)} %join.2.after_ref.first_ref, bf16[3072,2,2304]{2,1,0:T(2,128)(2,1)} %bitcast.18), custom_call_target="tpu_custom_call" | custom-call | bytes 7077888 | tf_op jit(solution)/shard_map/hold/pallas_call | solution.py:255
  12.7 1.6 %collective-permute-start.2 = (bf16[4,4,3072]{2,1,0:T(4,128)(2,1)S(1)}, bf16[4,4,3072]{2,1,0:T(4,128)(2,1)S(1)}, u32[]{:S(2)}, u32[]{:S(2)}) collective-permute-start(bf16[4,4,3072]{2,1,0:T(4,128)(2,1)S(1)} %join.3.after_ref.near_ref), channel_id=1, source_target_pairs={{0,2},{2,0},{4,6},{6,4},{1,3},{3,1},{5,7},{7,5},{8,10},{10,8},{12,... | collective-permute-start | bytes 294920 | tf_op jit(solution)/shard_map/ppermute | solution.py:449
  14.4 3.0 %hold.3.c_ref = bf16[768,2,2304]{2,1,0:T(2,128)(2,1)S(1)} custom-call(bf16[4,4,3072]{2,1,0:T(4,128)(2,1)S(1)} %join.3.after_ref.near_ref, bf16[3072,2,2304]{2,1,0:T(2,128)(2,1)} %bitcast.19), custom_call_target="tpu_custom_call" | custom-call | bytes 7077888 | tf_op jit(solution)/shard_map/hold/pallas_call | solution.py:255
  17.4 0.0 collective-permute-done.2.far_ref
  17.4 5.7 %gate_up_sums.1.own_ref = bf16[64,2304]{1,0:T(8,128)(2,1)S(1)} custom-call(bf16[4,4,3072]{2,1,0:T(4,128)(2,1)S(1)} %join.3.after_ref.near_ref, bf16[4,4,3072]{2,1,0:T(4,128)(2,1)S(1)} %collective-permute-done.2.far_ref, bf16[768,2,2304]{2,1,0:T(2,128)(2,1)S(1)} %get-tuple-element.19.a_ref, bf16[768,2,2304]{2,1,0:T(2,128)(2,1)S(1)} %hold.2.b_ref, ...), custom_call_target="tpu_custom_call" | custom-call | flops 1811939328 | bytes 28311552 | tf_op jit(solution)/shard_map/gate_up_sums/pallas_call | solution.py:312
  23.1 0.1 collective-permute-start.3
  23.2 1.6 %collective-permute-done.3.other_ref = bf16[64,2304]{1,0:T(8,128)(2,1)S(1)} collective-permute-done((bf16[64,2304]{1,0:T(8,128)(2,1)S(1)}, bf16[64,2304]{1,0:T(8,128)(2,1)S(1)}, u32[]{:S(2)}, u32[]{:S(2)}) %collective-permute-start.3) | collective-permute-done | bytes 294944 | tf_op jit(solution)/shard_map/ppermute | solution.py:451
  24.8 0.1 hidden_units.1
  24.9 1.1 %collective-permute-start.5 = (bf16[32,1152]{1,0:T(8,128)(2,1)S(1)}, bf16[32,1152]{1,0:T(8,128)(2,1)S(1)}, u32[]{:S(2)}, u32[]{:S(2)}) collective-permute-start(bf16[32,1152]{1,0:T(8,128)(2,1)S(1)} %get-tuple-element.24), channel_id=1, source_target_pairs={{0,8},{8,0},{1,9},{9,1},{2,10},{10,2},{3,11},{11,3},{4,12},{12,4},... | collective-permute-start | bytes 221192 | tf_op jit(solution)/shard_map/ppermute | solution.py:452
  26.1 1.3 %down_own.1.own_ref = f32[32,1536]{1,0:T(8,128)S(1)} custom-call(bf16[32,2304]{1,0:T(8,128)(2,1)S(1)} %get-tuple-element.21.hidden_ref, bf16[4608,1536]{1,0:T(8,128)(2,1)S(1)} %bitcast.9), custom_call_target="tpu_custom_call" | custom-call | flops 226492416 | bytes 7077888 | tf_op jit(solution)/shard_map/down_own/pallas_call | solution.py:391
  27.4 1.0 %collective-permute-start.4 = (bf16[1024,128]{1,0:T(8,128)(2,1)S(1)}, bf16[1024,128]{1,0:T(8,128)(2,1)S(1)}, u32[]{:S(2)}, u32[]{:S(2)}) collective-permute-start(bf16[1024,128]{1,0:T(8,128)(2,1)S(1)} %get-tuple-element.23), channel_id=1, source_target_pairs={{0,8},{8,0},{1,9},{9,1},{2,10},{10,2},{3,11},{11,3},{4,12},{12,4},... | collective-permute-start | bytes 786440 | tf_op jit(solution)/shard_map/ppermute | solution.py:456
  28.4 1.0 %collective-permute-done.5.part_ref = bf16[32,1152]{1,0:T(8,128)(2,1)S(1)} collective-permute-done((bf16[32,1152]{1,0:T(8,128)(2,1)S(1)}, bf16[32,1152]{1,0:T(8,128)(2,1)S(1)}, u32[]{:S(2)}, u32[]{:S(2)}) %collective-permute-start.5) | collective-permute-done | bytes 73760 | tf_op jit(solution)/shard_map/ppermute | solution.py:452
  29.4 0.7 %down_near.1.own_ref = f32[32,1536]{1,0:T(8,128)S(1)} custom-call(bf16[32,1152]{1,0:T(8,128)(2,1)S(1)} %collective-permute-done.5.part_ref, bf16[4608,1536]{1,0:T(8,128)(2,1)S(1)} %bitcast.10, f32[32,1536]{1,0:T(8,128)S(1)} %down_own.1.own_ref), custom_call_target="tpu_custom_call" | custom-call | flops 113246208 | bytes 3538944 | tf_op jit(solution)/shard_map/down_near/pallas_call | solution.py:391
  30.1 0.0 copy-start.1
  30.1 0.0 copy-start.2
  30.1 0.5 %collective-permute-done.6.part_ref = bf16[32,1152]{1,0:T(8,128)(2,1)S(1)} collective-permute-done((bf16[32,1152]{1,0:T(8,128)(2,1)S(1)}, bf16[32,1152]{1,0:T(8,128)(2,1)S(1)}, u32[]{:S(2)}, u32[]{:S(2)}) %collective-permute-start.6) | collective-permute-done | bytes 73760 | tf_op jit(solution)/shard_map/ppermute | solution.py:457
  30.6 1.4 %down_far.1 = bf16[8,4,1536]{2,1,0:T(4,128)(2,1)} custom-call(bf16[32,1152]{1,0:T(8,128)(2,1)S(1)} %collective-permute-done.6.part_ref, bf16[4608,1536]{1,0:T(8,128)(2,1)S(1)} %bitcast.11, f32[32,1536]{1,0:T(8,128)S(1)} %down_near.1.own_ref), custom_call_target="tpu_custom_call" | custom-call | flops 113246208 | bytes 3538944 | tf_op jit(solution)/shard_map/down_far/pallas_call | solution.py:391
  32.0 4.5 %all-to-all-start = ((bf16[8,4,1536]{2,1,0:T(4,128)(2,1)}), bf16[8,4,1536]{2,1,0:T(4,128)(2,1)S(1)}, u32[]{:S(2)}, u32[]{:S(2)}) async-start(bf16[8,4,1536]{2,1,0:T(4,128)(2,1)} %down_far.1), calls=%async_computation | async-start | bytes 196608 | tf_op jit(solution)/shard_map/all_to_all | solution.py:463
  36.5 1.5 %finish.1 = bf16[128,1024]{1,0:T(8,128)(2,1)} custom-call(bf16[128,1024]{1,0:T(8,128)(2,1)S(1)} %copy-done, f32[128,1024]{1,0:T(8,128)S(1)} %get-tuple-element.14.intra_ref, f32[128,8]{1,0:T(8,128)S(1)} %get-tuple-element.15.cum_ref, bf16[1024,128]{1,0:T(8,128)(2,1)S(1)} %collective-permute-done.4.state_ref), custom_call_target="tpu_custom_call" | custom-call | flops 33554432 | bytes 1310720 | tf_op jit(solution)/shard_map/finish/pallas_call | solution.py:217
  37.9 5.8 %all-to-all-done = bf16[8,4,1536]{2,1,0:T(4,128)(2,1)S(1)} async-done(((bf16[8,4,1536]{2,1,0:T(4,128)(2,1)}), bf16[8,4,1536]{2,1,0:T(4,128)(2,1)S(1)}, u32[]{:S(2)}, u32[]{:S(2)}) %all-to-all-start) | async-done | bytes 98336 | tf_op jit(solution)/shard_map/all_to_all | solution.py:463
  43.7 0.8 %merge.1 = bf16[4,3072]{1,0:T(4,128)(2,1)} custom-call(s32[2,4]{1,0:T(2,128)S(1)} %bitcast.13, f32[2,4]{1,0:T(2,128)S(1)} %bitcast.14, bf16[2,4,4,1536]{3,2,1,0:T(4,128)(2,1)S(1)} %bitcast.12), custom_call_target="tpu_custom_call" | custom-call | flops 196608 | bytes 98304 | tf_op jit(solution)/shard_map/merge/pallas_call | solution.py:419
  (21 shorter events, 0.1 us)
Async XLA Ops:
  0.6 7.5 %collective-permute-start = (bf16[1,4,3072]{2,1,0:T(4,128)(2,1)}, bf16[1,4,3072]{2,1,0:T(4,128)(2,1)S(1)}, u32[]{:S(2)}, u32[]{:S(2)}) collective-permute-start(bf16[1,4,3072]{2,1,0:T(4,128)(2,1)} %bitcast.15), channel_id=1, source_target_pairs={{0,4},{2,6},{4,0},{6,2},{1,5},{3,7},{5,1},{7,3},{8,12},{10,14},{12... | collective-permute-start | bytes 73736 | tf_op jit(solution)/shard_map/ppermute | solution.py:440
  4.7 3.4 %copy-start.3 = (bf16[4,3072]{1,0:T(4,128)(2,1)S(1)}, bf16[4,3072]{1,0:T(4,128)(2,1)}, u32[]{:S(2)}) copy-start(bf16[4,3072]{1,0:T(4,128)(2,1)} %param.13) | copy-start | bytes 73732
  8.1 4.6 %collective-permute-start.1 = (bf16[2,4,3072]{2,1,0:T(4,128)(2,1)S(1)}, bf16[2,4,3072]{2,1,0:T(4,128)(2,1)S(1)}, u32[]{:S(2)}, u32[]{:S(2)}) collective-permute-start(bf16[2,4,3072]{2,1,0:T(4,128)(2,1)S(1)} %join.2.after_ref.first_ref), channel_id=1, source_target_pairs={{0,8},{8,0},{1,9},{9,1},{2,10},{10,2},{3,11},{11,3},{4,12},{12,4},... | collective-permute-start | bytes 147464 | tf_op jit(solution)/shard_map/ppermute | solution.py:446
  12.7 4.7 %collective-permute-start.2 = (bf16[4,4,3072]{2,1,0:T(4,128)(2,1)S(1)}, bf16[4,4,3072]{2,1,0:T(4,128)(2,1)S(1)}, u32[]{:S(2)}, u32[]{:S(2)}) collective-permute-start(bf16[4,4,3072]{2,1,0:T(4,128)(2,1)S(1)} %join.3.after_ref.near_ref), channel_id=1, source_target_pairs={{0,2},{2,0},{4,6},{6,4},{1,3},{3,1},{5,7},{7,5},{8,10},{10,8},{12,... | collective-permute-start | bytes 294920 | tf_op jit(solution)/shard_map/ppermute | solution.py:449
  17.4 8.6 %slice-start = ((s8[14155776]{0:T(1024)(128)(4,1)}), s8[4194304]{0:T(1024)(128)(4,1)S(1)}, s32[]{:S(2)}) async-start(s8[14155776]{0:T(1024)(128)(4,1)} %bitcast.7), calls=%async_computation.1 | async-start | bytes 8388608
  17.4 8.6 %slice-start.1 = ((s8[14155776]{0:T(1024)(128)(4,1)}), s8[4194304]{0:T(1024)(128)(4,1)S(1)}, s32[]{:S(2)}) async-start(s8[14155776]{0:T(1024)(128)(4,1)} %bitcast.7), calls=%async_computation.2 | async-start | bytes 8388608
  17.4 8.6 %slice-start.2 = ((s8[14155776]{0:T(1024)(128)(4,1)}), s8[4194304]{0:T(1024)(128)(4,1)S(1)}, s32[]{:S(2)}) async-start(s8[14155776]{0:T(1024)(128)(4,1)} %bitcast.7), calls=%async_computation.3 | async-start | bytes 8388608
  17.4 8.6 %slice-start.3 = ((s8[14155776]{0:T(1024)(128)(4,1)}), s8[1572864]{0:T(1024)(128)(4,1)S(1)}, s32[]{:S(2)}) async-start(s8[14155776]{0:T(1024)(128)(4,1)} %bitcast.7), calls=%async_computation.4 | async-start | bytes 3145728
  23.1 1.6 %collective-permute-start.3 = (bf16[64,2304]{1,0:T(8,128)(2,1)S(1)}, bf16[64,2304]{1,0:T(8,128)(2,1)S(1)}, u32[]{:S(2)}, u32[]{:S(2)}) collective-permute-start(bf16[64,2304]{1,0:T(8,128)(2,1)S(1)} %gate_up_sums.1.own_ref), channel_id=1, source_target_pairs={{0,1},{1,0},{2,3},{3,2},{4,5},{5,4},{6,7},{7,6},{8,9},{9,8},{10,11... | collective-permute-start | bytes 884744 | tf_op jit(solution)/shard_map/ppermute | solution.py:451
  24.9 4.4 %collective-permute-start.5 = (bf16[32,1152]{1,0:T(8,128)(2,1)S(1)}, bf16[32,1152]{1,0:T(8,128)(2,1)S(1)}, u32[]{:S(2)}, u32[]{:S(2)}) collective-permute-start(bf16[32,1152]{1,0:T(8,128)(2,1)S(1)} %get-tuple-element.24), channel_id=1, source_target_pairs={{0,8},{8,0},{1,9},{9,1},{2,10},{10,2},{3,11},{11,3},{4,12},{12,4},... | collective-permute-start | bytes 221192 | tf_op jit(solution)/shard_map/ppermute | solution.py:452
  27.4 9.1 %collective-permute-start.4 = (bf16[1024,128]{1,0:T(8,128)(2,1)S(1)}, bf16[1024,128]{1,0:T(8,128)(2,1)S(1)}, u32[]{:S(2)}, u32[]{:S(2)}) collective-permute-start(bf16[1024,128]{1,0:T(8,128)(2,1)S(1)} %get-tuple-element.23), channel_id=1, source_target_pairs={{0,8},{8,0},{1,9},{9,1},{2,10},{10,2},{3,11},{11,3},{4,12},{12,4},... | collective-permute-start | bytes 786440 | tf_op jit(solution)/shard_map/ppermute | solution.py:456
  29.4 1.3 %collective-permute-start.6 = (bf16[32,1152]{1,0:T(8,128)(2,1)S(1)}, bf16[32,1152]{1,0:T(8,128)(2,1)S(1)}, u32[]{:S(2)}, u32[]{:S(2)}) collective-permute-start(bf16[32,1152]{1,0:T(8,128)(2,1)S(1)} %collective-permute-done.5.part_ref), channel_id=1, source_target_pairs={{0,1},{1,0},{2,3},{3,2},{4,5},{5,4},{6,7},{7,6},{8,9},{9,8},{10,11... | collective-permute-start | bytes 221192 | tf_op jit(solution)/shard_map/ppermute | solution.py:457
  30.1 6.4 %copy-start = (bf16[128,1024]{1,0:T(8,128)(2,1)S(1)}, bf16[128,1024]{1,0:T(8,128)(2,1)}, u32[]{:S(2)}) copy-start(bf16[128,1024]{1,0:T(8,128)(2,1)} %q_ref.1) | copy-start | bytes 786436
  30.1 13.6 %copy-start.1 = (s32[4,2]{0,1:T(2,128)S(1)}, s32[4,2]{0,1:T(2,128)}, u32[]{:S(2)}) copy-start(s32[4,2]{0,1:T(2,128)} %param.14) | copy-start | bytes 100
  30.1 13.6 %copy-start.2 = (f32[4,2]{0,1:T(2,128)S(1)}, f32[4,2]{0,1:T(2,128)}, u32[]{:S(2)}) copy-start(f32[4,2]{0,1:T(2,128)} %param.15) | copy-start | bytes 100
  32.0 11.7 %all-to-all-start = ((bf16[8,4,1536]{2,1,0:T(4,128)(2,1)}), bf16[8,4,1536]{2,1,0:T(4,128)(2,1)S(1)}, u32[]{:S(2)}, u32[]{:S(2)}) async-start(bf16[8,4,1536]{2,1,0:T(4,128)(2,1)} %down_far.1), calls=%async_computation | async-start | bytes 196608 | tf_op jit(solution)/shard_map/all_to_all | solution.py:463

commit v5 on v4

--- a/solution.py
+++ b/solution.py
@@ -225,22 +225,22 @@
     )(queries, intra, cum, state)
 
 
-def join_kernel(first_ref, second_ref, out_ref):
-    count = first_ref.shape[0]
-    out_ref[:count] = first_ref[...]
-    out_ref[count:] = second_ref[...]
-
-
-def join(first, second):
+def join_kernel(*refs):
+    out_ref = refs[-1]
+    for i, part_ref in enumerate(refs[:-1]):
+        out_ref[i : i + 1] = part_ref[...]
+
+
+def join(*parts):
     return pl.pallas_call(
         join_kernel,
-        in_specs=[WHOLE] * 2,
-        out_specs=WHOLE,
-        out_shape=jax.ShapeDtypeStruct((2 * first.shape[0],) + first.shape[1:], first.dtype),
+        in_specs=[WHOLE] * len(parts),
+        out_specs=WHOLE,
+        out_shape=jax.ShapeDtypeStruct((len(parts),) + parts[0].shape[1:], parts[0].dtype),
         compiler_params=pltpu.CompilerParams(vmem_limit_bytes=4 * MIB),
-        cost_estimate=cost(3 * 10**9, 8 * first.size),
+        cost_estimate=cost(0, 16 * parts[0].size),
         name="join",
-    )(first, second)
+    )(*parts)
 
 
 def hold_kernel(first, after_ref, weights_hbm, held_ref, sem):
@@ -265,9 +265,9 @@
 
 
 def gate_up_kernel(
-    near_ref, far_ref, a_ref, b_ref, c_ref, weights_hbm, sums_ref, spread, last_ref, sem
+    near_ref, far_ref, a_ref, b_ref, weights_hbm, sums_ref, spread, last_ref, sem
 ):
-    held = (a_ref, b_ref, c_ref, last_ref)
+    held = (a_ref, b_ref, last_ref)
     first = sum(part.shape[0] for part in held[:-1])
     fetch = pltpu.make_async_copy(
         weights_hbm.at[pl.ds(first, last_ref.shape[0])], last_ref, sem
@@ -311,7 +311,7 @@
     held = [pltpu.with_memory_space_constraint(part, pltpu.VMEM) for part in held]
     return pl.pallas_call(
         gate_up_kernel,
-        in_specs=[WHOLE] * 5 + [THERE],
+        in_specs=[WHOLE] * 4 + [THERE],
         out_specs=WHOLE,
         out_shape=jax.ShapeDtypeStruct((2 * rows, units), BF16),
         scratch_shapes=[
@@ -319,7 +319,7 @@
             pltpu.VMEM((rest,) + weights.shape[1:], BF16),
             pltpu.SemaphoreType.DMA,
         ],
-        compiler_params=pltpu.CompilerParams(vmem_limit_bytes=16 * MIB),
+        compiler_params=pltpu.CompilerParams(vmem_limit_bytes=20 * MIB),
         cost_estimate=cost(4 * rows * weights.size, 2 * weights.size),
         name="gate_up_sums",
     )(near, far, *held, pltpu.with_memory_space_constraint(weights, pltpu.HBM))
@@ -367,20 +367,19 @@
 
 def down_near_kernel(part_ref, down_ref, own_ref, out_ref):
     other = other_product(part_ref[...], down_ref, lax.axis_index("tp"))
-    count = other.shape[0] // 4
-    pairs = [other[count * i : count * (i + 1)] for i in (1, 0, 3, 2)]
-    out_ref[...] = own_ref[...] + jnp.concatenate(pairs)
+    half = other.shape[0] // 2
+    out_ref[...] = own_ref[...] + jnp.concatenate([other[half:], other[:half]])
 
 
 def down_far_kernel(part_ref, down_ref, own_ref, out_ref):
     experts = lax.axis_size("exp")
     rows = out_ref.shape[1]
     other = other_product(part_ref[...], down_ref, 1 - lax.axis_index("tp"))
-    pairs = [other[2 * rows * i : 2 * rows * (i + 1)] for i in (1, 0, 3, 2)]
-    total = (own_ref[...] + jnp.concatenate(pairs)).astype(BF16)
+    half = other.shape[0] // 2
+    total = (own_ref[...] + jnp.concatenate([other[half:], other[:half]])).astype(BF16)
     for block in range(out_ref.shape[0]):
-        ctx = lax.axis_index("ctx") ^ ((block >> 1) & 1)
-        exp = lax.axis_index("exp") ^ (2 * (block & 1) + (block >> 2))
+        ctx = lax.axis_index("ctx") ^ (block // experts)
+        exp = lax.axis_index("exp") ^ (block % experts)
         out_ref[ctx * experts + exp] = total[block * rows : (block + 1) * rows]
 
 
@@ -437,17 +436,18 @@
     peers = ctx_count * expert_list
     swap = [(0, 1), (1, 0)]
     own_tokens = moe_input[None]
-    tokens = join(own_tokens, lax.ppermute(own_tokens, "exp", [(e, e ^ 2) for e in range(4)]))
+    moved = {
+        d: lax.ppermute(own_tokens, "exp", [(e, e ^ d) for e in range(expert_list)])
+        for d in range(expert_list - 1, 0, -1)
+    }
+    tokens = join(own_tokens, *(moved[d] for d in range(1, expert_list)))
     weights, w_down = (gate_up.reshape(gate_up.shape[1:]), down.reshape(down.shape[1:]))
-    quarter = weights.shape[0] // 4
-    intra, local, cum, held = attend(queries, keys, values, log_decay, weights, quarter)
+    part = weights.shape[0] // 24
+    intra, local, cum, held = attend(queries, keys, values, log_decay, weights, 8 * part)
     tokens, local = lax.optimization_barrier((tokens, local))
-    held_next = hold(tokens, weights, quarter, quarter)
-    arrived, held_next = lax.optimization_barrier((lax.ppermute(tokens, "ctx", swap), held_next))
-    tokens = join(tokens, arrived)
-    held_last = hold(tokens, weights, 2 * quarter, quarter)
-    far_tokens = lax.ppermute(tokens, "exp", [(e, e ^ 1) for e in range(4)])
-    sums = gate_up_sums(tokens, far_tokens, (held, held_next, held_last), weights)
+    held_next = hold(tokens, weights, 8 * part, 8 * part)
+    far_tokens = lax.ppermute(tokens, "ctx", swap)
+    sums = gate_up_sums(tokens, far_tokens, (held, held_next), weights)
     hidden, part = hidden_units(sums, lax.ppermute(sums, "tp", swap))
     part = lax.ppermute(part, "ctx", swap)
     sums_shape = (hidden.shape[0], w_down.shape[1])

time: 44.8 us -> 44.5 us (level)
  Pallas kernels: 20.8 us -> 19.9 us
  starting transfers between devices: 13.9 us -> 14.5 us
    pallas_call x2 -> x1, Pallas kernels: 6.03 us -> 3.84 us  [hold(): pl.pallas_call(functools.partial(hold_kernel, first), in_specs=[THERE, TH...]
    pallas_call x1, Pallas kernels: 3.34 us -> 4.01 us  [attend(): pl.pallas_call(functools.partial(attend_kernel, heads), in_specs=[THERE]...]
    pallas_call x3 -> x2, Pallas kernels: 5.7 us -> 6.29 us  [the longest x1 6.29 us: gate_up_sums(): pl.pallas_call(gate_up_kernel, in_specs=[WHOLE] * 4 + [THERE], out_specs=...]
    all_to_all x1, starting transfers between devices: 4.45 us -> 4.96 us  [on_device(): lax.all_to_all(expert_out, ('ctx', 'exp'), split_axis=0, concat_axis=0, t...]
    ppermute x3 -> x4, starting transfers between devices: 7.3 us -> 7.31 us  [the longest x3 5.76 us: on_device(): lax.ppermute(own_tokens, 'exp', [(e, e ^ d) for e in range(expert_list)])]
  transfers between devices with their start and end apart: 8 -> 9, of which waited for: 4 -> 5; matrix products, arithmetic and copies ran while one was open for 0% -> 0% of each run, Pallas kernels for 32% -> 29%
where the time goes in v5:
time: 44.5 us; the launch traced here: 44.3 us
  Pallas kernels  19.9 us (45%)
  starting transfers between devices  14.5 us (33%)
  waiting for transfers between devices  9.1 us (20%)
  between operations  0.76 us (2%)
    pallas_call x1, Pallas kernels, gate_up_sums(): pl.pallas_call(gate_up_kernel, in_specs=[WHOLE] * 4 + [THERE], out_specs=...  6.29 us
    all_to_all x1, waiting for transfers between devices, on_device(): lax.all_to_all(expert_out, ('ctx', 'exp'), split_axis=0, concat_axis=0, t...  5.78 us
    ppermute x3, starting transfers between devices, on_device(): lax.ppermute(own_tokens, 'exp', [(e, e ^ d) for e in range(expert_list)])  5.76 us
    all_to_all x1, starting transfers between devices, on_device(): lax.all_to_all(expert_out, ('ctx', 'exp'), split_axis=0, concat_axis=0, t...  4.96 us
    pallas_call x1, Pallas kernels, attend(): pl.pallas_call(functools.partial(attend_kernel, heads), in_specs=[THERE]...  4.01 us
    pallas_call x1, Pallas kernels, hold(): pl.pallas_call(functools.partial(hold_kernel, first), in_specs=[THERE, TH...  3.84 us
    pallas_call x3, Pallas kernels, down_sums(): pl.pallas_call(kernel, in_specs=[WHOLE] * (2 + len(sums)), out_specs=WHOL...  3.37 us
    ppermute x1, waiting for transfers between devices, on_device(): hidden, part = hidden_units(sums, lax.ppermute(sums, 'tp', swap))  1.57 us
  transfers between devices with their start and end apart: 9, of which 5 were waited for; matrix products, arithmetic and copies ran while one was open for 0% of the time, Pallas kernels for 29%

profile of v5, /device:TPU:0, one launch (start us, length us, event | category | flops | bytes accessed | tf_op | source)
XLA Modules:
  0.0 44.3 jit_solution(10149108686539305702)
XLA Ops:
  0.6 5.1 %collective-permute-start.2 = (bf16[1,4,3072]{2,1,0:T(4,128)(2,1)}, bf16[1,4,3072]{2,1,0:T(4,128)(2,1)S(1)}, u32[]{:S(2)}, u32[]{:S(2)}) collective-permute-start(bf16[1,4,3072]{2,1,0:T(4,128)(2,1)} %bitcast.13), channel_id=1, source_target_pairs={{0,6},{2,4},{4,2},{6,0},{1,7},{3,5},{5,3},{7,1},{8,14},{10,12},{12... | collective-permute-start | bytes 73736 | tf_op jit(solution)/shard_map/ppermute | solution.py:440
  5.7 0.0 collective-permute-start.1
  5.7 0.6 %collective-permute-start = (bf16[1,4,3072]{2,1,0:T(4,128)(2,1)}, bf16[1,4,3072]{2,1,0:T(4,128)(2,1)S(1)}, u32[]{:S(2)}, u32[]{:S(2)}) collective-permute-start(bf16[1,4,3072]{2,1,0:T(4,128)(2,1)} %bitcast.15), channel_id=1, source_target_pairs={{0,2},{2,0},{4,6},{6,4},{1,3},{3,1},{5,7},{7,5},{8,10},{10,8},{12,... | collective-permute-start | bytes 73736 | tf_op jit(solution)/shard_map/ppermute | solution.py:440
  6.4 4.0 %attend.1 = (f32[128,1024]{1,0:T(8,128)S(1)}, bf16[1024,128]{1,0:T(8,128)(2,1)S(1)}, f32[128,8]{1,0:T(8,128)S(1)}, bf16[1024,2,2304]{2,1,0:T(2,128)(2,1)S(1)}) custom-call(bf16[128,1024]{1,0:T(8,128)(2,1)} %q_ref.1, bf16[128,1024]{1,0:T(8,128)(2,1)} %k_hbm.1, bf16[128,1024]{1,0:T(8,128)(2,1)} %v_hbm.1, f32[8,128]{1,0:T(8,128)} %bitcast.22, ...), custom_call_target="tpu_custom_call" | custom-call | flops 10000000000 | bytes 786432 | tf_op jit(solution)/shard_map/attend/pallas_call | solution.py:183
  10.4 0.3 collective-permute-done.1.refs_2_
  10.7 1.6 %collective-permute-start.3 = (bf16[4,4,3072]{2,1,0:T(4,128)(2,1)S(1)}, bf16[4,4,3072]{2,1,0:T(4,128)(2,1)S(1)}, u32[]{:S(2)}, u32[]{:S(2)}) collective-permute-start(bf16[4,4,3072]{2,1,0:T(4,128)(2,1)S(1)} %join.1.after_ref.near_ref), channel_id=1, source_target_pairs={{0,8},{8,0},{1,9},{9,1},{2,10},{10,2},{3,11},{11,3},{4,12},{12,4},... | collective-permute-start | bytes 294920 | tf_op jit(solution)/shard_map/ppermute | solution.py:449
  12.3 3.8 %hold.1.b_ref = bf16[1024,2,2304]{2,1,0:T(2,128)(2,1)S(1)} custom-call(bf16[4,4,3072]{2,1,0:T(4,128)(2,1)S(1)} %join.1.after_ref.near_ref, bf16[3072,2,2304]{2,1,0:T(2,128)(2,1)} %bitcast.20), custom_call_target="tpu_custom_call" | custom-call | bytes 9437184 | tf_op jit(solution)/shard_map/hold/pallas_call | solution.py:255
  16.1 0.0 slice-start.2
  16.1 6.3 %gate_up_sums.1.own_ref = bf16[64,2304]{1,0:T(8,128)(2,1)S(1)} custom-call(bf16[4,4,3072]{2,1,0:T(4,128)(2,1)S(1)} %join.1.after_ref.near_ref, bf16[4,4,3072]{2,1,0:T(4,128)(2,1)S(1)} %collective-permute-done.3.far_ref, bf16[1024,2,2304]{2,1,0:T(2,128)(2,1)S(1)} %get-tuple-element.16.a_ref, bf16[1024,2,2304]{2,1,0:T(2,128)(2,1)S(1)} %hold.1.b_ref, ...), custom_call_target="tpu_custom_call" | custom-call | flops 1811939328 | bytes 28311552 | tf_op jit(solution)/shard_map/gate_up_sums/pallas_call | solution.py:312
  22.4 0.1 collective-permute-start.4
  22.5 1.6 %collective-permute-done.4.other_ref = bf16[64,2304]{1,0:T(8,128)(2,1)S(1)} collective-permute-done((bf16[64,2304]{1,0:T(8,128)(2,1)S(1)}, bf16[64,2304]{1,0:T(8,128)(2,1)S(1)}, u32[]{:S(2)}, u32[]{:S(2)}) %collective-permute-start.4) | collective-permute-done | bytes 294944 | tf_op jit(solution)/shard_map/ppermute | solution.py:451
  24.1 0.1 hidden_units.1
  24.2 0.8 %collective-permute-start.6 = (bf16[32,1152]{1,0:T(8,128)(2,1)S(1)}, bf16[32,1152]{1,0:T(8,128)(2,1)S(1)}, u32[]{:S(2)}, u32[]{:S(2)}) collective-permute-start(bf16[32,1152]{1,0:T(8,128)(2,1)S(1)} %get-tuple-element.20), channel_id=1, source_target_pairs={{0,8},{8,0},{1,9},{9,1},{2,10},{10,2},{3,11},{11,3},{4,12},{12,4},... | collective-permute-start | bytes 221192 | tf_op jit(solution)/shard_map/ppermute | solution.py:452
  25.1 1.3 %down_own.1.own_ref = f32[32,1536]{1,0:T(8,128)S(1)} custom-call(bf16[32,2304]{1,0:T(8,128)(2,1)S(1)} %get-tuple-element.17.hidden_ref, bf16[4608,1536]{1,0:T(8,128)(2,1)S(1)} %bitcast.9), custom_call_target="tpu_custom_call" | custom-call | flops 226492416 | bytes 7077888 | tf_op jit(solution)/shard_map/down_own/pallas_call | solution.py:390
  26.4 0.0 copy-start.3
  26.4 1.4 %collective-permute-start.5 = (bf16[1024,128]{1,0:T(8,128)(2,1)S(1)}, bf16[1024,128]{1,0:T(8,128)(2,1)S(1)}, u32[]{:S(2)}, u32[]{:S(2)}) collective-permute-start(bf16[1024,128]{1,0:T(8,128)(2,1)S(1)} %get-tuple-element.19), channel_id=1, source_target_pairs={{0,8},{8,0},{1,9},{9,1},{2,10},{10,2},{3,11},{11,3},{4,12},{12,4},... | collective-permute-start | bytes 786440 | tf_op jit(solution)/shard_map/ppermute | solution.py:456
  27.8 0.9 %collective-permute-done.6.part_ref = bf16[32,1152]{1,0:T(8,128)(2,1)S(1)} collective-permute-done((bf16[32,1152]{1,0:T(8,128)(2,1)S(1)}, bf16[32,1152]{1,0:T(8,128)(2,1)S(1)}, u32[]{:S(2)}, u32[]{:S(2)}) %collective-permute-start.6) | collective-permute-done | bytes 73760 | tf_op jit(solution)/shard_map/ppermute | solution.py:452
  28.7 0.7 %down_near.1.own_ref = f32[32,1536]{1,0:T(8,128)S(1)} custom-call(bf16[32,1152]{1,0:T(8,128)(2,1)S(1)} %collective-permute-done.6.part_ref, bf16[4608,1536]{1,0:T(8,128)(2,1)S(1)} %bitcast.10, f32[32,1536]{1,0:T(8,128)S(1)} %down_own.1.own_ref), custom_call_target="tpu_custom_call" | custom-call | flops 113246208 | bytes 3538944 | tf_op jit(solution)/shard_map/down_near/pallas_call | solution.py:390
  29.4 0.6 %collective-permute-done.7.part_ref = bf16[32,1152]{1,0:T(8,128)(2,1)S(1)} collective-permute-done((bf16[32,1152]{1,0:T(8,128)(2,1)S(1)}, bf16[32,1152]{1,0:T(8,128)(2,1)S(1)}, u32[]{:S(2)}, u32[]{:S(2)}) %collective-permute-start.7) | collective-permute-done | bytes 73760 | tf_op jit(solution)/shard_map/ppermute | solution.py:457
  29.9 1.4 %down_far.1 = bf16[8,4,1536]{2,1,0:T(4,128)(2,1)} custom-call(bf16[32,1152]{1,0:T(8,128)(2,1)S(1)} %collective-permute-done.7.part_ref, bf16[4608,1536]{1,0:T(8,128)(2,1)S(1)} %bitcast.11, f32[32,1536]{1,0:T(8,128)S(1)} %down_near.1.own_ref), custom_call_target="tpu_custom_call" | custom-call | flops 113246208 | bytes 3538944 | tf_op jit(solution)/shard_map/down_far/pallas_call | solution.py:390
  31.3 5.0 %all-to-all-start = ((bf16[8,4,1536]{2,1,0:T(4,128)(2,1)}), bf16[8,4,1536]{2,1,0:T(4,128)(2,1)S(1)}, u32[]{:S(2)}, u32[]{:S(2)}) async-start(bf16[8,4,1536]{2,1,0:T(4,128)(2,1)} %down_far.1), calls=%async_computation | async-start | bytes 196608 | tf_op jit(solution)/shard_map/all_to_all | solution.py:463
  36.3 1.5 %finish.1 = bf16[128,1024]{1,0:T(8,128)(2,1)} custom-call(bf16[128,1024]{1,0:T(8,128)(2,1)S(1)} %copy-done, f32[128,1024]{1,0:T(8,128)S(1)} %get-tuple-element.12.intra_ref, f32[128,8]{1,0:T(8,128)S(1)} %get-tuple-element.13.cum_ref, bf16[1024,128]{1,0:T(8,128)(2,1)S(1)} %collective-permute-done.5.state_ref), custom_call_target="tpu_custom_call" | custom-call | flops 33554432 | bytes 1310720 | tf_op jit(solution)/shard_map/finish/pallas_call | solution.py:217
  37.7 5.8 %all-to-all-done = bf16[8,4,1536]{2,1,0:T(4,128)(2,1)S(1)} async-done(((bf16[8,4,1536]{2,1,0:T(4,128)(2,1)}), bf16[8,4,1536]{2,1,0:T(4,128)(2,1)S(1)}, u32[]{:S(2)}, u32[]{:S(2)}) %all-to-all-start) | async-done | bytes 98336 | tf_op jit(solution)/shard_map/all_to_all | solution.py:463
  43.5 0.8 %merge.1 = bf16[4,3072]{1,0:T(4,128)(2,1)} custom-call(s32[2,4]{1,0:T(2,128)S(1)} %bitcast.17, f32[2,4]{1,0:T(2,128)S(1)} %bitcast.18, bf16[2,4,4,1536]{3,2,1,0:T(4,128)(2,1)S(1)} %bitcast.12), custom_call_target="tpu_custom_call" | custom-call | flops 196608 | bytes 98304 | tf_op jit(solution)/shard_map/merge/pallas_call | solution.py:418
  (21 shorter events, 0.0 us)
Async XLA Ops:
  0.6 9.8 %collective-permute-start.2 = (bf16[1,4,3072]{2,1,0:T(4,128)(2,1)}, bf16[1,4,3072]{2,1,0:T(4,128)(2,1)S(1)}, u32[]{:S(2)}, u32[]{:S(2)}) collective-permute-start(bf16[1,4,3072]{2,1,0:T(4,128)(2,1)} %bitcast.13), channel_id=1, source_target_pairs={{0,6},{2,4},{4,2},{6,0},{1,7},{3,5},{5,3},{7,1},{8,14},{10,12},{12... | collective-permute-start | bytes 73736 | tf_op jit(solution)/shard_map/ppermute | solution.py:440
  5.7 4.9 %collective-permute-start.1 = (bf16[1,4,3072]{2,1,0:T(4,128)(2,1)}, bf16[1,4,3072]{2,1,0:T(4,128)(2,1)S(1)}, u32[]{:S(2)}, u32[]{:S(2)}) collective-permute-start(bf16[1,4,3072]{2,1,0:T(4,128)(2,1)} %bitcast.14), channel_id=1, source_target_pairs={{0,4},{2,6},{4,0},{6,2},{1,5},{3,7},{5,1},{7,3},{8,12},{10,14},{12... | collective-permute-start | bytes 73736 | tf_op jit(solution)/shard_map/ppermute | solution.py:440
  5.7 4.9 %collective-permute-start = (bf16[1,4,3072]{2,1,0:T(4,128)(2,1)}, bf16[1,4,3072]{2,1,0:T(4,128)(2,1)S(1)}, u32[]{:S(2)}, u32[]{:S(2)}) collective-permute-start(bf16[1,4,3072]{2,1,0:T(4,128)(2,1)} %bitcast.15), channel_id=1, source_target_pairs={{0,2},{2,0},{4,6},{6,4},{1,3},{3,1},{5,7},{7,5},{8,10},{10,8},{12,... | collective-permute-start | bytes 73736 | tf_op jit(solution)/shard_map/ppermute | solution.py:440
  6.4 4.3 %copy-start.1 = (bf16[4,3072]{1,0:T(4,128)(2,1)S(1)}, bf16[4,3072]{1,0:T(4,128)(2,1)}, u32[]{:S(2)}) copy-start(bf16[4,3072]{1,0:T(4,128)(2,1)} %param.13) | copy-start | bytes 73732
  10.7 5.4 %collective-permute-start.3 = (bf16[4,4,3072]{2,1,0:T(4,128)(2,1)S(1)}, bf16[4,4,3072]{2,1,0:T(4,128)(2,1)S(1)}, u32[]{:S(2)}, u32[]{:S(2)}) collective-permute-start(bf16[4,4,3072]{2,1,0:T(4,128)(2,1)S(1)} %join.1.after_ref.near_ref), channel_id=1, source_target_pairs={{0,8},{8,0},{1,9},{9,1},{2,10},{10,2},{3,11},{11,3},{4,12},{12,4},... | collective-permute-start | bytes 294920 | tf_op jit(solution)/shard_map/ppermute | solution.py:449
  12.3 12.8 %slice-start = ((s8[14155776]{0:T(1024)(128)(4,1)}), s8[4194304]{0:T(1024)(128)(4,1)S(1)}, s32[]{:S(2)}) async-start(s8[14155776]{0:T(1024)(128)(4,1)} %bitcast.7), calls=%async_computation.1 | async-start | bytes 8388608
  12.3 12.8 %slice-start.1 = ((s8[14155776]{0:T(1024)(128)(4,1)}), s8[4194304]{0:T(1024)(128)(4,1)S(1)}, s32[]{:S(2)}) async-start(s8[14155776]{0:T(1024)(128)(4,1)} %bitcast.7), calls=%async_computation.2 | async-start | bytes 8388608
  16.1 8.9 %slice-start.2 = ((s8[14155776]{0:T(1024)(128)(4,1)}), s8[4194304]{0:T(1024)(128)(4,1)S(1)}, s32[]{:S(2)}) async-start(s8[14155776]{0:T(1024)(128)(4,1)} %bitcast.7), calls=%async_computation.3 | async-start | bytes 8388608
  16.1 8.9 %slice-start.3 = ((s8[14155776]{0:T(1024)(128)(4,1)}), s8[1572864]{0:T(1024)(128)(4,1)S(1)}, s32[]{:S(2)}) async-start(s8[14155776]{0:T(1024)(128)(4,1)} %bitcast.7), calls=%async_computation.4 | async-start | bytes 3145728
  22.4 1.6 %collective-permute-start.4 = (bf16[64,2304]{1,0:T(8,128)(2,1)S(1)}, bf16[64,2304]{1,0:T(8,128)(2,1)S(1)}, u32[]{:S(2)}, u32[]{:S(2)}) collective-permute-start(bf16[64,2304]{1,0:T(8,128)(2,1)S(1)} %gate_up_sums.1.own_ref), channel_id=1, source_target_pairs={{0,1},{1,0},{2,3},{3,2},{4,5},{5,4},{6,7},{7,6},{8,9},{9,8},{10,11... | collective-permute-start | bytes 884744 | tf_op jit(solution)/shard_map/ppermute | solution.py:451
  24.2 4.4 %collective-permute-start.6 = (bf16[32,1152]{1,0:T(8,128)(2,1)S(1)}, bf16[32,1152]{1,0:T(8,128)(2,1)S(1)}, u32[]{:S(2)}, u32[]{:S(2)}) collective-permute-start(bf16[32,1152]{1,0:T(8,128)(2,1)S(1)} %get-tuple-element.20), channel_id=1, source_target_pairs={{0,8},{8,0},{1,9},{9,1},{2,10},{10,2},{3,11},{11,3},{4,12},{12,4},... | collective-permute-start | bytes 221192 | tf_op jit(solution)/shard_map/ppermute | solution.py:452
  26.4 9.9 %copy-start = (bf16[128,1024]{1,0:T(8,128)(2,1)S(1)}, bf16[128,1024]{1,0:T(8,128)(2,1)}, u32[]{:S(2)}) copy-start(bf16[128,1024]{1,0:T(8,128)(2,1)} %q_ref.1) | copy-start | bytes 786436
  26.4 17.1 %copy-start.2 = (s32[4,2]{0,1:T(2,128)S(1)}, s32[4,2]{0,1:T(2,128)}, u32[]{:S(2)}) copy-start(s32[4,2]{0,1:T(2,128)} %param.14) | copy-start | bytes 100
  26.4 17.1 %copy-start.3 = (f32[4,2]{0,1:T(2,128)S(1)}, f32[4,2]{0,1:T(2,128)}, u32[]{:S(2)}) copy-start(f32[4,2]{0,1:T(2,128)} %param.15) | copy-start | bytes 100
  26.4 9.8 %collective-permute-start.5 = (bf16[1024,128]{1,0:T(8,128)(2,1)S(1)}, bf16[1024,128]{1,0:T(8,128)(2,1)S(1)}, u32[]{:S(2)}, u32[]{:S(2)}) collective-permute-start(bf16[1024,128]{1,0:T(8,128)(2,1)S(1)} %get-tuple-element.19), channel_id=1, source_target_pairs={{0,8},{8,0},{1,9},{9,1},{2,10},{10,2},{3,11},{11,3},{4,12},{12,4},... | collective-permute-start | bytes 786440 | tf_op jit(solution)/shard_map/ppermute | solution.py:456
  28.7 1.3 %collective-permute-start.7 = (bf16[32,1152]{1,0:T(8,128)(2,1)S(1)}, bf16[32,1152]{1,0:T(8,128)(2,1)S(1)}, u32[]{:S(2)}, u32[]{:S(2)}) collective-permute-start(bf16[32,1152]{1,0:T(8,128)(2,1)S(1)} %collective-permute-done.6.part_ref), channel_id=1, source_target_pairs={{0,1},{1,0},{2,3},{3,2},{4,5},{5,4},{6,7},{7,6},{8,9},{9,8},{10,11... | collective-permute-start | bytes 221192 | tf_op jit(solution)/shard_map/ppermute | solution.py:457
  31.3 12.2 %all-to-all-start = ((bf16[8,4,1536]{2,1,0:T(4,128)(2,1)}), bf16[8,4,1536]{2,1,0:T(4,128)(2,1)S(1)}, u32[]{:S(2)}, u32[]{:S(2)}) async-start(bf16[8,4,1536]{2,1,0:T(4,128)(2,1)} %down_far.1), calls=%async_computation | async-start | bytes 196608 | tf_op jit(solution)/shard_map/all_to_all | solution.py:463

commit v6 on v5

--- a/solution.py
+++ b/solution.py
@@ -438,7 +438,7 @@
     own_tokens = moe_input[None]
     moved = {
         d: lax.ppermute(own_tokens, "exp", [(e, e ^ d) for e in range(expert_list)])
-        for d in range(expert_list - 1, 0, -1)
+        for d in (3, 1, 2)
     }
     tokens = join(own_tokens, *(moved[d] for d in range(1, expert_list)))
     weights, w_down = (gate_up.reshape(gate_up.shape[1:]), down.reshape(down.shape[1:]))

time: 44.5 us -> 44.5 us (level)
  no operation moved by 1% of the time
where the time goes in v6:
time: 44.5 us; the launch traced here: 44.3 us
  Pallas kernels  19.9 us (45%)
  starting transfers between devices  14.5 us (33%)
  waiting for transfers between devices  9.1 us (20%)
  between operations  0.76 us (2%)
    pallas_call x1, Pallas kernels, gate_up_sums(): pl.pallas_call(gate_up_kernel, in_specs=[WHOLE] * 4 + [THERE], out_specs=...  6.29 us
    all_to_all x1, waiting for transfers between devices, on_device(): lax.all_to_all(expert_out, ('ctx', 'exp'), split_axis=0, concat_axis=0, t...  5.78 us
    ppermute x3, starting transfers between devices, on_device(): lax.ppermute(own_tokens, 'exp', [(e, e ^ d) for e in range(expert_list)])  5.76 us
    all_to_all x1, starting transfers between devices, on_device(): lax.all_to_all(expert_out, ('ctx', 'exp'), split_axis=0, concat_axis=0, t...  4.96 us
    pallas_call x1, Pallas kernels, attend(): pl.pallas_call(functools.partial(attend_kernel, heads), in_specs=[THERE]...  4.01 us
    pallas_call x1, Pallas kernels, hold(): pl.pallas_call(functools.partial(hold_kernel, first), in_specs=[THERE, TH...  3.84 us
    pallas_call x3, Pallas kernels, down_sums(): pl.pallas_call(kernel, in_specs=[WHOLE] * (2 + len(sums)), out_specs=WHOL...  3.37 us
    ppermute x1, waiting for transfers between devices, on_device(): hidden, part = hidden_units(sums, lax.ppermute(sums, 'tp', swap))  1.57 us
  transfers between devices with their start and end apart: 9, of which 5 were waited for; matrix products, arithmetic and copies ran while one was open for 0% of the time, Pallas kernels for 29%

profile of v6, /device:TPU:0, one launch (start us, length us, event | category | flops | bytes accessed | tf_op | source)
XLA Modules:
  0.0 44.3 jit_solution(10149108686539305702)
XLA Ops:
  0.6 5.1 %collective-permute-start.2 = (bf16[1,4,3072]{2,1,0:T(4,128)(2,1)}, bf16[1,4,3072]{2,1,0:T(4,128)(2,1)S(1)}, u32[]{:S(2)}, u32[]{:S(2)}) collective-permute-start(bf16[1,4,3072]{2,1,0:T(4,128)(2,1)} %bitcast.13), channel_id=1, source_target_pairs={{0,6},{2,4},{4,2},{6,0},{1,7},{3,5},{5,3},{7,1},{8,14},{10,12},{12... | collective-permute-start | bytes 73736 | tf_op jit(solution)/shard_map/ppermute | solution.py:440
  5.7 0.0 collective-permute-start.1
  5.7 0.6 %collective-permute-start = (bf16[1,4,3072]{2,1,0:T(4,128)(2,1)}, bf16[1,4,3072]{2,1,0:T(4,128)(2,1)S(1)}, u32[]{:S(2)}, u32[]{:S(2)}) collective-permute-start(bf16[1,4,3072]{2,1,0:T(4,128)(2,1)} %bitcast.15), channel_id=1, source_target_pairs={{0,2},{2,0},{4,6},{6,4},{1,3},{3,1},{5,7},{7,5},{8,10},{10,8},{12,... | collective-permute-start | bytes 73736 | tf_op jit(solution)/shard_map/ppermute | solution.py:440
  6.4 4.0 %attend.1 = (f32[128,1024]{1,0:T(8,128)S(1)}, bf16[1024,128]{1,0:T(8,128)(2,1)S(1)}, f32[128,8]{1,0:T(8,128)S(1)}, bf16[1024,2,2304]{2,1,0:T(2,128)(2,1)S(1)}) custom-call(bf16[128,1024]{1,0:T(8,128)(2,1)} %q_ref.1, bf16[128,1024]{1,0:T(8,128)(2,1)} %k_hbm.1, bf16[128,1024]{1,0:T(8,128)(2,1)} %v_hbm.1, f32[8,128]{1,0:T(8,128)} %bitcast.22, ...), custom_call_target="tpu_custom_call" | custom-call | flops 10000000000 | bytes 786432 | tf_op jit(solution)/shard_map/attend/pallas_call | solution.py:183
  10.4 0.3 collective-permute-done.1.refs_2_
  10.7 1.6 %collective-permute-start.3 = (bf16[4,4,3072]{2,1,0:T(4,128)(2,1)S(1)}, bf16[4,4,3072]{2,1,0:T(4,128)(2,1)S(1)}, u32[]{:S(2)}, u32[]{:S(2)}) collective-permute-start(bf16[4,4,3072]{2,1,0:T(4,128)(2,1)S(1)} %join.1.after_ref.near_ref), channel_id=1, source_target_pairs={{0,8},{8,0},{1,9},{9,1},{2,10},{10,2},{3,11},{11,3},{4,12},{12,4},... | collective-permute-start | bytes 294920 | tf_op jit(solution)/shard_map/ppermute | solution.py:449
  12.3 3.8 %hold.1.b_ref = bf16[1024,2,2304]{2,1,0:T(2,128)(2,1)S(1)} custom-call(bf16[4,4,3072]{2,1,0:T(4,128)(2,1)S(1)} %join.1.after_ref.near_ref, bf16[3072,2,2304]{2,1,0:T(2,128)(2,1)} %bitcast.20), custom_call_target="tpu_custom_call" | custom-call | bytes 9437184 | tf_op jit(solution)/shard_map/hold/pallas_call | solution.py:255
  16.1 0.0 slice-start.2
  16.1 6.3 %gate_up_sums.1.own_ref = bf16[64,2304]{1,0:T(8,128)(2,1)S(1)} custom-call(bf16[4,4,3072]{2,1,0:T(4,128)(2,1)S(1)} %join.1.after_ref.near_ref, bf16[4,4,3072]{2,1,0:T(4,128)(2,1)S(1)} %collective-permute-done.3.far_ref, bf16[1024,2,2304]{2,1,0:T(2,128)(2,1)S(1)} %get-tuple-element.16.a_ref, bf16[1024,2,2304]{2,1,0:T(2,128)(2,1)S(1)} %hold.1.b_ref, ...), custom_call_target="tpu_custom_call" | custom-call | flops 1811939328 | bytes 28311552 | tf_op jit(solution)/shard_map/gate_up_sums/pallas_call | solution.py:312
  22.4 0.1 collective-permute-start.4
  22.5 1.6 %collective-permute-done.4.other_ref = bf16[64,2304]{1,0:T(8,128)(2,1)S(1)} collective-permute-done((bf16[64,2304]{1,0:T(8,128)(2,1)S(1)}, bf16[64,2304]{1,0:T(8,128)(2,1)S(1)}, u32[]{:S(2)}, u32[]{:S(2)}) %collective-permute-start.4) | collective-permute-done | bytes 294944 | tf_op jit(solution)/shard_map/ppermute | solution.py:451
  24.1 0.1 hidden_units.1
  24.2 0.8 %collective-permute-start.6 = (bf16[32,1152]{1,0:T(8,128)(2,1)S(1)}, bf16[32,1152]{1,0:T(8,128)(2,1)S(1)}, u32[]{:S(2)}, u32[]{:S(2)}) collective-permute-start(bf16[32,1152]{1,0:T(8,128)(2,1)S(1)} %get-tuple-element.20), channel_id=1, source_target_pairs={{0,8},{8,0},{1,9},{9,1},{2,10},{10,2},{3,11},{11,3},{4,12},{12,4},... | collective-permute-start | bytes 221192 | tf_op jit(solution)/shard_map/ppermute | solution.py:452
  25.1 1.3 %down_own.1.own_ref = f32[32,1536]{1,0:T(8,128)S(1)} custom-call(bf16[32,2304]{1,0:T(8,128)(2,1)S(1)} %get-tuple-element.17.hidden_ref, bf16[4608,1536]{1,0:T(8,128)(2,1)S(1)} %bitcast.9), custom_call_target="tpu_custom_call" | custom-call | flops 226492416 | bytes 7077888 | tf_op jit(solution)/shard_map/down_own/pallas_call | solution.py:390
  26.4 0.0 copy-start.3
  26.4 1.4 %collective-permute-start.5 = (bf16[1024,128]{1,0:T(8,128)(2,1)S(1)}, bf16[1024,128]{1,0:T(8,128)(2,1)S(1)}, u32[]{:S(2)}, u32[]{:S(2)}) collective-permute-start(bf16[1024,128]{1,0:T(8,128)(2,1)S(1)} %get-tuple-element.19), channel_id=1, source_target_pairs={{0,8},{8,0},{1,9},{9,1},{2,10},{10,2},{3,11},{11,3},{4,12},{12,4},... | collective-permute-start | bytes 786440 | tf_op jit(solution)/shard_map/ppermute | solution.py:456
  27.8 0.9 %collective-permute-done.6.part_ref = bf16[32,1152]{1,0:T(8,128)(2,1)S(1)} collective-permute-done((bf16[32,1152]{1,0:T(8,128)(2,1)S(1)}, bf16[32,1152]{1,0:T(8,128)(2,1)S(1)}, u32[]{:S(2)}, u32[]{:S(2)}) %collective-permute-start.6) | collective-permute-done | bytes 73760 | tf_op jit(solution)/shard_map/ppermute | solution.py:452
  28.7 0.7 %down_near.1.own_ref = f32[32,1536]{1,0:T(8,128)S(1)} custom-call(bf16[32,1152]{1,0:T(8,128)(2,1)S(1)} %collective-permute-done.6.part_ref, bf16[4608,1536]{1,0:T(8,128)(2,1)S(1)} %bitcast.10, f32[32,1536]{1,0:T(8,128)S(1)} %down_own.1.own_ref), custom_call_target="tpu_custom_call" | custom-call | flops 113246208 | bytes 3538944 | tf_op jit(solution)/shard_map/down_near/pallas_call | solution.py:390
  29.4 0.6 %collective-permute-done.7.part_ref = bf16[32,1152]{1,0:T(8,128)(2,1)S(1)} collective-permute-done((bf16[32,1152]{1,0:T(8,128)(2,1)S(1)}, bf16[32,1152]{1,0:T(8,128)(2,1)S(1)}, u32[]{:S(2)}, u32[]{:S(2)}) %collective-permute-start.7) | collective-permute-done | bytes 73760 | tf_op jit(solution)/shard_map/ppermute | solution.py:457
  29.9 1.4 %down_far.1 = bf16[8,4,1536]{2,1,0:T(4,128)(2,1)} custom-call(bf16[32,1152]{1,0:T(8,128)(2,1)S(1)} %collective-permute-done.7.part_ref, bf16[4608,1536]{1,0:T(8,128)(2,1)S(1)} %bitcast.11, f32[32,1536]{1,0:T(8,128)S(1)} %down_near.1.own_ref), custom_call_target="tpu_custom_call" | custom-call | flops 113246208 | bytes 3538944 | tf_op jit(solution)/shard_map/down_far/pallas_call | solution.py:390
  31.3 5.0 %all-to-all-start = ((bf16[8,4,1536]{2,1,0:T(4,128)(2,1)}), bf16[8,4,1536]{2,1,0:T(4,128)(2,1)S(1)}, u32[]{:S(2)}, u32[]{:S(2)}) async-start(bf16[8,4,1536]{2,1,0:T(4,128)(2,1)} %down_far.1), calls=%async_computation | async-start | bytes 196608 | tf_op jit(solution)/shard_map/all_to_all | solution.py:463
  36.3 1.5 %finish.1 = bf16[128,1024]{1,0:T(8,128)(2,1)} custom-call(bf16[128,1024]{1,0:T(8,128)(2,1)S(1)} %copy-done, f32[128,1024]{1,0:T(8,128)S(1)} %get-tuple-element.12.intra_ref, f32[128,8]{1,0:T(8,128)S(1)} %get-tuple-element.13.cum_ref, bf16[1024,128]{1,0:T(8,128)(2,1)S(1)} %collective-permute-done.5.state_ref), custom_call_target="tpu_custom_call" | custom-call | flops 33554432 | bytes 1310720 | tf_op jit(solution)/shard_map/finish/pallas_call | solution.py:217
  37.7 5.8 %all-to-all-done = bf16[8,4,1536]{2,1,0:T(4,128)(2,1)S(1)} async-done(((bf16[8,4,1536]{2,1,0:T(4,128)(2,1)}), bf16[8,4,1536]{2,1,0:T(4,128)(2,1)S(1)}, u32[]{:S(2)}, u32[]{:S(2)}) %all-to-all-start) | async-done | bytes 98336 | tf_op jit(solution)/shard_map/all_to_all | solution.py:463
  43.5 0.8 %merge.1 = bf16[4,3072]{1,0:T(4,128)(2,1)} custom-call(s32[2,4]{1,0:T(2,128)S(1)} %bitcast.17, f32[2,4]{1,0:T(2,128)S(1)} %bitcast.18, bf16[2,4,4,1536]{3,2,1,0:T(4,128)(2,1)S(1)} %bitcast.12), custom_call_target="tpu_custom_call" | custom-call | flops 196608 | bytes 98304 | tf_op jit(solution)/shard_map/merge/pallas_call | solution.py:418
  (21 shorter events, 0.0 us)
Async XLA Ops:
  0.6 9.8 %collective-permute-start.2 = (bf16[1,4,3072]{2,1,0:T(4,128)(2,1)}, bf16[1,4,3072]{2,1,0:T(4,128)(2,1)S(1)}, u32[]{:S(2)}, u32[]{:S(2)}) collective-permute-start(bf16[1,4,3072]{2,1,0:T(4,128)(2,1)} %bitcast.13), channel_id=1, source_target_pairs={{0,6},{2,4},{4,2},{6,0},{1,7},{3,5},{5,3},{7,1},{8,14},{10,12},{12... | collective-permute-start | bytes 73736 | tf_op jit(solution)/shard_map/ppermute | solution.py:440
  5.7 4.9 %collective-permute-start.1 = (bf16[1,4,3072]{2,1,0:T(4,128)(2,1)}, bf16[1,4,3072]{2,1,0:T(4,128)(2,1)S(1)}, u32[]{:S(2)}, u32[]{:S(2)}) collective-permute-start(bf16[1,4,3072]{2,1,0:T(4,128)(2,1)} %bitcast.14), channel_id=1, source_target_pairs={{0,4},{2,6},{4,0},{6,2},{1,5},{3,7},{5,1},{7,3},{8,12},{10,14},{12... | collective-permute-start | bytes 73736 | tf_op jit(solution)/shard_map/ppermute | solution.py:440
  5.7 4.9 %collective-permute-start = (bf16[1,4,3072]{2,1,0:T(4,128)(2,1)}, bf16[1,4,3072]{2,1,0:T(4,128)(2,1)S(1)}, u32[]{:S(2)}, u32[]{:S(2)}) collective-permute-start(bf16[1,4,3072]{2,1,0:T(4,128)(2,1)} %bitcast.15), channel_id=1, source_target_pairs={{0,2},{2,0},{4,6},{6,4},{1,3},{3,1},{5,7},{7,5},{8,10},{10,8},{12,... | collective-permute-start | bytes 73736 | tf_op jit(solution)/shard_map/ppermute | solution.py:440
  6.4 4.3 %copy-start.1 = (bf16[4,3072]{1,0:T(4,128)(2,1)S(1)}, bf16[4,3072]{1,0:T(4,128)(2,1)}, u32[]{:S(2)}) copy-start(bf16[4,3072]{1,0:T(4,128)(2,1)} %param.13) | copy-start | bytes 73732
  10.7 5.4 %collective-permute-start.3 = (bf16[4,4,3072]{2,1,0:T(4,128)(2,1)S(1)}, bf16[4,4,3072]{2,1,0:T(4,128)(2,1)S(1)}, u32[]{:S(2)}, u32[]{:S(2)}) collective-permute-start(bf16[4,4,3072]{2,1,0:T(4,128)(2,1)S(1)} %join.1.after_ref.near_ref), channel_id=1, source_target_pairs={{0,8},{8,0},{1,9},{9,1},{2,10},{10,2},{3,11},{11,3},{4,12},{12,4},... | collective-permute-start | bytes 294920 | tf_op jit(solution)/shard_map/ppermute | solution.py:449
  12.3 12.8 %slice-start = ((s8[14155776]{0:T(1024)(128)(4,1)}), s8[4194304]{0:T(1024)(128)(4,1)S(1)}, s32[]{:S(2)}) async-start(s8[14155776]{0:T(1024)(128)(4,1)} %bitcast.7), calls=%async_computation.1 | async-start | bytes 8388608
  12.3 12.8 %slice-start.1 = ((s8[14155776]{0:T(1024)(128)(4,1)}), s8[4194304]{0:T(1024)(128)(4,1)S(1)}, s32[]{:S(2)}) async-start(s8[14155776]{0:T(1024)(128)(4,1)} %bitcast.7), calls=%async_computation.2 | async-start | bytes 8388608
  16.1 8.9 %slice-start.2 = ((s8[14155776]{0:T(1024)(128)(4,1)}), s8[4194304]{0:T(1024)(128)(4,1)S(1)}, s32[]{:S(2)}) async-start(s8[14155776]{0:T(1024)(128)(4,1)} %bitcast.7), calls=%async_computation.3 | async-start | bytes 8388608
  16.1 8.9 %slice-start.3 = ((s8[14155776]{0:T(1024)(128)(4,1)}), s8[1572864]{0:T(1024)(128)(4,1)S(1)}, s32[]{:S(2)}) async-start(s8[14155776]{0:T(1024)(128)(4,1)} %bitcast.7), calls=%async_computation.4 | async-start | bytes 3145728
  22.4 1.6 %collective-permute-start.4 = (bf16[64,2304]{1,0:T(8,128)(2,1)S(1)}, bf16[64,2304]{1,0:T(8,128)(2,1)S(1)}, u32[]{:S(2)}, u32[]{:S(2)}) collective-permute-start(bf16[64,2304]{1,0:T(8,128)(2,1)S(1)} %gate_up_sums.1.own_ref), channel_id=1, source_target_pairs={{0,1},{1,0},{2,3},{3,2},{4,5},{5,4},{6,7},{7,6},{8,9},{9,8},{10,11... | collective-permute-start | bytes 884744 | tf_op jit(solution)/shard_map/ppermute | solution.py:451
  24.2 4.4 %collective-permute-start.6 = (bf16[32,1152]{1,0:T(8,128)(2,1)S(1)}, bf16[32,1152]{1,0:T(8,128)(2,1)S(1)}, u32[]{:S(2)}, u32[]{:S(2)}) collective-permute-start(bf16[32,1152]{1,0:T(8,128)(2,1)S(1)} %get-tuple-element.20), channel_id=1, source_target_pairs={{0,8},{8,0},{1,9},{9,1},{2,10},{10,2},{3,11},{11,3},{4,12},{12,4},... | collective-permute-start | bytes 221192 | tf_op jit(solution)/shard_map/ppermute | solution.py:452
  26.4 9.9 %copy-start = (bf16[128,1024]{1,0:T(8,128)(2,1)S(1)}, bf16[128,1024]{1,0:T(8,128)(2,1)}, u32[]{:S(2)}) copy-start(bf16[128,1024]{1,0:T(8,128)(2,1)} %q_ref.1) | copy-start | bytes 786436
  26.4 17.1 %copy-start.2 = (s32[4,2]{0,1:T(2,128)S(1)}, s32[4,2]{0,1:T(2,128)}, u32[]{:S(2)}) copy-start(s32[4,2]{0,1:T(2,128)} %param.14) | copy-start | bytes 100
  26.4 17.1 %copy-start.3 = (f32[4,2]{0,1:T(2,128)S(1)}, f32[4,2]{0,1:T(2,128)}, u32[]{:S(2)}) copy-start(f32[4,2]{0,1:T(2,128)} %param.15) | copy-start | bytes 100
  26.4 9.8 %collective-permute-start.5 = (bf16[1024,128]{1,0:T(8,128)(2,1)S(1)}, bf16[1024,128]{1,0:T(8,128)(2,1)S(1)}, u32[]{:S(2)}, u32[]{:S(2)}) collective-permute-start(bf16[1024,128]{1,0:T(8,128)(2,1)S(1)} %get-tuple-element.19), channel_id=1, source_target_pairs={{0,8},{8,0},{1,9},{9,1},{2,10},{10,2},{3,11},{11,3},{4,12},{12,4},... | collective-permute-start | bytes 786440 | tf_op jit(solution)/shard_map/ppermute | solution.py:456
  28.7 1.3 %collective-permute-start.7 = (bf16[32,1152]{1,0:T(8,128)(2,1)S(1)}, bf16[32,1152]{1,0:T(8,128)(2,1)S(1)}, u32[]{:S(2)}, u32[]{:S(2)}) collective-permute-start(bf16[32,1152]{1,0:T(8,128)(2,1)S(1)} %collective-permute-done.6.part_ref), channel_id=1, source_target_pairs={{0,1},{1,0},{2,3},{3,2},{4,5},{5,4},{6,7},{7,6},{8,9},{9,8},{10,11... | collective-permute-start | bytes 221192 | tf_op jit(solution)/shard_map/ppermute | solution.py:457
  31.3 12.2 %all-to-all-start = ((bf16[8,4,1536]{2,1,0:T(4,128)(2,1)}), bf16[8,4,1536]{2,1,0:T(4,128)(2,1)S(1)}, u32[]{:S(2)}, u32[]{:S(2)}) async-start(bf16[8,4,1536]{2,1,0:T(4,128)(2,1)} %down_far.1), calls=%async_computation | async-start | bytes 196608 | tf_op jit(solution)/shard_map/all_to_all | solution.py:463
